TPU v7x, 512 devices: a whole 4x4x16 slice. The times are simulated.
512 devices in a mesh: chain: 128 (over z, y, core), rep: 4 (over x).
Axes of the slice: x: 4, y: 4, z: 16, core: 2. Of those that a mesh axis runs over, the one named last changes fastest.
Arguments:
- sub_inverse: bfloat16 [128, 4, 384, 384], P('chain', 'rep'), may hold values from -1.5 to 1.5
- sub_rhs: bfloat16 [128, 4, 384, 256], P('chain', 'rep'), may hold values from -6 to 6
- sub_tiles: int32 [128, 4], P('chain', 'rep'), may hold values from 1 to 3, as said below
- update: bfloat16 [128, 4, 768, 384], P('chain', 'rep'), may hold values from -0.3125 to 0.3125
- update_rows: int32 [128, 4, 6], P('chain', 'rep'), may hold values from 0 to 1
- level_inverse: float32 [128, 256, 256], P('chain'), may hold values from -1.5 to 1.5
- coupling: float32 [128, 256, 128], P('chain'), may hold values from -1.5 to 1.5
- level_rhs: float32 [128, 256, 256], P('chain'), may hold values from -6 to 6
Outputs:
- level_solution: float32 [128, 256, 256], P('chain')
- sub_solution: float32 [128, 4, 384, 256], P('chain', 'rep')
Inputs may be any that keep to these rules, and one draw needn't show every extreme that they name: `sub_tiles`: some subtree block has all 3 tiles live.
All inputs are finite; a program needn't handle non-finite values.
Results may differ from a plain program's by a relative error of at most 0.0049.
Values sent between devices are 32-bit elements; how exact they have to be, the bound alone decides.
No kernel may reach another device: no remote copies, remote signals or barrier semaphores. Data moves between devices by JAX's collectives and lax.ppermute only.
A program may use at most 128 MiB of HBM per device.

v0:
```python
import jax
import jax.numpy as jnp
from jax import lax
from jax.sharding import PartitionSpec as P

TILE = 128


def prefix(value, axis, join, neutral, backward):
    count, mine = (lax.axis_size(axis), lax.axis_index(axis))
    pieces = jax.tree.map(lambda part: lax.all_gather(part, axis), value)
    if backward:
        pieces = jax.tree.map(lambda part: part[::-1], pieces)
        mine = count - 1 - mine
    so_far = jax.tree.map(
        lambda part, zero: jnp.full_like(part, 0) + jnp.asarray(zero, part.dtype), value, neutral
    )

    def lap(position, so_far):
        longer = join(so_far, jax.tree.map(lambda part: part[position], pieces))
        return jax.tree.map(lambda new, old: jnp.where(position < mine, new, old), longer, so_far)

    return lax.fori_loop(0, count - 1, lap, so_far)


def affine_compose(earlier, later):
    highest = lax.Precision.HIGHEST
    matrix = jnp.dot(later[0], earlier[0], precision=highest)
    offset = jnp.dot(later[0], earlier[1], precision=highest) + later[1]
    return (matrix, offset)


def shards(
    sub_inverse, sub_rhs, sub_tiles, update, update_rows, level_inverse, coupling, level_rhs
):
    highest = lax.Precision.HIGHEST
    subtree_inverse = sub_inverse[0, 0]
    block = update[0, 0]
    rhs_sub = sub_rhs[0, 0]
    sub_rows = subtree_inverse.shape[0]
    width = level_inverse.shape[1]
    columns = level_rhs.shape[2]
    live = lax.broadcasted_iota(jnp.int32, (sub_rows, 1), 0) < TILE * sub_tiles[0, 0]
    masked = jnp.where(live, rhs_sub, jnp.zeros_like(rhs_sub))
    solved = jnp.dot(subtree_inverse, masked, preferred_element_type=jnp.float32)
    forward_sub = jnp.where(live, solved, jnp.zeros_like(solved)).astype(jnp.bfloat16)
    contrib = jnp.dot(block, forward_sub, preferred_element_type=jnp.float32)
    table = (
        update_rows[0, 0][None, :]
        == lax.broadcasted_iota(jnp.int32, (width // TILE, block.shape[0] // TILE), 0)
    ).astype(jnp.float32)
    placed = jnp.einsum(
        "st,tpr->spr",
        table,
        contrib.reshape(block.shape[0] // TILE, TILE, columns),
        precision=highest,
    )
    partial_update = placed.reshape(width, columns)
    total = lax.psum_scatter(partial_update, "rep", scatter_dimension=1, tiled=True)
    share = total.shape[1]
    rhs_level = lax.dynamic_slice_in_dim(level_rhs[0], lax.axis_index("rep") * share, share, 1)
    inverse = level_inverse[0]
    couple = coupling[0]
    tile_rows = couple.shape[1]
    gain = -jnp.dot(inverse, couple, precision=highest)
    offset = jnp.dot(inverse, rhs_level - total, precision=highest)
    gain_last = gain[width - tile_rows :]
    offset_last = offset[width - tile_rows :]
    tail = inverse[width - tile_rows :, :].T
    identity = (jnp.eye(tile_rows, dtype=jnp.float32), jnp.zeros_like(offset_last))
    carried_map, before = prefix((gain_last, offset_last), "chain", affine_compose, identity, False)
    forward = jnp.dot(gain, before, precision=highest) + offset
    back_offset = jnp.dot(inverse.T, forward, precision=highest)
    back_gain = -jnp.dot(couple.T, tail, precision=highest)
    back_term = jnp.dot(couple.T, back_offset, precision=highest)
    later_map, after = prefix((back_gain, back_term), "chain", affine_compose, identity, True)
    solution = back_offset - jnp.dot(tail, after, precision=highest)
    solution = lax.all_gather(solution, "rep", axis=1, tiled=True)
    rounded = solution.astype(jnp.bfloat16).astype(jnp.float32)
    picked = jnp.einsum(
        "st,spr->tpr",
        table,
        rounded.reshape(width // TILE, TILE, rounded.shape[1]),
        precision=highest,
    )
    picked = picked.reshape(block.shape[0], rounded.shape[1]).astype(jnp.bfloat16)
    pulled = lax.dot_general(
        block, picked, (((0,), (0,)), ((), ())), preferred_element_type=jnp.float32
    )
    leftover_remainder = (
        forward_sub.astype(jnp.float32) - jnp.where(live, pulled, jnp.zeros_like(pulled))
    ).astype(jnp.bfloat16)
    final = lax.dot_general(
        subtree_inverse,
        leftover_remainder,
        (((0,), (0,)), ((), ())),
        preferred_element_type=jnp.float32,
    )
    final = jnp.where(live, final, jnp.zeros_like(final))
    return (solution[None], final[None, None])


def solution(mesh):
    return jax.shard_map(
        shards,
        mesh=mesh,
        in_specs=(
            P("chain", "rep", None, None),
            P("chain", "rep", None, None),
            P("chain", "rep"),
            P("chain", "rep", None, None),
            P("chain", "rep", None),
            P("chain", None, None),
            P("chain", None, None),
            P("chain", None, None),
        ),
        out_specs=(P("chain", None, None), P("chain", "rep", None, None)),
        check_vma=False,
    )
```

profile of v0, /device:TPU:1, one launch (start us, length us, event | category | flops | bytes accessed | tf_op | source)
XLA Modules:
  0.0 910.2 jit_solution(1511358080054148583)
XLA Ops:
  8.0 1.5 fusion.19
  10.1 1.7 fusion.21
  12.8 31.4 %reduce-scatter.4.cloned.1.call-done = f32[64,256]{1,0:T(8,128)} async-done(((f32[256,256]{1,0:T(8,128)}), f32[64,256]{1,0:T(8,128)}) %reduce-scatter.4.cloned.1.call-update) | async-done | bytes 65552
  48.5 138.7 %all-gather.11.cloned.1.call-done = f32[16384,64]{0,1:T(8,128)} async-done(((f32[128,64]{0,1:T(8,128)}), f32[16384,64]{0,1:T(8,128)}) %all-gather.11.cloned.1.call-update) | async-done | bytes 4194320 | tf_op jit(solution)/shard_map/all_gather | solution.py:11
  187.2 4.9 copy.38
  192.0 142.8 %all-gather.9.cloned.1.call-done = f32[16384,128]{1,0:T(8,128)} async-done(((f32[128,128]{1,0:T(8,128)}), f32[16384,128]{1,0:T(8,128)}) %all-gather.9.cloned.1.call-update) | async-done | bytes 8388624 | tf_op jit(solution)/shard_map/all_gather | solution.py:11
  334.8 268.5 %while.28 = (s32[]{:T(128)}, f32[128,64]{0,1:T(8,128)S(1)}, s32[]{:T(128)}, f32[128,128,128]{2,1,0:T(8,128)}, f32[128,128,64]{1,0,2:T(8,128)}, /*index=5*/s32[]{:T(128)}, s32[]{:T(128)}) while((s32[]{:T(128)}, f32[128,64]{0,1:T(8,128)S(1)}, s32[]{:T(128)}, f32[128,128,128]{2,1,0:T(8,128)}, f32[128,128,64]{1,0,2:T(8,128)}, ...), condition=%wide.region_2.3_spmd.clone, body=%wide.region_1.2_spmd.clone.sunk | while | flops 12615684 | bytes 329835 | solution.py:23
  337.9 1.1 fusion.71
  340.1 1.1 fusion.71
  342.2 1.1 fusion.71
  344.3 1.1 fusion.71
  348.5 1.1 fusion.71
  350.6 1.1 fusion.71
  359.1 1.1 fusion.71
  424.6 1.1 fusion.71
  428.9 1.1 fusion.71
  437.3 1.1 fusion.71
  441.6 1.1 fusion.71
  447.9 1.1 fusion.71
  454.3 1.1 fusion.71
  456.4 1.1 fusion.71
  460.7 1.1 fusion.71
  462.8 1.1 fusion.71
  464.9 1.1 fusion.71
  479.7 1.1 fusion.71
  604.8 7.7 rev.6
  612.5 124.6 %all-gather.15.cloned.1.call-done = f32[16384,64]{0,1:T(8,128)} async-done(((f32[128,64]{0,1:T(8,128)}), f32[16384,64]{0,1:T(8,128)}) %all-gather.15.cloned.1.call-update) | async-done | bytes 4194320 | tf_op jit(solution)/shard_map/all_gather | solution.py:11
  737.1 4.8 copy_bitcast_fusion
  741.9 4.7 rev.7
  746.6 143.6 %while.29 = (s32[]{:T(128)}, f32[128,64]{0,1:T(8,128)S(1)}, s32[]{:T(128)}, f32[128,128,128]{2,1,0:T(8,128)}, f32[128,128,64]{1,2,0:T(8,128)}, /*index=5*/s32[]{:T(128)}, s32[]{:T(128)}) while((s32[]{:T(128)}, f32[128,64]{0,1:T(8,128)S(1)}, s32[]{:T(128)}, f32[128,128,128]{2,1,0:T(8,128)}, f32[128,128,64]{1,2,0:T(8,128)}, ...), condition=%wide.region_4.5_spmd.clone, body=%wide.region_3.4_spmd.clone.sunk | while | flops 12615684 | bytes 264807 | solution.py:23
  746.6 1.1 fusion.74
  890.4 10.3 %all_gather.35 = f32[256,256]{0,1:T(8,128)S(1)} all-gather(f32[256,64]{0,1:T(8,128)S(1)} %fusion.20), channel_id=1, replica_groups=mesh['chain'=128,'rep'=4] {'rep'}, dimensions={1}, use_global_device_ids=true | all-gather | bytes 327680 | tf_op jit(solution)/shard_map/all_gather | solution.py:78
  (664 shorter events, 391.2 us)
Async XLA Ops:
  7.2 2.3 copy-start
  7.2 38.0 %copy-start.1 = (f32[1,256,256]{2,1,0:T(8,128)S(1)}, f32[1,256,256]{2,1,0:T(8,128)}, u32[]{:S(2)}) copy-start(f32[1,256,256]{2,1,0:T(8,128)} %param.17) | copy-start | bytes 786436
  7.2 38.0 %copy-start.3 = (f32[1,256,256]{2,1,0:T(8,128)S(1)}, f32[1,256,256]{2,1,0:T(8,128)}, u32[]{:S(2)}) copy-start(f32[1,256,256]{2,1,0:T(8,128)} %param.19) | copy-start | bytes 786436
  7.2 39.1 %copy-start.2 = (f32[1,256,128]{2,1,0:T(8,128)S(1)}, f32[1,256,128]{2,1,0:T(8,128)}, u32[]{:S(2)}) copy-start(f32[1,256,128]{2,1,0:T(8,128)} %param.18) | copy-start | bytes 393220
  7.2 37.0 %reduce-scatter.4.cloned.1.call-start = ((), (), s32[]{:S(2)}) async-start(), calls=%async_computation.5 | async-start | bytes 327680
  12.7 174.4 %all-gather.11.cloned.1.call-start = ((), (), s32[]{:S(2)}) async-start(), calls=%async_computation.2 | async-start | bytes 4227072 | tf_op jit(solution)/shard_map/all_gather | solution.py:11
  46.2 288.6 %all-gather.9.cloned.1.call-start = ((), (), s32[]{:S(2)}) async-start(), calls=%async_computation.1 | async-start | bytes 8454144 | tf_op jit(solution)/shard_map/all_gather | solution.py:11
  47.3 557.5 %all-gather.13.cloned.1.call-start = ((), (), s32[]{:S(2)}) async-start(), calls=%async_computation.3 | async-start | bytes 8454144 | tf_op jit(solution)/shard_map/all_gather | solution.py:11
  48.4 688.7 %all-gather.15.cloned.1.call-start = ((), (), s32[]{:S(2)}) async-start(), calls=%async_computation.4 | async-start | bytes 4227072 | tf_op jit(solution)/shard_map/all_gather | solution.py:11
  741.9 159.9 %copy-start.4 = (s32[1,1,6]{2,1,0:T(1,128)S(1)}, s32[1,1,6]{2,1,0:T(1,128)}, u32[]{:S(2)}) copy-start(s32[1,1,6]{2,1,0:T(1,128)} %param.16) | copy-start | bytes 76
  746.6 155.6 %copy-start.5 = (bf16[1,1,384,384]{3,2,1,0:T(8,128)(2,1)S(1)}, bf16[1,1,384,384]{3,2,1,0:T(8,128)(2,1)}, u32[]{:S(2)}) copy-start(bf16[1,1,384,384]{3,2,1,0:T(8,128)(2,1)} %param.12) | copy-start | bytes 884740
Sparse Core Ops, SparseCore 0:
  12.8 31.3 reduce-scatter.3
  47.7 139.4 all-gather.10
  191.4 143.4 all-gather.8
  338.9 142.1 all-gather.12
  604.9 132.1 all-gather.14
where the time goes:
time: 928 us; the launch traced here: 910 us
  waiting for transfers between devices  438 us (47%)
  matrix products  284 us (31%)
  local copies, waits for them, and re-layouts  153 us (16%)
  between operations  14.8 us (2%)
  loops' own time  10.6 us (1%)
  blocking collectives  10.3 us (1%)
    all_gather x4, waiting for transfers between devices, prefix(): pieces = jax.tree.map(lambda part: lax.all_gather(part, axis), value)  406 us
    dot_general x254, matrix products, affine_compose(): offset = jnp.dot(later[0], earlier[1], precision=highest) + later[1]  276 us
    dynamic_slice x127, local copies, waits for them, and re-layouts, lap(): longer = join(so_far, jax.tree.map(lambda part: part[position], pieces))  125 us
    unnamed x6, waiting for transfers between devices  31.5 us
  transfers between devices with their start and end apart: 5, of which 4 were waited for; matrix products, arithmetic and copies ran while one was open for 31% of the time, Pallas kernels for 0%

commit v1 on v0

v1 whole, which is shorter than its diff:
```python
import functools

import jax
import jax.numpy as jnp
from jax import lax
from jax.experimental import pallas as pl
from jax.experimental.pallas import tpu as pltpu
from jax.sharding import PartitionSpec as P

TILE = 128
HIGHEST = lax.Precision.HIGHEST
SWAP = (1, 2, 6, 8, 16, 32, 96)


def dot(a, b, dims=((1,), (0,)), precision=HIGHEST):
    return lax.dot_general(
        a, b, (dims, ((), ())), precision=precision, preferred_element_type=jnp.float32
    )


def swap(value, j, count):
    return lax.ppermute(value, "chain", [(k, k ^ SWAP[j]) for k in range(count)])


def level_maps(inverse, couple):
    gain = -dot(inverse, couple)
    return gain, jnp.concatenate([gain[TILE:], -dot(gain, gain, ((0,), (0,)))], axis=0)


def subtree_forward(subtree_inverse, rhs_sub, live, block, rows, rhs_level, inverse):
    masked = jnp.where(live, rhs_sub, jnp.zeros_like(rhs_sub))
    solved = jnp.dot(subtree_inverse, masked, preferred_element_type=jnp.float32)
    forward_sub = jnp.where(live, solved, jnp.zeros_like(solved)).astype(jnp.bfloat16)
    contrib = jnp.dot(block, forward_sub, preferred_element_type=jnp.float32)
    contrib = contrib.reshape(rows.shape[0], TILE, -1)
    tiles = inverse.shape[0] // TILE
    placed = [
        sum(jnp.where(rows[t] == s, contrib[t], 0.0) for t in range(rows.shape[0]))
        for s in range(tiles)
    ]
    rest = 0.25 * rhs_level - jnp.concatenate(placed, axis=0)
    return forward_sub, dot(rest, inverse, ((0,), (1,)))


def subtree_backward(solution, forward_sub, subtree_inverse, live, block, rows):
    rounded = solution.astype(jnp.bfloat16)
    picked = jnp.concatenate(
        [
            jnp.where(rows[t] == 0, rounded[:TILE], rounded[TILE:])
            for t in range(rows.shape[0])
        ],
        axis=0,
    )
    pulled = dot(block, picked, ((0,), (0,)), None)
    residue = (forward_sub.astype(jnp.float32) - jnp.where(live, pulled, 0.0)).astype(
        jnp.bfloat16
    )
    final = dot(subtree_inverse, residue, ((0,), (0,)), None)
    return jnp.where(live, final, 0.0)


def shards(
    sub_inverse, sub_rhs, sub_tiles, update, update_rows, level_inverse, coupling, level_rhs
):
    count, reps = lax.axis_size("chain"), lax.axis_size("rep")
    place = lax.axis_index("chain")
    subtree_inverse, block, rows = sub_inverse[0, 0], update[0, 0], update_rows[0, 0]
    inverse, couple = level_inverse[0], coupling[0]
    sub_rows = subtree_inverse.shape[0]
    live = lax.broadcasted_iota(jnp.int32, (sub_rows, 1), 0) < TILE * sub_tiles[0, 0]
    gain, maps = level_maps(inverse, couple)
    forward_sub, part = subtree_forward(
        subtree_inverse, sub_rhs[0, 0], live, block, rows, level_rhs[0], inverse
    )
    columns = part.shape[0] // reps
    parts = lax.all_to_all(part.reshape(reps, columns, -1), "rep", 0, 0)
    own = parts[0] + parts[1] + parts[2] + parts[3]
    state = jnp.concatenate([own[:, TILE:], -dot(own, gain)], axis=1)
    descent = []
    rounds = len(SWAP)
    for j in range(rounds):
        right = ((place >> j) & 1) == 1
        last = j == rounds - 1
        other = swap(maps[TILE:] if last else maps, j, count)
        other_state = swap(state, j, count)
        other_k = other if last else other[TILE:]
        push = jnp.where(
            right,
            other_state[:, :TILE],
            other_state[:, TILE:] + dot(state[:, :TILE], other_k),
        )
        if last:
            descent.append((right, None, push))
            break
        first = jnp.where(right, other, maps)
        second = jnp.where(right, maps, other)
        product = dot(second, first[:TILE])
        turned = dot(first[:TILE], product[TILE:], ((0,), (0,)))
        step = jnp.where(
            right,
            jnp.concatenate([other[:TILE].T, jnp.zeros_like(turned)], axis=0),
            jnp.concatenate([product[TILE:].T, other[:TILE]], axis=0),
        )
        descent.append((right, step, push))
        early = jnp.where(right, other_state, state)
        late = jnp.where(right, state, other_state)
        state = jnp.concatenate(
            [
                late[:, :TILE] + dot(early[:, :TILE], second[:TILE], ((1,), (1,))),
                early[:, TILE:]
                + dot(late[:, TILE:], first[:TILE])
                + dot(early[:, :TILE], product[TILE:]),
            ],
            axis=1,
        )
        maps = jnp.concatenate([product[:TILE], first[TILE:] + turned], axis=0)
    before = jnp.zeros((columns, TILE), jnp.float32)
    after = before
    for right, step, push in reversed(descent):
        if step is not None:
            push = push + dot(jnp.concatenate([before, after], axis=1), step)
        before, after = jnp.where(right, push, before), jnp.where(right, after, push)
    forward = own + dot(before, gain, ((1,), (1,)))
    forward = jnp.concatenate([forward[:, :TILE], forward[:, TILE:] - after], axis=1)
    share = dot(forward, inverse)
    spread = lax.all_to_all(
        jnp.broadcast_to(share[None], (reps,) + share.shape), "rep", 0, 0
    )
    solution = spread.reshape(-1, share.shape[1]).T
    final = subtree_backward(solution, forward_sub, subtree_inverse, live, block, rows)
    return (solution[None], final[None, None])


def solution(mesh):
    return jax.shard_map(
        shards,
        mesh=mesh,
        in_specs=(
            P("chain", "rep", None, None),
            P("chain", "rep", None, None),
            P("chain", "rep"),
            P("chain", "rep", None, None),
            P("chain", "rep", None),
            P("chain", None, None),
            P("chain", None, None),
            P("chain", None, None),
        ),
        out_specs=(P("chain", None, None), P("chain", "rep", None, None)),
        check_vma=False,
    )
```

time: 928 us -> 129 us (0.14)
  the two profiles are of different devices: /device:TPU:1 before, /device:TPU:96 now
where the time goes in v1:
time: 129 us; the launch traced here: 128 us
  starting transfers between devices  55.7 us (43%)
  waiting for transfers between devices  31.3 us (24%)
  matrix products  15.3 us (12%)
  between operations  9.95 us (8%)
  blocking collectives  9.07 us (7%)
  local copies, waits for them, and re-layouts  6.19 us (5%)
    ppermute x14, starting transfers between devices, swap(): lax.ppermute(value, 'chain', [(k, k ^ SWAP[j]) for k in range(count)])  51.4 us
    ppermute x14, waiting for transfers between devices, swap(): lax.ppermute(value, 'chain', [(k, k ^ SWAP[j]) for k in range(count)])  28.3 us
    dot_general x50, matrix products, dot(): lax.dot_general(a, b, (dims, ((), ())), precision=precision, preferred_el...  14.5 us
    all_to_all x1, blocking collectives, shards(): lax.all_to_all(jnp.broadcast_to(share[None], (reps,) + share.shape), 'rep...  9.07 us
    unnamed x26, local copies, waits for them, and re-layouts  4.92 us
    all_to_all x1, starting transfers between devices, shards(): parts = lax.all_to_all(part.reshape(reps, columns, -1), 'rep', 0, 0)  4.29 us
    all_to_all x1, waiting for transfers between devices, shards(): parts = lax.all_to_all(part.reshape(reps, columns, -1), 'rep', 0, 0)  3.01 us
  transfers between devices with their start and end apart: 15, of which 9 were waited for; matrix products, arithmetic and copies ran while one was open for 7% of the time, Pallas kernels for 0%

profile of v1, /device:TPU:96, one launch (start us, length us, event | category | flops | bytes accessed | tf_op | source)
XLA Modules:
  0.0 128.2 jit_solution(14284091068295925050)
XLA Ops:
  0.6 1.4 %convolution_negate_fusion = f32[256,128]{1,0:T(8,128)S(1)} fusion(f32[1,256,256]{2,1,0:T(8,128)} %param.13, f32[1,256,128]{2,1,0:T(8,128)} %param.14), kind=kOutput, calls=%fused_computation.8 | convolution fusion | flops 100696064 | bytes 524288 | tf_op jit(solution)/shard_map/dot_general | solution.py:16
  2.5 2.1 %collective-permute-start.1 = (f32[256,128]{1,0:T(8,128)S(1)}, f32[256,128]{1,0:T(8,128)S(1)}, u32[]{:S(2)}, u32[]{:S(2)}) collective-permute-start(f32[256,128]{1,0:T(8,128)S(1)} %pad_maximum_fusion), channel_id=1, source_target_pairs={{0,4},{4,0},{8,12},{12,8},{16,20},{20,16},{24,28},{28,24},{32,36},... | collective-permute-start | bytes 393224 | tf_op jit(solution)/shard_map/ppermute | solution.py:22
  4.6 0.7 fusion.272
  13.7 0.8 copy-done.6
  15.5 0.9 copy-done.1
  16.4 1.1 fusion.10
  17.5 4.3 %all-to-all-start = ((f32[4,64,256]{2,1,0:T(8,128)}), f32[4,64,256]{2,1,0:T(8,128)S(1)}, u32[]{:S(2)}, u32[]{:S(2)}) async-start(f32[4,64,256]{2,1,0:T(8,128)} %fusion.10), calls=%async_computation | async-start | bytes 524288 | tf_op jit(solution)/shard_map/all_to_all | solution.py:76
  22.4 3.5 %collective-permute-start.3 = (f32[256,128]{1,0:T(8,128)S(1)}, f32[256,128]{1,0:T(8,128)S(1)}, u32[]{:S(2)}, u32[]{:S(2)}) collective-permute-start(f32[256,128]{1,0:T(8,128)S(1)} %pad_maximum_fusion.1), channel_id=1, source_target_pairs={{0,8},{4,12},{8,0},{12,4},{16,24},{20,28},{24,16},{28,20},{32,40},... | collective-permute-start | bytes 393224 | tf_op jit(solution)/shard_map/ppermute | solution.py:22
  26.1 3.0 %all-to-all-done = f32[4,64,256]{2,1,0:T(8,128)S(1)} async-done(((f32[4,64,256]{2,1,0:T(8,128)}), f32[4,64,256]{2,1,0:T(8,128)S(1)}, u32[]{:S(2)}, u32[]{:S(2)}) %all-to-all-start) | async-done | bytes 262176 | tf_op jit(solution)/shard_map/all_to_all | solution.py:76
  29.4 1.9 %collective-permute-start = (f32[64,256]{1,0:T(8,128)S(1)}, f32[64,256]{1,0:T(8,128)S(1)}, u32[]{:S(2)}, u32[]{:S(2)}) collective-permute-start(f32[64,256]{1,0:T(8,128)S(1)} %pad_maximum_fusion.6), channel_id=1, source_target_pairs={{0,4},{4,0},{8,12},{12,8},{16,20},{20,16},{24,28},{28,24},{32,36},... | collective-permute-start | bytes 196616 | tf_op jit(solution)/shard_map/ppermute | solution.py:22
  33.2 3.5 %collective-permute-start.2 = (f32[64,256]{1,0:T(8,128)S(1)}, f32[64,256]{1,0:T(8,128)S(1)}, u32[]{:S(2)}, u32[]{:S(2)}) collective-permute-start(f32[64,256]{1,0:T(8,128)S(1)} %pad_maximum_fusion.7), channel_id=1, source_target_pairs={{0,8},{4,12},{8,0},{12,4},{16,24},{20,28},{24,16},{28,20},{32,40},... | collective-permute-start | bytes 196616 | tf_op jit(solution)/shard_map/ppermute | solution.py:22
  36.7 4.1 %collective-permute-start.5 = (f32[256,128]{1,0:T(8,128)S(1)}, f32[256,128]{1,0:T(8,128)S(1)}, u32[]{:S(2)}, u32[]{:S(2)}) collective-permute-start(f32[256,128]{1,0:T(8,128)S(1)} %pad_maximum_fusion.2), channel_id=1, source_target_pairs={{0,24},{4,28},{8,16},{12,20},{16,8},{20,12},{24,0},{28,4},{32,56},... | collective-permute-start | bytes 393224 | tf_op jit(solution)/shard_map/ppermute | solution.py:22
  41.9 3.1 %collective-permute-start.4 = (f32[64,256]{1,0:T(8,128)S(1)}, f32[64,256]{1,0:T(8,128)S(1)}, u32[]{:S(2)}, u32[]{:S(2)}) collective-permute-start(f32[64,256]{1,0:T(8,128)S(1)} %pad_maximum_fusion.8), channel_id=1, source_target_pairs={{0,24},{4,28},{8,16},{12,20},{16,8},{20,12},{24,0},{28,4},{32,56},... | collective-permute-start | bytes 196616 | tf_op jit(solution)/shard_map/ppermute | solution.py:22
  45.7 2.0 %collective-permute-start.7 = (f32[256,128]{1,0:T(8,128)S(1)}, f32[256,128]{1,0:T(8,128)S(1)}, u32[]{:S(2)}, u32[]{:S(2)}) collective-permute-start(f32[256,128]{1,0:T(8,128)S(1)} %pad_maximum_fusion.3), channel_id=1, source_target_pairs={{0,32},{4,36},{8,40},{12,44},{16,48},{20,52},{24,56},{28,60},{32,0... | collective-permute-start | bytes 393224 | tf_op jit(solution)/shard_map/ppermute | solution.py:22
  47.7 1.5 %collective-permute-done.4 = f32[64,256]{1,0:T(8,128)S(1)} collective-permute-done((f32[64,256]{1,0:T(8,128)S(1)}, f32[64,256]{1,0:T(8,128)S(1)}, u32[]{:S(2)}, u32[]{:S(2)}) %collective-permute-start.4) | collective-permute-done | bytes 65568 | tf_op jit(solution)/shard_map/ppermute | solution.py:22
  49.9 2.3 %collective-permute-start.6 = (f32[64,256]{1,0:T(8,128)S(1)}, f32[64,256]{1,0:T(8,128)S(1)}, u32[]{:S(2)}, u32[]{:S(2)}) collective-permute-start(f32[64,256]{1,0:T(8,128)S(1)} %pad_maximum_fusion.9), channel_id=1, source_target_pairs={{0,32},{4,36},{8,40},{12,44},{16,48},{20,52},{24,56},{28,60},{32,0... | collective-permute-start | bytes 196616 | tf_op jit(solution)/shard_map/ppermute | solution.py:22
  52.7 3.4 %collective-permute-done.6 = f32[64,256]{1,0:T(8,128)S(1)} collective-permute-done((f32[64,256]{1,0:T(8,128)S(1)}, f32[64,256]{1,0:T(8,128)S(1)}, u32[]{:S(2)}, u32[]{:S(2)}) %collective-permute-start.6) | collective-permute-done | bytes 65568 | tf_op jit(solution)/shard_map/ppermute | solution.py:22
  57.2 3.5 %collective-permute-start.9 = (f32[256,128]{1,0:T(8,128)S(1)}, f32[256,128]{1,0:T(8,128)S(1)}, u32[]{:S(2)}, u32[]{:S(2)}) collective-permute-start(f32[256,128]{1,0:T(8,128)S(1)} %pad_maximum_fusion.4), channel_id=1, source_target_pairs={{0,64},{4,68},{8,72},{12,76},{16,80},{20,84},{24,88},{28,92},{32,9... | collective-permute-start | bytes 393224 | tf_op jit(solution)/shard_map/ppermute | solution.py:22
  60.9 3.2 %collective-permute-start.8 = (f32[64,256]{1,0:T(8,128)S(1)}, f32[64,256]{1,0:T(8,128)S(1)}, u32[]{:S(2)}, u32[]{:S(2)}) collective-permute-start(f32[64,256]{1,0:T(8,128)S(1)} %pad_maximum_fusion.10), channel_id=1, source_target_pairs={{0,64},{4,68},{8,72},{12,76},{16,80},{20,84},{24,88},{28,92},{32,9... | collective-permute-start | bytes 196616 | tf_op jit(solution)/shard_map/ppermute | solution.py:22
  64.5 4.5 %collective-permute-done.8 = f32[64,256]{1,0:T(8,128)S(1)} collective-permute-done((f32[64,256]{1,0:T(8,128)S(1)}, f32[64,256]{1,0:T(8,128)S(1)}, u32[]{:S(2)}, u32[]{:S(2)}) %collective-permute-start.8) | collective-permute-done | bytes 65568 | tf_op jit(solution)/shard_map/ppermute | solution.py:22
  70.1 8.4 %collective-permute-start.11 = (f32[256,128]{1,0:T(8,128)S(1)}, f32[256,128]{1,0:T(8,128)S(1)}, u32[]{:S(2)}, u32[]{:S(2)}) collective-permute-start(f32[256,128]{1,0:T(8,128)S(1)} %pad_maximum_fusion.5), channel_id=1, source_target_pairs={{0,128},{4,132},{8,136},{12,140},{16,144},{20,148},{24,152},{28,15... | collective-permute-start | bytes 393224 | tf_op jit(solution)/shard_map/ppermute | solution.py:22
  78.7 1.9 %collective-permute-start.10 = (f32[64,256]{1,0:T(8,128)S(1)}, f32[64,256]{1,0:T(8,128)S(1)}, u32[]{:S(2)}, u32[]{:S(2)}) collective-permute-start(f32[64,256]{1,0:T(8,128)S(1)} %pad_maximum_fusion.11), channel_id=1, source_target_pairs={{0,128},{4,132},{8,136},{12,140},{16,144},{20,148},{24,152},{28,15... | collective-permute-start | bytes 196616 | tf_op jit(solution)/shard_map/ppermute | solution.py:22
  81.0 10.5 %collective-permute-done.10 = f32[64,256]{1,0:T(8,128)S(1)} collective-permute-done((f32[64,256]{1,0:T(8,128)S(1)}, f32[64,256]{1,0:T(8,128)S(1)}, u32[]{:S(2)}, u32[]{:S(2)}) %collective-permute-start.10) | collective-permute-done | bytes 65568 | tf_op jit(solution)/shard_map/ppermute | solution.py:22
  91.8 0.9 slice_add_fusion
  92.8 10.0 %collective-permute-start.13 = (f32[128,128]{1,0:T(8,128)}, f32[128,128]{1,0:T(8,128)S(1)}, u32[]{:S(2)}, u32[]{:S(2)}) collective-permute-start(f32[128,128]{1,0:T(8,128)} %slice_add_fusion), channel_id=1, source_target_pairs={{0,384},{4,388},{8,392},{12,396},{16,400},{20,404},{24,408},{28,41... | collective-permute-start | bytes 196616 | tf_op jit(solution)/shard_map/ppermute | solution.py:22
  103.5 1.9 %collective-permute-start.12 = (f32[64,256]{1,0:T(8,128)S(1)}, f32[64,256]{1,0:T(8,128)S(1)}, u32[]{:S(2)}, u32[]{:S(2)}) collective-permute-start(f32[64,256]{1,0:T(8,128)S(1)} %pad_maximum_fusion.12), channel_id=1, source_target_pairs={{0,384},{4,388},{8,392},{12,396},{16,400},{20,404},{24,408},{28,41... | collective-permute-start | bytes 196616 | tf_op jit(solution)/shard_map/ppermute | solution.py:22
  105.7 1.4 %collective-permute-done.13 = f32[128,128]{1,0:T(8,128)S(1)} collective-permute-done((f32[128,128]{1,0:T(8,128)}, f32[128,128]{1,0:T(8,128)S(1)}, u32[]{:S(2)}, u32[]{:S(2)}) %collective-permute-start.13) | collective-permute-done | bytes 65568 | tf_op jit(solution)/shard_map/ppermute | solution.py:22
  107.1 6.5 %collective-permute-done.12 = f32[64,256]{1,0:T(8,128)S(1)} collective-permute-done((f32[64,256]{1,0:T(8,128)S(1)}, f32[64,256]{1,0:T(8,128)S(1)}, u32[]{:S(2)}, u32[]{:S(2)}) %collective-permute-start.12) | collective-permute-done | bytes 65568 | tf_op jit(solution)/shard_map/ppermute | solution.py:22
  115.7 9.1 %all_to_all.10 = f32[4,64,256]{2,1,0:T(8,128)S(1)} all-to-all(f32[4,64,256]{2,1,0:T(8,128)S(1)} %broadcast_in_dim.70), channel_id=1, replica_groups=mesh['chain'=128,'rep'=4] {'rep'}, dimensions={0} | all-to-all | bytes 524288 | tf_op jit(solution)/shard_map/all_to_all | solution.py:126
  125.0 0.8 copy-done.5
  126.4 0.9 copy.23
  127.3 0.8 copy.22
  (132 shorter events, 14.4 us)
Async XLA Ops:
  0.6 14.3 %copy-start = (bf16[1,1,768,384]{3,2,1,0:T(8,128)(2,1)S(1)}, bf16[1,1,768,384]{3,2,1,0:T(8,128)(2,1)}, u32[]{:S(2)}) copy-start(bf16[1,1,768,384]{3,2,1,0:T(8,128)(2,1)} %param.11) | copy-start | bytes 1769476
  2.5 11.1 %copy-start.2 = (f32[1,256,256]{2,1,0:T(8,128)S(1)}, f32[1,256,256]{2,1,0:T(8,128)}, u32[]{:S(2)}) copy-start(f32[1,256,256]{2,1,0:T(8,128)} %param.15) | copy-start | bytes 786436
  2.5 2.1 %copy-start.3 = (s32[1,1,6]{2,1,0:T(1,128)S(1)}, s32[1,1,6]{2,1,0:T(1,128)}, u32[]{:S(2)}) copy-start(s32[1,1,6]{2,1,0:T(1,128)} %param.12) | copy-start | bytes 76
  2.5 11.2 %copy-start.4 = (bf16[1,1,384,384]{3,2,1,0:T(8,128)(2,1)S(1)}, bf16[1,1,384,384]{3,2,1,0:T(8,128)(2,1)}, u32[]{:S(2)}) copy-start(bf16[1,1,384,384]{3,2,1,0:T(8,128)(2,1)} %param.8) | copy-start | bytes 884740
  2.5 19.3 %collective-permute-start.1 = (f32[256,128]{1,0:T(8,128)S(1)}, f32[256,128]{1,0:T(8,128)S(1)}, u32[]{:S(2)}, u32[]{:S(2)}) collective-permute-start(f32[256,128]{1,0:T(8,128)S(1)} %pad_maximum_fusion), channel_id=1, source_target_pairs={{0,4},{4,0},{8,12},{12,8},{16,20},{20,16},{24,28},{28,24},{32,36},... | collective-permute-start | bytes 393224 | tf_op jit(solution)/shard_map/ppermute | solution.py:22
  13.6 0.9 copy-start.6
  15.4 1.0 copy-start.1
  17.5 11.6 %all-to-all-start = ((f32[4,64,256]{2,1,0:T(8,128)}), f32[4,64,256]{2,1,0:T(8,128)S(1)}, u32[]{:S(2)}, u32[]{:S(2)}) async-start(f32[4,64,256]{2,1,0:T(8,128)} %fusion.10), calls=%async_computation | async-start | bytes 524288 | tf_op jit(solution)/shard_map/all_to_all | solution.py:76
  22.4 9.1 %collective-permute-start.3 = (f32[256,128]{1,0:T(8,128)S(1)}, f32[256,128]{1,0:T(8,128)S(1)}, u32[]{:S(2)}, u32[]{:S(2)}) collective-permute-start(f32[256,128]{1,0:T(8,128)S(1)} %pad_maximum_fusion.1), channel_id=1, source_target_pairs={{0,8},{4,12},{8,0},{12,4},{16,24},{20,28},{24,16},{28,20},{32,40},... | collective-permute-start | bytes 393224 | tf_op jit(solution)/shard_map/ppermute | solution.py:22
  29.4 3.1 %collective-permute-start = (f32[64,256]{1,0:T(8,128)S(1)}, f32[64,256]{1,0:T(8,128)S(1)}, u32[]{:S(2)}, u32[]{:S(2)}) collective-permute-start(f32[64,256]{1,0:T(8,128)S(1)} %pad_maximum_fusion.6), channel_id=1, source_target_pairs={{0,4},{4,0},{8,12},{12,8},{16,20},{20,16},{24,28},{28,24},{32,36},... | collective-permute-start | bytes 196616 | tf_op jit(solution)/shard_map/ppermute | solution.py:22
  33.2 8.0 %collective-permute-start.2 = (f32[64,256]{1,0:T(8,128)S(1)}, f32[64,256]{1,0:T(8,128)S(1)}, u32[]{:S(2)}, u32[]{:S(2)}) collective-permute-start(f32[64,256]{1,0:T(8,128)S(1)} %pad_maximum_fusion.7), channel_id=1, source_target_pairs={{0,8},{4,12},{8,0},{12,4},{16,24},{20,28},{24,16},{28,20},{32,40},... | collective-permute-start | bytes 196616 | tf_op jit(solution)/shard_map/ppermute | solution.py:22
  36.7 8.4 %collective-permute-start.5 = (f32[256,128]{1,0:T(8,128)S(1)}, f32[256,128]{1,0:T(8,128)S(1)}, u32[]{:S(2)}, u32[]{:S(2)}) collective-permute-start(f32[256,128]{1,0:T(8,128)S(1)} %pad_maximum_fusion.2), channel_id=1, source_target_pairs={{0,24},{4,28},{8,16},{12,20},{16,8},{20,12},{24,0},{28,4},{32,56},... | collective-permute-start | bytes 393224 | tf_op jit(solution)/shard_map/ppermute | solution.py:22
  41.9 7.4 %collective-permute-start.4 = (f32[64,256]{1,0:T(8,128)S(1)}, f32[64,256]{1,0:T(8,128)S(1)}, u32[]{:S(2)}, u32[]{:S(2)}) collective-permute-start(f32[64,256]{1,0:T(8,128)S(1)} %pad_maximum_fusion.8), channel_id=1, source_target_pairs={{0,24},{4,28},{8,16},{12,20},{16,8},{20,12},{24,0},{28,4},{32,56},... | collective-permute-start | bytes 196616 | tf_op jit(solution)/shard_map/ppermute | solution.py:22
  45.7 10.4 %collective-permute-start.7 = (f32[256,128]{1,0:T(8,128)S(1)}, f32[256,128]{1,0:T(8,128)S(1)}, u32[]{:S(2)}, u32[]{:S(2)}) collective-permute-start(f32[256,128]{1,0:T(8,128)S(1)} %pad_maximum_fusion.3), channel_id=1, source_target_pairs={{0,32},{4,36},{8,40},{12,44},{16,48},{20,52},{24,56},{28,60},{32,0... | collective-permute-start | bytes 393224 | tf_op jit(solution)/shard_map/ppermute | solution.py:22
  49.9 6.2 %collective-permute-start.6 = (f32[64,256]{1,0:T(8,128)S(1)}, f32[64,256]{1,0:T(8,128)S(1)}, u32[]{:S(2)}, u32[]{:S(2)}) collective-permute-start(f32[64,256]{1,0:T(8,128)S(1)} %pad_maximum_fusion.9), channel_id=1, source_target_pairs={{0,32},{4,36},{8,40},{12,44},{16,48},{20,52},{24,56},{28,60},{32,0... | collective-permute-start | bytes 196616 | tf_op jit(solution)/shard_map/ppermute | solution.py:22
  57.2 11.8 %collective-permute-start.9 = (f32[256,128]{1,0:T(8,128)S(1)}, f32[256,128]{1,0:T(8,128)S(1)}, u32[]{:S(2)}, u32[]{:S(2)}) collective-permute-start(f32[256,128]{1,0:T(8,128)S(1)} %pad_maximum_fusion.4), channel_id=1, source_target_pairs={{0,64},{4,68},{8,72},{12,76},{16,80},{20,84},{24,88},{28,92},{32,9... | collective-permute-start | bytes 393224 | tf_op jit(solution)/shard_map/ppermute | solution.py:22
  60.9 8.1 %collective-permute-start.8 = (f32[64,256]{1,0:T(8,128)S(1)}, f32[64,256]{1,0:T(8,128)S(1)}, u32[]{:S(2)}, u32[]{:S(2)}) collective-permute-start(f32[64,256]{1,0:T(8,128)S(1)} %pad_maximum_fusion.10), channel_id=1, source_target_pairs={{0,64},{4,68},{8,72},{12,76},{16,80},{20,84},{24,88},{28,92},{32,9... | collective-permute-start | bytes 196616 | tf_op jit(solution)/shard_map/ppermute | solution.py:22
  70.1 21.4 %collective-permute-start.11 = (f32[256,128]{1,0:T(8,128)S(1)}, f32[256,128]{1,0:T(8,128)S(1)}, u32[]{:S(2)}, u32[]{:S(2)}) collective-permute-start(f32[256,128]{1,0:T(8,128)S(1)} %pad_maximum_fusion.5), channel_id=1, source_target_pairs={{0,128},{4,132},{8,136},{12,140},{16,144},{20,148},{24,152},{28,15... | collective-permute-start | bytes 393224 | tf_op jit(solution)/shard_map/ppermute | solution.py:22
  78.7 12.8 %collective-permute-start.10 = (f32[64,256]{1,0:T(8,128)S(1)}, f32[64,256]{1,0:T(8,128)S(1)}, u32[]{:S(2)}, u32[]{:S(2)}) collective-permute-start(f32[64,256]{1,0:T(8,128)S(1)} %pad_maximum_fusion.11), channel_id=1, source_target_pairs={{0,128},{4,132},{8,136},{12,140},{16,144},{20,148},{24,152},{28,15... | collective-permute-start | bytes 196616 | tf_op jit(solution)/shard_map/ppermute | solution.py:22
  92.8 14.3 %collective-permute-start.13 = (f32[128,128]{1,0:T(8,128)}, f32[128,128]{1,0:T(8,128)S(1)}, u32[]{:S(2)}, u32[]{:S(2)}) collective-permute-start(f32[128,128]{1,0:T(8,128)} %slice_add_fusion), channel_id=1, source_target_pairs={{0,384},{4,388},{8,392},{12,396},{16,400},{20,404},{24,408},{28,41... | collective-permute-start | bytes 196616 | tf_op jit(solution)/shard_map/ppermute | solution.py:22
  103.5 10.1 %collective-permute-start.12 = (f32[64,256]{1,0:T(8,128)S(1)}, f32[64,256]{1,0:T(8,128)S(1)}, u32[]{:S(2)}, u32[]{:S(2)}) collective-permute-start(f32[64,256]{1,0:T(8,128)S(1)} %pad_maximum_fusion.12), channel_id=1, source_target_pairs={{0,384},{4,388},{8,392},{12,396},{16,400},{20,404},{24,408},{28,41... | collective-permute-start | bytes 196616 | tf_op jit(solution)/shard_map/ppermute | solution.py:22
  124.9 1.0 copy-start.5

commit v2 on v1

--- a/solution.py
+++ b/solution.py
@@ -27,36 +27,61 @@
     return gain, jnp.concatenate([gain[TILE:], -dot(gain, gain, ((0,), (0,)))], axis=0)
 
 
-def subtree_forward(subtree_inverse, rhs_sub, live, block, rows, rhs_level, inverse):
-    masked = jnp.where(live, rhs_sub, jnp.zeros_like(rhs_sub))
-    solved = jnp.dot(subtree_inverse, masked, preferred_element_type=jnp.float32)
-    forward_sub = jnp.where(live, solved, jnp.zeros_like(solved)).astype(jnp.bfloat16)
-    contrib = jnp.dot(block, forward_sub, preferred_element_type=jnp.float32)
-    contrib = contrib.reshape(rows.shape[0], TILE, -1)
-    tiles = inverse.shape[0] // TILE
-    placed = [
-        sum(jnp.where(rows[t] == s, contrib[t], 0.0) for t in range(rows.shape[0]))
-        for s in range(tiles)
-    ]
-    rest = 0.25 * rhs_level - jnp.concatenate(placed, axis=0)
-    return forward_sub, dot(rest, inverse, ((0,), (1,)))
+def live_columns(tiles_ref, rows, columns):
+    return lax.broadcasted_iota(jnp.int32, (rows, columns), 1) < TILE * tiles_ref[...]
 
 
-def subtree_backward(solution, forward_sub, subtree_inverse, live, block, rows):
-    rounded = solution.astype(jnp.bfloat16)
-    picked = jnp.concatenate(
-        [
-            jnp.where(rows[t] == 0, rounded[:TILE], rounded[TILE:])
-            for t in range(rows.shape[0])
-        ],
-        axis=0,
-    )
-    pulled = dot(block, picked, ((0,), (0,)), None)
-    residue = (forward_sub.astype(jnp.float32) - jnp.where(live, pulled, 0.0)).astype(
-        jnp.bfloat16
-    )
-    final = dot(subtree_inverse, residue, ((0,), (0,)), None)
-    return jnp.where(live, final, 0.0)
+def subtree_forward_kernel(
+    subtree_inverse_ref, rhs_ref, tiles_ref, update_ref, rows_ref, level_rhs_ref, inverse_ref,
+    forward_ref, part_ref,
+):
+    columns, sub_rows = forward_ref.shape
+    live = live_columns(tiles_ref, columns, sub_rows)
+    masked = jnp.where(live, rhs_ref[...].astype(jnp.float32).T, 0.0).astype(jnp.bfloat16)
+    solved = dot(masked, subtree_inverse_ref[...], ((1,), (1,)), None)
+    forward = jnp.where(live, solved, 0.0).astype(jnp.bfloat16)
+    forward_ref[...] = forward
+    contrib = dot(forward, update_ref[...], ((1,), (1,)), None)
+    totals = []
+    for s in range(inverse_ref.shape[0] // TILE):
+        total = jnp.zeros((columns, TILE), jnp.float32)
+        for t in range(rows_ref.shape[1]):
+            here = rows_ref[:, t : t + 1] == s
+            total = total + jnp.where(here, contrib[:, t * TILE : (t + 1) * TILE], 0.0)
+        totals.append(total)
+    rest = 0.25 * level_rhs_ref[...].T - jnp.concatenate(totals, axis=1)
+    part_ref[...] = dot(rest, inverse_ref[...], ((1,), (1,)))
+
+
+def subtree_backward_kernel(
+    solution_ref, forward_ref, subtree_inverse_ref, tiles_ref, update_ref, rows_ref,
+    level_ref, final_ref,
+):
+    columns, sub_rows = forward_ref.shape
+    live = live_columns(tiles_ref, columns, sub_rows)
+    level_ref[...] = solution_ref[...].T
+    picked = []
+    for t in range(rows_ref.shape[1]):
+        tile = solution_ref[:, :TILE]
+        for s in range(1, solution_ref.shape[1] // TILE):
+            here = rows_ref[:, t : t + 1] == s
+            tile = jnp.where(here, solution_ref[:, s * TILE : (s + 1) * TILE], tile)
+        picked.append(tile.astype(jnp.bfloat16))
+    pulled = dot(jnp.concatenate(picked, axis=1), update_ref[...], precision=None)
+    residue = forward_ref[...].astype(jnp.float32) - jnp.where(live, pulled, 0.0)
+    final = dot(residue.astype(jnp.bfloat16), subtree_inverse_ref[...], precision=None)
+    final_ref[...] = jnp.where(live, final, 0.0).T
+
+
+def local_call(kernel, out_shape, *operands):
+    vmem = pl.BlockSpec(memory_space=pltpu.VMEM)
+    return pl.pallas_call(
+        kernel,
+        out_shape=out_shape,
+        in_specs=[vmem] * len(operands),
+        out_specs=[vmem] * len(out_shape),
+        compiler_params=pltpu.CompilerParams(vmem_limit_bytes=24 * 2**20),
+    )(*operands)
 
 
 def shards(
@@ -64,13 +89,17 @@
 ):
     count, reps = lax.axis_size("chain"), lax.axis_size("rep")
     place = lax.axis_index("chain")
-    subtree_inverse, block, rows = sub_inverse[0, 0], update[0, 0], update_rows[0, 0]
-    inverse, couple = level_inverse[0], coupling[0]
-    sub_rows = subtree_inverse.shape[0]
-    live = lax.broadcasted_iota(jnp.int32, (sub_rows, 1), 0) < TILE * sub_tiles[0, 0]
+    subtree_inverse, rhs_sub, block, rows = sub_inverse[0, 0], sub_rhs[0, 0], update[0, 0], update_rows[0]
+    inverse, couple, rhs_level = level_inverse[0], coupling[0], level_rhs[0]
+    sub_rows, width = subtree_inverse.shape[0], rhs_level.shape[1]
     gain, maps = level_maps(inverse, couple)
-    forward_sub, part = subtree_forward(
-        subtree_inverse, sub_rhs[0, 0], live, block, rows, level_rhs[0], inverse
+    forward_sub, part = local_call(
+        subtree_forward_kernel,
+        [
+            jax.ShapeDtypeStruct((width, sub_rows), jnp.bfloat16),
+            jax.ShapeDtypeStruct((width, inverse.shape[0]), jnp.float32),
+        ],
+        subtree_inverse, rhs_sub, sub_tiles, block, rows, rhs_level, inverse,
     )
     columns = part.shape[0] // reps
     parts = lax.all_to_all(part.reshape(reps, columns, -1), "rep", 0, 0)
@@ -126,8 +155,14 @@
     spread = lax.all_to_all(
         jnp.broadcast_to(share[None], (reps,) + share.shape), "rep", 0, 0
     )
-    solution = spread.reshape(-1, share.shape[1]).T
-    final = subtree_backward(solution, forward_sub, subtree_inverse, live, block, rows)
+    solution, final = local_call(
+        subtree_backward_kernel,
+        [
+            jax.ShapeDtypeStruct((inverse.shape[0], width), jnp.float32),
+            jax.ShapeDtypeStruct((sub_rows, width), jnp.float32),
+        ],
+        spread.reshape(width, -1), forward_sub, subtree_inverse, sub_tiles, block, rows,
+    )
     return (solution[None], final[None, None])
 
 

time: 129 us -> 127 us (0.984)
  between operations: 9.95 us -> 2.23 us
  Pallas kernels: 0 us -> 3.34 us
  local copies, waits for them, and re-layouts: 6.19 us -> 8.57 us
  waiting for transfers between devices: 31.3 us -> 29.1 us
    pallas_call x0 -> x2, Pallas kernels: none -> 3.34 us  [local_call(): pl.pallas_call(kernel, out_shape=out_shape, in_specs=[vmem] * len(operand...]
    unnamed x26 -> x43, local copies, waits for them, and re-layouts: 4.92 us -> 7.96 us
    ppermute x14, waiting for transfers between devices: 28.3 us -> 26.1 us  [swap(): lax.ppermute(value, 'chain', [(k, k ^ SWAP[j]) for k in range(count)])]
    dot_general x50 -> x48, matrix products: 14.5 us -> 16 us  [dot(): lax.dot_general(a, b, (dims, ((), ())), precision=precision, preferred_el...]
  transfers between devices with their start and end apart: 15 -> 15, of which waited for: 9 -> 8; matrix products, arithmetic and copies ran while one was open for 7% -> 7% of each run, Pallas kernels for 0% -> 1%
where the time goes in v2:
time: 127 us; the launch traced here: 126 us
  starting transfers between devices  56.8 us (45%)
  waiting for transfers between devices  29.1 us (23%)
  matrix products  16 us (13%)
  blocking collectives  9.07 us (7%)
  local copies, waits for them, and re-layouts  8.57 us (7%)
  Pallas kernels  3.34 us (3%)
  between operations  2.23 us (2%)
    ppermute x14, starting transfers between devices, swap(): lax.ppermute(value, 'chain', [(k, k ^ SWAP[j]) for k in range(count)])  52.5 us
    ppermute x14, waiting for transfers between devices, swap(): lax.ppermute(value, 'chain', [(k, k ^ SWAP[j]) for k in range(count)])  26.1 us
    dot_general x48, matrix products, dot(): lax.dot_general(a, b, (dims, ((), ())), precision=precision, preferred_el...  16 us
    all_to_all x1, blocking collectives, shards(): lax.all_to_all(jnp.broadcast_to(share[None], (reps,) + share.shape), 'rep...  9.07 us
    unnamed x43, local copies, waits for them, and re-layouts  7.96 us
    all_to_all x1, starting transfers between devices, shards(): parts = lax.all_to_all(part.reshape(reps, columns, -1), 'rep', 0, 0)  4.29 us
    pallas_call x2, Pallas kernels, local_call(): pl.pallas_call(kernel, out_shape=out_shape, in_specs=[vmem] * len(operand...  3.34 us
    all_to_all x1, waiting for transfers between devices, shards(): parts = lax.all_to_all(part.reshape(reps, columns, -1), 'rep', 0, 0)  3 us
  transfers between devices with their start and end apart: 15, of which 8 were waited for; matrix products, arithmetic and copies ran while one was open for 7% of the time, Pallas kernels for 1%

profile of v2, /device:TPU:96, one launch (start us, length us, event | category | flops | bytes accessed | tf_op | source)
XLA Modules:
  0.0 126.1 jit_solution(1594134243440988402)
XLA Ops:
  0.7 0.9 copy-done
  1.5 1.3 %convolution_negate_fusion = f32[256,128]{1,0:T(8,128)S(1)} fusion(f32[1,256,128]{2,1,0:T(8,128)S(1)} %copy-done, f32[1,256,256]{2,1,0:T(8,128)} %param.13), kind=kOutput, calls=%fused_computation | convolution fusion | flops 100696064 | bytes 524288 | tf_op jit(solution)/shard_map/dot_general | solution.py:16
  3.3 2.1 %collective-permute-start.1 = (f32[256,128]{1,0:T(8,128)S(1)}, f32[256,128]{1,0:T(8,128)S(1)}, u32[]{:S(2)}, u32[]{:S(2)}) collective-permute-start(f32[256,128]{1,0:T(8,128)S(1)} %pad_maximum_fusion), channel_id=1, source_target_pairs={{0,4},{4,0},{8,12},{12,8},{16,20},{20,16},{24,28},{28,24},{32,36},... | collective-permute-start | bytes 393224 | tf_op jit(solution)/shard_map/ppermute | solution.py:22
  6.7 0.9 copy-done.4
  7.6 0.9 copy-done.5
  8.6 1.9 %shard_map.95 = (bf16[256,384]{1,0:T(8,128)(2,1)S(1)}, f32[256,256]{1,0:T(8,128)}) custom-call(bf16[384,384]{1,0:T(8,128)(2,1)S(1)} %bitcast.53, bf16[384,256]{1,0:T(8,128)(2,1)S(1)} %bitcast.57, s32[1,1]{1,0:T(1,128)S(6)} %copy.26.tiles_ref, bf16[768,384]{1,0:T(8,128)(2,1)S(1)} %bitcast.50, s32[1,6]{1,0:T(1,128)S(1)} %bitcast.58, f32[256,256]{1,0:T(8,128)S(1)} %bitcast.56, ...), custom_call_target="tpu_custom_call" | custom-call | tf_op jit(solution)/shard_map/pallas_call | solution.py:78
  10.4 4.3 %all-to-all-start = ((f32[4,64,256]{2,1,0:T(8,128)}), f32[4,64,256]{2,1,0:T(8,128)S(1)}, u32[]{:S(2)}, u32[]{:S(2)}) async-start(f32[4,64,256]{2,1,0:T(8,128)} %bitcast.6), calls=%async_computation | async-start | bytes 524288 | tf_op jit(solution)/shard_map/all_to_all | solution.py:105
  15.3 3.5 %collective-permute-start.3 = (f32[256,128]{1,0:T(8,128)S(1)}, f32[256,128]{1,0:T(8,128)S(1)}, u32[]{:S(2)}, u32[]{:S(2)}) collective-permute-start(f32[256,128]{1,0:T(8,128)S(1)} %pad_maximum_fusion.1), channel_id=1, source_target_pairs={{0,8},{4,12},{8,0},{12,4},{16,24},{20,28},{24,16},{28,20},{32,40},... | collective-permute-start | bytes 393224 | tf_op jit(solution)/shard_map/ppermute | solution.py:22
  19.0 3.0 %all-to-all-done = f32[4,64,256]{2,1,0:T(8,128)S(1)} async-done(((f32[4,64,256]{2,1,0:T(8,128)}), f32[4,64,256]{2,1,0:T(8,128)S(1)}, u32[]{:S(2)}, u32[]{:S(2)}) %all-to-all-start) | async-done | bytes 262176 | tf_op jit(solution)/shard_map/all_to_all | solution.py:105
  22.3 1.9 %collective-permute-start = (f32[64,256]{1,0:T(8,128)S(1)}, f32[64,256]{1,0:T(8,128)S(1)}, u32[]{:S(2)}, u32[]{:S(2)}) collective-permute-start(f32[64,256]{1,0:T(8,128)S(1)} %pad_maximum_fusion.6), channel_id=1, source_target_pairs={{0,4},{4,0},{8,12},{12,8},{16,20},{20,16},{24,28},{28,24},{32,36},... | collective-permute-start | bytes 196616 | tf_op jit(solution)/shard_map/ppermute | solution.py:22
  24.2 0.8 fusion.49
  26.9 3.5 %collective-permute-start.2 = (f32[64,256]{1,0:T(8,128)S(1)}, f32[64,256]{1,0:T(8,128)S(1)}, u32[]{:S(2)}, u32[]{:S(2)}) collective-permute-start(f32[64,256]{1,0:T(8,128)S(1)} %pad_maximum_fusion.7), channel_id=1, source_target_pairs={{0,8},{4,12},{8,0},{12,4},{16,24},{20,28},{24,16},{28,20},{32,40},... | collective-permute-start | bytes 196616 | tf_op jit(solution)/shard_map/ppermute | solution.py:22
  30.5 4.1 %collective-permute-start.5 = (f32[256,128]{1,0:T(8,128)S(1)}, f32[256,128]{1,0:T(8,128)S(1)}, u32[]{:S(2)}, u32[]{:S(2)}) collective-permute-start(f32[256,128]{1,0:T(8,128)S(1)} %pad_maximum_fusion.2), channel_id=1, source_target_pairs={{0,24},{4,28},{8,16},{12,20},{16,8},{20,12},{24,0},{28,4},{32,56},... | collective-permute-start | bytes 393224 | tf_op jit(solution)/shard_map/ppermute | solution.py:22
  35.6 3.3 %collective-permute-start.4 = (f32[64,256]{1,0:T(8,128)S(1)}, f32[64,256]{1,0:T(8,128)S(1)}, u32[]{:S(2)}, u32[]{:S(2)}) collective-permute-start(f32[64,256]{1,0:T(8,128)S(1)} %pad_maximum_fusion.8), channel_id=1, source_target_pairs={{0,24},{4,28},{8,16},{12,20},{16,8},{20,12},{24,0},{28,4},{32,56},... | collective-permute-start | bytes 196616 | tf_op jit(solution)/shard_map/ppermute | solution.py:22
  39.8 2.0 %collective-permute-start.7 = (f32[256,128]{1,0:T(8,128)S(1)}, f32[256,128]{1,0:T(8,128)S(1)}, u32[]{:S(2)}, u32[]{:S(2)}) collective-permute-start(f32[256,128]{1,0:T(8,128)S(1)} %pad_maximum_fusion.3), channel_id=1, source_target_pairs={{0,32},{4,36},{8,40},{12,44},{16,48},{20,52},{24,56},{28,60},{32,0... | collective-permute-start | bytes 393224 | tf_op jit(solution)/shard_map/ppermute | solution.py:22
  41.8 1.2 collective-permute-done.4
  43.7 2.7 %collective-permute-start.6 = (f32[64,256]{1,0:T(8,128)S(1)}, f32[64,256]{1,0:T(8,128)S(1)}, u32[]{:S(2)}, u32[]{:S(2)}) collective-permute-start(f32[64,256]{1,0:T(8,128)S(1)} %pad_maximum_fusion.9), channel_id=1, source_target_pairs={{0,32},{4,36},{8,40},{12,44},{16,48},{20,52},{24,56},{28,60},{32,0... | collective-permute-start | bytes 196616 | tf_op jit(solution)/shard_map/ppermute | solution.py:22
  47.4 2.5 %collective-permute-done.6 = f32[64,256]{1,0:T(8,128)S(1)} collective-permute-done((f32[64,256]{1,0:T(8,128)S(1)}, f32[64,256]{1,0:T(8,128)S(1)}, u32[]{:S(2)}, u32[]{:S(2)}) %collective-permute-start.6) | collective-permute-done | bytes 65568 | tf_op jit(solution)/shard_map/ppermute | solution.py:22
  50.9 3.9 %collective-permute-start.9 = (f32[256,128]{1,0:T(8,128)S(1)}, f32[256,128]{1,0:T(8,128)S(1)}, u32[]{:S(2)}, u32[]{:S(2)}) collective-permute-start(f32[256,128]{1,0:T(8,128)S(1)} %pad_maximum_fusion.4), channel_id=1, source_target_pairs={{0,64},{4,68},{8,72},{12,76},{16,80},{20,84},{24,88},{28,92},{32,9... | collective-permute-start | bytes 393224 | tf_op jit(solution)/shard_map/ppermute | solution.py:22
  55.0 2.9 %collective-permute-start.8 = (f32[64,256]{1,0:T(8,128)S(1)}, f32[64,256]{1,0:T(8,128)S(1)}, u32[]{:S(2)}, u32[]{:S(2)}) collective-permute-start(f32[64,256]{1,0:T(8,128)S(1)} %pad_maximum_fusion.10), channel_id=1, source_target_pairs={{0,64},{4,68},{8,72},{12,76},{16,80},{20,84},{24,88},{28,92},{32,9... | collective-permute-start | bytes 196616 | tf_op jit(solution)/shard_map/ppermute | solution.py:22
  58.9 4.0 %collective-permute-done.8 = f32[64,256]{1,0:T(8,128)S(1)} collective-permute-done((f32[64,256]{1,0:T(8,128)S(1)}, f32[64,256]{1,0:T(8,128)S(1)}, u32[]{:S(2)}, u32[]{:S(2)}) %collective-permute-start.8) | collective-permute-done | bytes 65568 | tf_op jit(solution)/shard_map/ppermute | solution.py:22
  65.2 8.6 %collective-permute-start.11 = (f32[256,128]{1,0:T(8,128)}, f32[256,128]{1,0:T(8,128)S(1)}, u32[]{:S(2)}, u32[]{:S(2)}) collective-permute-start(f32[256,128]{1,0:T(8,128)} %pad_maximum_fusion.5), channel_id=1, source_target_pairs={{0,128},{4,132},{8,136},{12,140},{16,144},{20,148},{24,152},{28,15... | collective-permute-start | bytes 393224 | tf_op jit(solution)/shard_map/ppermute | solution.py:22
  74.0 1.9 %collective-permute-start.10 = (f32[64,256]{1,0:T(8,128)S(1)}, f32[64,256]{1,0:T(8,128)S(1)}, u32[]{:S(2)}, u32[]{:S(2)}) collective-permute-start(f32[64,256]{1,0:T(8,128)S(1)} %pad_maximum_fusion.11), channel_id=1, source_target_pairs={{0,128},{4,132},{8,136},{12,140},{16,144},{20,148},{24,152},{28,15... | collective-permute-start | bytes 196616 | tf_op jit(solution)/shard_map/ppermute | solution.py:22
  76.9 10.2 %collective-permute-done.10 = f32[64,256]{1,0:T(8,128)S(1)} collective-permute-done((f32[64,256]{1,0:T(8,128)S(1)}, f32[64,256]{1,0:T(8,128)S(1)}, u32[]{:S(2)}, u32[]{:S(2)}) %collective-permute-start.10) | collective-permute-done | bytes 65568 | tf_op jit(solution)/shard_map/ppermute | solution.py:22
  88.1 0.9 slice_add_fusion
  89.0 10.3 %collective-permute-start.13 = (f32[128,128]{1,0:T(8,128)}, f32[128,128]{1,0:T(8,128)}, u32[]{:S(2)}, u32[]{:S(2)}) collective-permute-start(f32[128,128]{1,0:T(8,128)} %slice_add_fusion), channel_id=1, source_target_pairs={{0,384},{4,388},{8,392},{12,396},{16,400},{20,404},{24,408},{28,41... | collective-permute-start | bytes 196616 | tf_op jit(solution)/shard_map/ppermute | solution.py:22
  100.1 1.9 %collective-permute-start.12 = (f32[64,256]{1,0:T(8,128)S(1)}, f32[64,256]{1,0:T(8,128)}, u32[]{:S(2)}, u32[]{:S(2)}) collective-permute-start(f32[64,256]{1,0:T(8,128)S(1)} %pad_maximum_fusion.12), channel_id=1, source_target_pairs={{0,384},{4,388},{8,392},{12,396},{16,400},{20,404},{24,408},{28,41... | collective-permute-start | bytes 196616 | tf_op jit(solution)/shard_map/ppermute | solution.py:22
  102.3 2.4 %collective-permute-done.13 = f32[128,128]{1,0:T(8,128)} collective-permute-done((f32[128,128]{1,0:T(8,128)}, f32[128,128]{1,0:T(8,128)}, u32[]{:S(2)}, u32[]{:S(2)}) %collective-permute-start.13) | collective-permute-done | bytes 65568 | tf_op jit(solution)/shard_map/ppermute | solution.py:22
  104.7 5.5 %collective-permute-done.12 = f32[64,256]{1,0:T(8,128)} collective-permute-done((f32[64,256]{1,0:T(8,128)S(1)}, f32[64,256]{1,0:T(8,128)}, u32[]{:S(2)}, u32[]{:S(2)}) %collective-permute-start.12) | collective-permute-done | bytes 65568 | tf_op jit(solution)/shard_map/ppermute | solution.py:22
  110.2 1.0 broadcast_select_fusion.25
  115.5 9.1 %all_to_all.10 = f32[4,64,256]{2,1,0:T(8,128)S(1)} all-to-all(f32[4,64,256]{2,1,0:T(8,128)S(1)} %broadcast_in_dim.16), channel_id=1, replica_groups=mesh['chain'=128,'rep'=4] {'rep'}, dimensions={0} | all-to-all | bytes 524288 | tf_op jit(solution)/shard_map/all_to_all | solution.py:155
  124.6 1.5 %shard_map.96 = (f32[256,256]{1,0:T(8,128)}, f32[384,256]{1,0:T(8,128)}) custom-call(f32[256,256]{1,0:T(8,128)S(1)} %bitcast.55, bf16[256,384]{1,0:T(8,128)(2,1)S(1)} %get-tuple-element.7.forward_ref, bf16[384,384]{1,0:T(8,128)(2,1)S(1)} %bitcast.54, s32[1,1]{1,0:T(1,128)S(6)} %copy.26.tiles_ref, bf16[768,384]{1,0:T(8,128)(2,1)S(1)} %bitcast.51, ...), custom_call_target="tpu_custom_call" | custom-call | tf_op jit(solution)/shard_map/pallas_call | solution.py:78
  (135 shorter events, 19.0 us)
Async XLA Ops:
  0.6 0.9 copy-start
  0.6 5.4 %copy-start.1 = (bf16[1,1,768,384]{3,2,1,0:T(8,128)(2,1)S(1)}, bf16[1,1,768,384]{3,2,1,0:T(8,128)(2,1)}, u32[]{:S(2)}) copy-start(bf16[1,1,768,384]{3,2,1,0:T(8,128)(2,1)} %param.11) | copy-start | bytes 1769476
  2.9 3.2 %copy-start.3 = (bf16[1,1,384,384]{3,2,1,0:T(8,128)(2,1)S(1)}, bf16[1,1,384,384]{3,2,1,0:T(8,128)(2,1)}, u32[]{:S(2)}) copy-start(bf16[1,1,384,384]{3,2,1,0:T(8,128)(2,1)} %param.8) | copy-start | bytes 884740
  3.3 2.8 %copy-start.2 = (f32[1,256,256]{2,1,0:T(8,128)S(1)}, f32[1,256,256]{2,1,0:T(8,128)}, u32[]{:S(2)}) copy-start(f32[1,256,256]{2,1,0:T(8,128)} %param.13) | copy-start | bytes 786436
  3.3 11.4 %collective-permute-start.1 = (f32[256,128]{1,0:T(8,128)S(1)}, f32[256,128]{1,0:T(8,128)S(1)}, u32[]{:S(2)}, u32[]{:S(2)}) collective-permute-start(f32[256,128]{1,0:T(8,128)S(1)} %pad_maximum_fusion), channel_id=1, source_target_pairs={{0,4},{4,0},{8,12},{12,8},{16,20},{20,16},{24,28},{28,24},{32,36},... | collective-permute-start | bytes 393224 | tf_op jit(solution)/shard_map/ppermute | solution.py:22
  6.0 0.7 copy-start.6
  6.7 0.9 copy-start.4
  7.6 0.9 copy-start.5
  10.4 11.6 %all-to-all-start = ((f32[4,64,256]{2,1,0:T(8,128)}), f32[4,64,256]{2,1,0:T(8,128)S(1)}, u32[]{:S(2)}, u32[]{:S(2)}) async-start(f32[4,64,256]{2,1,0:T(8,128)} %bitcast.6), calls=%async_computation | async-start | bytes 524288 | tf_op jit(solution)/shard_map/all_to_all | solution.py:105
  15.3 9.7 %collective-permute-start.3 = (f32[256,128]{1,0:T(8,128)S(1)}, f32[256,128]{1,0:T(8,128)S(1)}, u32[]{:S(2)}, u32[]{:S(2)}) collective-permute-start(f32[256,128]{1,0:T(8,128)S(1)} %pad_maximum_fusion.1), channel_id=1, source_target_pairs={{0,8},{4,12},{8,0},{12,4},{16,24},{20,28},{24,16},{28,20},{32,40},... | collective-permute-start | bytes 393224 | tf_op jit(solution)/shard_map/ppermute | solution.py:22
  22.3 3.3 %collective-permute-start = (f32[64,256]{1,0:T(8,128)S(1)}, f32[64,256]{1,0:T(8,128)S(1)}, u32[]{:S(2)}, u32[]{:S(2)}) collective-permute-start(f32[64,256]{1,0:T(8,128)S(1)} %pad_maximum_fusion.6), channel_id=1, source_target_pairs={{0,4},{4,0},{8,12},{12,8},{16,20},{20,16},{24,28},{28,24},{32,36},... | collective-permute-start | bytes 196616 | tf_op jit(solution)/shard_map/ppermute | solution.py:22
  25.7 0.6 copy-start.11
  26.9 8.0 %collective-permute-start.2 = (f32[64,256]{1,0:T(8,128)S(1)}, f32[64,256]{1,0:T(8,128)S(1)}, u32[]{:S(2)}, u32[]{:S(2)}) collective-permute-start(f32[64,256]{1,0:T(8,128)S(1)} %pad_maximum_fusion.7), channel_id=1, source_target_pairs={{0,8},{4,12},{8,0},{12,4},{16,24},{20,28},{24,16},{28,20},{32,40},... | collective-permute-start | bytes 196616 | tf_op jit(solution)/shard_map/ppermute | solution.py:22
  30.5 8.7 %collective-permute-start.5 = (f32[256,128]{1,0:T(8,128)S(1)}, f32[256,128]{1,0:T(8,128)S(1)}, u32[]{:S(2)}, u32[]{:S(2)}) collective-permute-start(f32[256,128]{1,0:T(8,128)S(1)} %pad_maximum_fusion.2), channel_id=1, source_target_pairs={{0,24},{4,28},{8,16},{12,20},{16,8},{20,12},{24,0},{28,4},{32,56},... | collective-permute-start | bytes 393224 | tf_op jit(solution)/shard_map/ppermute | solution.py:22
  35.6 7.4 %collective-permute-start.4 = (f32[64,256]{1,0:T(8,128)S(1)}, f32[64,256]{1,0:T(8,128)S(1)}, u32[]{:S(2)}, u32[]{:S(2)}) collective-permute-start(f32[64,256]{1,0:T(8,128)S(1)} %pad_maximum_fusion.8), channel_id=1, source_target_pairs={{0,24},{4,28},{8,16},{12,20},{16,8},{20,12},{24,0},{28,4},{32,56},... | collective-permute-start | bytes 196616 | tf_op jit(solution)/shard_map/ppermute | solution.py:22
  39.8 10.0 %collective-permute-start.7 = (f32[256,128]{1,0:T(8,128)S(1)}, f32[256,128]{1,0:T(8,128)S(1)}, u32[]{:S(2)}, u32[]{:S(2)}) collective-permute-start(f32[256,128]{1,0:T(8,128)S(1)} %pad_maximum_fusion.3), channel_id=1, source_target_pairs={{0,32},{4,36},{8,40},{12,44},{16,48},{20,52},{24,56},{28,60},{32,0... | collective-permute-start | bytes 393224 | tf_op jit(solution)/shard_map/ppermute | solution.py:22
  43.7 6.2 %collective-permute-start.6 = (f32[64,256]{1,0:T(8,128)S(1)}, f32[64,256]{1,0:T(8,128)S(1)}, u32[]{:S(2)}, u32[]{:S(2)}) collective-permute-start(f32[64,256]{1,0:T(8,128)S(1)} %pad_maximum_fusion.9), channel_id=1, source_target_pairs={{0,32},{4,36},{8,40},{12,44},{16,48},{20,52},{24,56},{28,60},{32,0... | collective-permute-start | bytes 196616 | tf_op jit(solution)/shard_map/ppermute | solution.py:22
  50.9 12.6 %collective-permute-start.9 = (f32[256,128]{1,0:T(8,128)S(1)}, f32[256,128]{1,0:T(8,128)S(1)}, u32[]{:S(2)}, u32[]{:S(2)}) collective-permute-start(f32[256,128]{1,0:T(8,128)S(1)} %pad_maximum_fusion.4), channel_id=1, source_target_pairs={{0,64},{4,68},{8,72},{12,76},{16,80},{20,84},{24,88},{28,92},{32,9... | collective-permute-start | bytes 393224 | tf_op jit(solution)/shard_map/ppermute | solution.py:22
  55.0 7.9 %collective-permute-start.8 = (f32[64,256]{1,0:T(8,128)S(1)}, f32[64,256]{1,0:T(8,128)S(1)}, u32[]{:S(2)}, u32[]{:S(2)}) collective-permute-start(f32[64,256]{1,0:T(8,128)S(1)} %pad_maximum_fusion.10), channel_id=1, source_target_pairs={{0,64},{4,68},{8,72},{12,76},{16,80},{20,84},{24,88},{28,92},{32,9... | collective-permute-start | bytes 196616 | tf_op jit(solution)/shard_map/ppermute | solution.py:22
  62.9 0.6 copy-start.7
  65.2 22.6 %collective-permute-start.11 = (f32[256,128]{1,0:T(8,128)}, f32[256,128]{1,0:T(8,128)S(1)}, u32[]{:S(2)}, u32[]{:S(2)}) collective-permute-start(f32[256,128]{1,0:T(8,128)} %pad_maximum_fusion.5), channel_id=1, source_target_pairs={{0,128},{4,132},{8,136},{12,140},{16,144},{20,148},{24,152},{28,15... | collective-permute-start | bytes 393224 | tf_op jit(solution)/shard_map/ppermute | solution.py:22
  74.0 13.2 %collective-permute-start.10 = (f32[64,256]{1,0:T(8,128)S(1)}, f32[64,256]{1,0:T(8,128)S(1)}, u32[]{:S(2)}, u32[]{:S(2)}) collective-permute-start(f32[64,256]{1,0:T(8,128)S(1)} %pad_maximum_fusion.11), channel_id=1, source_target_pairs={{0,128},{4,132},{8,136},{12,140},{16,144},{20,148},{24,152},{28,15... | collective-permute-start | bytes 196616 | tf_op jit(solution)/shard_map/ppermute | solution.py:22
  87.2 0.6 copy-start.9
  89.0 15.7 %collective-permute-start.13 = (f32[128,128]{1,0:T(8,128)}, f32[128,128]{1,0:T(8,128)}, u32[]{:S(2)}, u32[]{:S(2)}) collective-permute-start(f32[128,128]{1,0:T(8,128)} %slice_add_fusion), channel_id=1, source_target_pairs={{0,384},{4,388},{8,392},{12,396},{16,400},{20,404},{24,408},{28,41... | collective-permute-start | bytes 196616 | tf_op jit(solution)/shard_map/ppermute | solution.py:22
  100.1 10.2 %collective-permute-start.12 = (f32[64,256]{1,0:T(8,128)S(1)}, f32[64,256]{1,0:T(8,128)}, u32[]{:S(2)}, u32[]{:S(2)}) collective-permute-start(f32[64,256]{1,0:T(8,128)S(1)} %pad_maximum_fusion.12), channel_id=1, source_target_pairs={{0,384},{4,388},{8,392},{12,396},{16,400},{20,404},{24,408},{28,41... | collective-permute-start | bytes 196616 | tf_op jit(solution)/shard_map/ppermute | solution.py:22
  102.3 9.0 %copy-start.10 = (f32[64,256]{1,0:T(8,128)S(1)}, f32[64,256]{1,0:T(8,128)}, u32[]{:S(2)}) copy-start(f32[64,256]{1,0:T(8,128)} %copy-done.9) | copy-start | bytes 196612
  111.3 0.8 copy-start.8
  111.3 0.8 copy-start.15
  112.1 0.8 copy-start.14
  112.9 0.8 copy-start.13
  113.9 0.8 copy-start.12
  113.9 0.8 copy-start.16

commit v3 on v2

--- a/solution.py
+++ b/solution.py
@@ -1,15 +1,13 @@
-import functools
-
 import jax
 import jax.numpy as jnp
 from jax import lax
 from jax.experimental import pallas as pl
 from jax.experimental.pallas import tpu as pltpu
-from jax.sharding import PartitionSpec as P
+from jax.sharding import Mesh, PartitionSpec as P
 
 TILE = 128
 HIGHEST = lax.Precision.HIGHEST
-SWAP = (1, 2, 6, 8, 16, 32, 96)
+SWAP = (1, 3, 4, 8, 16, 48)
 
 
 def dot(a, b, dims=((1,), (0,)), precision=HIGHEST):
@@ -19,12 +17,32 @@
 
 
 def swap(value, j, count):
-    return lax.ppermute(value, "chain", [(k, k ^ SWAP[j]) for k in range(count)])
-
-
-def level_maps(inverse, couple):
-    gain = -dot(inverse, couple)
-    return gain, jnp.concatenate([gain[TILE:], -dot(gain, gain, ((0,), (0,)))], axis=0)
+    return lax.ppermute(value, "pair", [(n, n ^ SWAP[j]) for n in range(count)])
+
+
+def join_maps(first, second):
+    product = dot(second, first[:TILE])
+    turned = dot(first[:TILE], product[TILE:], ((0,), (0,)))
+    joined = jnp.concatenate([product[:TILE], first[TILE:] + turned], axis=0)
+    upper = jnp.concatenate([second[:TILE].T, product[TILE:]], axis=1)
+    lower = jnp.concatenate([jnp.zeros_like(turned), first[:TILE]], axis=1)
+    return joined, product[TILE:], jnp.concatenate([upper, lower], axis=0)
+
+
+def join_state(first, second, weights):
+    mixed = jnp.concatenate([first[:, :TILE], second[:, TILE:]], axis=1)
+    kept = jnp.concatenate([second[:, :TILE], first[:, TILE:]], axis=1)
+    return kept + dot(mixed, weights)
+
+
+def level_state(own, gain):
+    return jnp.concatenate([own[:, TILE:], -dot(own, gain)], axis=1)
+
+
+def level_solve(own, before, after, gain, inverse):
+    forward = own + dot(before, gain, ((1,), (1,)))
+    forward = jnp.concatenate([forward[:, :TILE], forward[:, TILE:] - after], axis=1)
+    return dot(forward, inverse)
 
 
 def live_columns(tiles_ref, rows, columns):
@@ -80,31 +98,53 @@
         out_shape=out_shape,
         in_specs=[vmem] * len(operands),
         out_specs=[vmem] * len(out_shape),
-        compiler_params=pltpu.CompilerParams(vmem_limit_bytes=24 * 2**20),
+        compiler_params=pltpu.CompilerParams(vmem_limit_bytes=10 * 2**20),
     )(*operands)
 
 
 def shards(
     sub_inverse, sub_rhs, sub_tiles, update, update_rows, level_inverse, coupling, level_rhs
 ):
-    count, reps = lax.axis_size("chain"), lax.axis_size("rep")
-    place = lax.axis_index("chain")
+    count, place = lax.axis_size("pair"), lax.axis_index("pair")
+    odd = lax.axis_index("core") == 1
+    group = ("core", "rep")
+    members = lax.axis_size(group)
     subtree_inverse, rhs_sub, block, rows = sub_inverse[0, 0], sub_rhs[0, 0], update[0, 0], update_rows[0]
     inverse, couple, rhs_level = level_inverse[0], coupling[0], level_rhs[0]
-    sub_rows, width = subtree_inverse.shape[0], rhs_level.shape[1]
-    gain, maps = level_maps(inverse, couple)
+    sub_rows, width, height = subtree_inverse.shape[0], rhs_level.shape[1], inverse.shape[0]
+    gain = -dot(inverse, couple)
+    level = jnp.concatenate(
+        [
+            gain,
+            -dot(gain, gain, ((0,), (0,))),
+            inverse[:, :TILE],
+            inverse[:, TILE:],
+        ],
+        axis=0,
+    )
+    sibling = lax.ppermute(level, "core", [(0, 1), (1, 0)])
+    levels = (jnp.where(odd, sibling, level), jnp.where(odd, level, sibling))
+    gains = [pair[:height] for pair in levels]
+    inverses = [
+        jnp.concatenate([pair[height + TILE : 2 * height + TILE], pair[2 * height + TILE :]], axis=1)
+        for pair in levels
+    ]
+    pair_maps = [pair[height - TILE : height + TILE] for pair in levels]
     forward_sub, part = local_call(
         subtree_forward_kernel,
         [
             jax.ShapeDtypeStruct((width, sub_rows), jnp.bfloat16),
-            jax.ShapeDtypeStruct((width, inverse.shape[0]), jnp.float32),
+            jax.ShapeDtypeStruct((width, height), jnp.float32),
         ],
         subtree_inverse, rhs_sub, sub_tiles, block, rows, rhs_level, inverse,
     )
-    columns = part.shape[0] // reps
-    parts = lax.all_to_all(part.reshape(reps, columns, -1), "rep", 0, 0)
-    own = parts[0] + parts[1] + parts[2] + parts[3]
-    state = jnp.concatenate([own[:, TILE:], -dot(own, gain)], axis=1)
+    columns = width // members
+    parts = lax.all_to_all(part.reshape(members, columns, height), group, 0, 0)
+    reps = members // 2
+    owns = [sum(parts[c * reps + r] for r in range(reps)) for c in range(2)]
+    states = [level_state(own, g) for own, g in zip(owns, gains)]
+    maps, pair_turn, weights = join_maps(*pair_maps)
+    state = join_state(*states, weights)
     descent = []
     rounds = len(SWAP)
     for j in range(rounds):
@@ -123,42 +163,40 @@
             break
         first = jnp.where(right, other, maps)
         second = jnp.where(right, maps, other)
-        product = dot(second, first[:TILE])
-        turned = dot(first[:TILE], product[TILE:], ((0,), (0,)))
+        maps, turn, weights = join_maps(first, second)
         step = jnp.where(
             right,
-            jnp.concatenate([other[:TILE].T, jnp.zeros_like(turned)], axis=0),
-            jnp.concatenate([product[TILE:].T, other[:TILE]], axis=0),
+            jnp.concatenate([other[:TILE].T, jnp.zeros_like(turn)], axis=0),
+            jnp.concatenate([turn.T, other[:TILE]], axis=0),
         )
         descent.append((right, step, push))
         early = jnp.where(right, other_state, state)
         late = jnp.where(right, state, other_state)
-        state = jnp.concatenate(
-            [
-                late[:, :TILE] + dot(early[:, :TILE], second[:TILE], ((1,), (1,))),
-                early[:, TILE:]
-                + dot(late[:, TILE:], first[:TILE])
-                + dot(early[:, :TILE], product[TILE:]),
-            ],
-            axis=1,
-        )
-        maps = jnp.concatenate([product[:TILE], first[TILE:] + turned], axis=0)
+        state = join_state(early, late, weights)
     before = jnp.zeros((columns, TILE), jnp.float32)
     after = before
     for right, step, push in reversed(descent):
         if step is not None:
             push = push + dot(jnp.concatenate([before, after], axis=1), step)
         before, after = jnp.where(right, push, before), jnp.where(right, after, push)
-    forward = own + dot(before, gain, ((1,), (1,)))
-    forward = jnp.concatenate([forward[:, :TILE], forward[:, TILE:] - after], axis=1)
-    share = dot(forward, inverse)
+    middle_before = states[0][:, :TILE] + dot(before, pair_maps[0][:TILE], ((1,), (1,)))
+    middle_after = (
+        states[1][:, TILE:]
+        + dot(states[0][:, :TILE], pair_maps[1][TILE:])
+        + dot(before, pair_turn, ((1,), (1,)))
+        + dot(after, pair_maps[1][:TILE])
+    )
+    shares = [
+        level_solve(owns[0], before, middle_after, gains[0], inverses[0]),
+        level_solve(owns[1], middle_before, after, gains[1], inverses[1]),
+    ]
     spread = lax.all_to_all(
-        jnp.broadcast_to(share[None], (reps,) + share.shape), "rep", 0, 0
+        jnp.stack([shares[c] for c in range(2) for _ in range(reps)]), group, 0, 0
     )
     solution, final = local_call(
         subtree_backward_kernel,
         [
-            jax.ShapeDtypeStruct((inverse.shape[0], width), jnp.float32),
+            jax.ShapeDtypeStruct((height, width), jnp.float32),
             jax.ShapeDtypeStruct((sub_rows, width), jnp.float32),
         ],
         spread.reshape(width, -1), forward_sub, subtree_inverse, sub_tiles, block, rows,
@@ -167,19 +205,22 @@
 
 
 def solution(mesh):
+    chain, reps = mesh.devices.shape
+    split = Mesh(mesh.devices.reshape(chain // 2, 2, reps), ("pair", "core", "rep"))
+    both = ("pair", "core")
     return jax.shard_map(
         shards,
-        mesh=mesh,
+        mesh=split,
         in_specs=(
-            P("chain", "rep", None, None),
-            P("chain", "rep", None, None),
-            P("chain", "rep"),
-            P("chain", "rep", None, None),
-            P("chain", "rep", None),
-            P("chain", None, None),
-            P("chain", None, None),
-            P("chain", None, None),
+            P(both, "rep", None, None),
+            P(both, "rep", None, None),
+            P(both, "rep"),
+            P(both, "rep", None, None),
+            P(both, "rep", None),
+            P(both, None, None),
+            P(both, None, None),
+            P(both, None, None),
         ),
-        out_specs=(P("chain", None, None), P("chain", "rep", None, None)),
+        out_specs=(P(both, None, None), P(both, "rep", None, None)),
         check_vma=False,
     )

time: 127 us -> 143 us (1.13)
  the two profiles are of different devices: /device:TPU:96 before, /device:TPU:1 now
where the time goes in v3:
time: 143 us; the launch traced here: 142 us
  starting transfers between devices  56.2 us (39%)
  waiting for transfers between devices  23.5 us (16%)
  local copies, waits for them, and re-layouts  21.4 us (15%)
  matrix products  17.8 us (12%)
  blocking collectives  15.6 us (11%)
  Pallas kernels  3.34 us (2%)
  between operations  2.46 us (2%)
    ppermute x12, starting transfers between devices, swap(): return lax.ppermute(value, 'pair', [(n, n ^ SWAP[j]) for n in range(count)])  44 us
    dot_general x41, matrix products, dot(): lax.dot_general(a, b, (dims, ((), ())), precision=precision, preferred_el...  17.8 us
    ppermute x12, waiting for transfers between devices, swap(): return lax.ppermute(value, 'pair', [(n, n ^ SWAP[j]) for n in range(count)])  17 us
    all_to_all x1, blocking collectives, shards(): lax.all_to_all(jnp.stack([shares[c] for c in range(2) for _ in range(reps...  15.6 us
    ppermute x1, starting transfers between devices, shards(): sibling = lax.ppermute(level, 'core', [(0, 1), (1, 0)])  8.92 us
    unnamed x97, local copies, waits for them, and re-layouts  7.75 us
    all_to_all x1, waiting for transfers between devices, shards(): parts = lax.all_to_all(part.reshape(members, columns, height), group, 0, 0)  6.52 us
    slice x9, local copies, waits for them, and re-layouts, join_state(): mixed = jnp.concatenate([first[:, :TILE], second[:, TILE:]], axis=1)  4.31 us
  transfers between devices with their start and end apart: 14, of which 7 were waited for; matrix products, arithmetic and copies ran while one was open for 14% of the time, Pallas kernels for 1%

profile of v3, /device:TPU:1, one launch (start us, length us, event | category | flops | bytes accessed | tf_op | source)
XLA Modules:
  0.0 141.5 jit_solution(3764173622494072089)
XLA Ops:
  0.7 1.0 fusion.251
  2.8 8.9 %collective-permute-start = (f32[896,128]{0,1:T(8,128)S(1)}, f32[896,128]{0,1:T(8,128)S(1)}, u32[]{:S(2)}, u32[]{:S(2)}) collective-permute-start(f32[896,128]{0,1:T(8,128)S(1)} %copy.10), channel_id=1, source_target_pairs={{0,4},{4,0},{1,5},{5,1},{2,6},{6,2},{3,7},{7,3},{8,12},{12,8},{9,1... | collective-permute-start | bytes 1376264 | tf_op jit(solution)/shard_map/ppermute | solution.py:125
  13.1 1.9 %shard_map.95 = (bf16[256,384]{1,0:T(8,128)(2,1)S(1)}, f32[256,256]{1,0:T(8,128)}) custom-call(bf16[384,384]{1,0:T(8,128)(2,1)S(1)} %bitcast.72, bf16[384,256]{1,0:T(8,128)(2,1)S(1)} %bitcast.76, s32[1,1]{1,0:T(1,128)S(6)} %copy.49.tiles_ref, bf16[768,384]{1,0:T(8,128)(2,1)S(1)} %bitcast.68, s32[1,6]{1,0:T(1,128)S(1)} %bitcast.77, f32[256,256]{1,0:T(8,128)S(1)} %bitcast.75, ...), custom_call_target="tpu_custom_call" | custom-call | tf_op jit(solution)/shard_map/pallas_call | solution.py:96
  14.9 3.4 %all-to-all-start = ((f32[8,32,256]{2,1,0:T(8,128)}), f32[8,32,256]{2,1,0:T(8,128)S(1)}, u32[]{:S(2)}, u32[]{:S(2)}) async-start(f32[8,32,256]{2,1,0:T(8,128)} %bitcast.6), calls=%async_computation | async-start | bytes 524288 | tf_op jit(solution)/shard_map/all_to_all | solution.py:142
  18.3 6.5 %all-to-all-done = f32[8,32,256]{2,1,0:T(8,128)S(1)} async-done(((f32[8,32,256]{2,1,0:T(8,128)}), f32[8,32,256]{2,1,0:T(8,128)S(1)}, u32[]{:S(2)}, u32[]{:S(2)}) %all-to-all-start) | async-done | bytes 262176 | tf_op jit(solution)/shard_map/all_to_all | solution.py:142
  25.7 1.0 copy.13
  26.7 1.0 copy-done.10
  30.0 1.9 %collective-permute-start.1 = (f32[32,256]{1,0:T(8,128)S(1)}, f32[32,256]{1,0:T(8,128)S(1)}, u32[]{:S(2)}, u32[]{:S(2)}) collective-permute-start(f32[32,256]{1,0:T(8,128)S(1)} %convolution_add_fusion.2), channel_id=1, source_target_pairs={{0,8},{8,0},{16,24},{24,16},{32,40},{40,32},{48,56},{56,48},{64,72... | collective-permute-start | bytes 98312 | tf_op jit(solution)/shard_map/ppermute | solution.py:20
  31.9 3.4 %collective-permute-start.2 = (f32[256,128]{0,1:T(8,128)S(1)}, f32[256,128]{0,1:T(8,128)S(1)}, u32[]{:S(2)}, u32[]{:S(2)}) collective-permute-start(f32[256,128]{0,1:T(8,128)S(1)} %pad_maximum_fusion.1), channel_id=1, source_target_pairs={{0,8},{8,0},{16,24},{24,16},{32,40},{40,32},{48,56},{56,48},{64,72... | collective-permute-start | bytes 393224 | tf_op jit(solution)/shard_map/ppermute | solution.py:20
  35.3 3.0 %collective-permute-done.2 = f32[256,128]{0,1:T(8,128)S(1)} collective-permute-done((f32[256,128]{0,1:T(8,128)S(1)}, f32[256,128]{0,1:T(8,128)S(1)}, u32[]{:S(2)}, u32[]{:S(2)}) %collective-permute-start.2) | collective-permute-done | bytes 131104 | tf_op jit(solution)/shard_map/ppermute | solution.py:20
  39.0 1.9 %collective-permute-start.4 = (f32[256,128]{0,1:T(8,128)S(1)}, f32[256,128]{0,1:T(8,128)S(1)}, u32[]{:S(2)}, u32[]{:S(2)}) collective-permute-start(f32[256,128]{0,1:T(8,128)S(1)} %pad_maximum_fusion.2), channel_id=1, source_target_pairs={{0,24},{8,16},{16,8},{24,0},{32,56},{40,48},{48,40},{56,32},{64,88... | collective-permute-start | bytes 393224 | tf_op jit(solution)/shard_map/ppermute | solution.py:20
  41.4 4.6 %collective-permute-start.3 = (f32[32,256]{1,0:T(8,128)S(1)}, f32[32,256]{1,0:T(8,128)S(1)}, u32[]{:S(2)}, u32[]{:S(2)}) collective-permute-start(f32[32,256]{1,0:T(8,128)S(1)} %maximum_add_fusion), channel_id=1, source_target_pairs={{0,24},{8,16},{16,8},{24,0},{32,56},{40,48},{48,40},{56,32},{64,88... | collective-permute-start | bytes 98312 | tf_op jit(solution)/shard_map/ppermute | solution.py:20
  46.0 0.8 fusion.86
  49.8 1.9 %collective-permute-start.6 = (f32[256,128]{0,1:T(8,128)S(1)}, f32[256,128]{0,1:T(8,128)S(1)}, u32[]{:S(2)}, u32[]{:S(2)}) collective-permute-start(f32[256,128]{0,1:T(8,128)S(1)} %pad_maximum_fusion.3), channel_id=1, source_target_pairs={{0,32},{8,40},{16,48},{24,56},{32,0},{40,8},{48,16},{56,24},{64,96... | collective-permute-start | bytes 393224 | tf_op jit(solution)/shard_map/ppermute | solution.py:20
  52.2 3.4 %collective-permute-start.5 = (f32[32,256]{1,0:T(8,128)S(1)}, f32[32,256]{1,0:T(8,128)S(1)}, u32[]{:S(2)}, u32[]{:S(2)}) collective-permute-start(f32[32,256]{1,0:T(8,128)S(1)} %maximum_add_fusion.1), channel_id=1, source_target_pairs={{0,32},{8,40},{16,48},{24,56},{32,0},{40,8},{48,16},{56,24},{64,96... | collective-permute-start | bytes 98312 | tf_op jit(solution)/shard_map/ppermute | solution.py:20
  60.6 4.6 %collective-permute-start.8 = (f32[256,128]{0,1:T(8,128)S(1)}, f32[256,128]{0,1:T(8,128)S(1)}, u32[]{:S(2)}, u32[]{:S(2)}) collective-permute-start(f32[256,128]{0,1:T(8,128)S(1)} %pad_maximum_fusion.4), channel_id=1, source_target_pairs={{0,64},{8,72},{16,80},{24,88},{32,96},{40,104},{48,112},{56,120},{... | collective-permute-start | bytes 393224 | tf_op jit(solution)/shard_map/ppermute | solution.py:20
  65.9 1.2 maximum_add_fusion.2
  67.1 2.1 %collective-permute-start.7 = (f32[32,256]{1,0:T(8,128)S(1)}, f32[32,256]{1,0:T(8,128)S(1)}, u32[]{:S(2)}, u32[]{:S(2)}) collective-permute-start(f32[32,256]{1,0:T(8,128)S(1)} %maximum_add_fusion.2), channel_id=1, source_target_pairs={{0,64},{8,72},{16,80},{24,88},{32,96},{40,104},{48,112},{56,120},{... | collective-permute-start | bytes 98312 | tf_op jit(solution)/shard_map/ppermute | solution.py:20
  69.8 0.8 fusion.82
  71.4 2.1 %collective-permute-done.7 = f32[32,256]{1,0:T(8,128)S(1)} collective-permute-done((f32[32,256]{1,0:T(8,128)S(1)}, f32[32,256]{1,0:T(8,128)S(1)}, u32[]{:S(2)}, u32[]{:S(2)}) %collective-permute-start.7) | collective-permute-done | bytes 32800 | tf_op jit(solution)/shard_map/ppermute | solution.py:20
  77.2 8.9 %collective-permute-start.10 = (f32[256,128]{0,1:T(8,128)S(1)}, f32[256,128]{0,1:T(8,128)S(1)}, u32[]{:S(2)}, u32[]{:S(2)}) collective-permute-start(f32[256,128]{0,1:T(8,128)S(1)} %pad_maximum_fusion.5), channel_id=1, source_target_pairs={{0,128},{8,136},{16,144},{24,152},{32,160},{40,168},{48,176},{56,1... | collective-permute-start | bytes 393224 | tf_op jit(solution)/shard_map/ppermute | solution.py:20
  86.9 1.9 %maximum_add_fusion.3 = f32[32,256]{1,0:T(8,128)} fusion(f32[32,128]{1,0:T(8,128)} %get-tuple-element.71, f32[32,128]{1,0:T(8,128)} %get-tuple-element.73, f32[128,128]{0,1:T(8,128)S(1)} %copy-done.29, f32[128,128]{0,1:T(8,128)S(1)} %copy-done.28, f32[128,128]{0,1:T(8,128)} %copy.23, f32[32,128]{1,0:T(8,128)} %get-tuple-element.72, ...), kind=kOutput, calls=%fused_computation.171 | convolution fusion | flops 25452544 | bytes 294912 | tf_op jit(solution)/shard_map/dot_general | solution.py:14
  88.8 2.0 %collective-permute-start.9 = (f32[32,256]{1,0:T(8,128)}, f32[32,256]{1,0:T(8,128)S(1)}, u32[]{:S(2)}, u32[]{:S(2)}) collective-permute-start(f32[32,256]{1,0:T(8,128)} %maximum_add_fusion.3), channel_id=1, source_target_pairs={{0,128},{8,136},{16,144},{24,152},{32,160},{40,168},{48,176},{56,1... | collective-permute-start | bytes 98312 | tf_op jit(solution)/shard_map/ppermute | solution.py:20
  91.8 6.9 %collective-permute-done.9 = f32[32,256]{1,0:T(8,128)S(1)} collective-permute-done((f32[32,256]{1,0:T(8,128)}, f32[32,256]{1,0:T(8,128)S(1)}, u32[]{:S(2)}, u32[]{:S(2)}) %collective-permute-start.9) | collective-permute-done | bytes 32800 | tf_op jit(solution)/shard_map/ppermute | solution.py:20
  101.2 6.4 %collective-permute-start.12 = (f32[128,128]{0,1:T(8,128)S(1)}, f32[128,128]{0,1:T(8,128)S(1)}, u32[]{:S(2)}, u32[]{:S(2)}) collective-permute-start(f32[128,128]{0,1:T(8,128)S(1)} %slice_add_fusion), channel_id=1, source_target_pairs={{0,384},{8,392},{16,400},{24,408},{32,416},{40,424},{48,432},{56,4... | collective-permute-start | bytes 196616 | tf_op jit(solution)/shard_map/ppermute | solution.py:20
  107.8 1.0 maximum_add_fusion.4
  108.8 2.9 %collective-permute-start.11 = (f32[32,256]{1,0:T(8,128)}, f32[32,256]{1,0:T(8,128)S(1)}, u32[]{:S(2)}, u32[]{:S(2)}) collective-permute-start(f32[32,256]{1,0:T(8,128)} %maximum_add_fusion.4), channel_id=1, source_target_pairs={{0,384},{8,392},{16,400},{24,408},{32,416},{40,424},{48,432},{56,4... | collective-permute-start | bytes 98312 | tf_op jit(solution)/shard_map/ppermute | solution.py:20
  111.7 1.5 %fusion.78 = f32[32,128]{1,0:T(8,128)} fusion(f32[256,128]{0,1:T(8,128)S(1)} %collective-permute-done.10, f32[32,256]{1,0:T(8,128)} %maximum_add_fusion.3), kind=kOutput, calls=%fused_computation.112 | convolution fusion | flops 6291456 | bytes 98304 | tf_op jit(solution)/shard_map/dot_general | solution.py:14
  113.3 4.2 %collective-permute-done.11 = f32[32,256]{1,0:T(8,128)S(1)} collective-permute-done((f32[32,256]{1,0:T(8,128)}, f32[32,256]{1,0:T(8,128)S(1)}, u32[]{:S(2)}, u32[]{:S(2)}) %collective-permute-start.11) | collective-permute-done | bytes 32800 | tf_op jit(solution)/shard_map/ppermute | solution.py:20
  118.2 1.0 broadcast_select_fusion.23
  124.4 15.6 %all_to_all.10 = f32[8,32,256]{2,1,0:T(8,128)S(1)} all-to-all(f32[8,32,256]{2,1,0:T(8,128)S(1)} %constant_dynamic-update-slice_fusion), channel_id=1, replica_groups=mesh['pair'=64,'core'=2,'rep'=4] {'core','rep'}, dimensions={0} | all-to-all | bytes 524288 | tf_op jit(solution)/shard_map/all_to_all | solution.py:193
  140.1 1.5 %shard_map.96 = (f32[256,256]{1,0:T(8,128)}, f32[384,256]{1,0:T(8,128)}) custom-call(f32[256,256]{1,0:T(8,128)S(1)} %bitcast.74, bf16[256,384]{1,0:T(8,128)(2,1)S(1)} %get-tuple-element.7.forward_ref, bf16[384,384]{1,0:T(8,128)(2,1)S(1)} %bitcast.73, s32[1,1]{1,0:T(1,128)S(6)} %copy.49.tiles_ref, bf16[768,384]{1,0:T(8,128)(2,1)S(1)} %bitcast.69, ...), custom_call_target="tpu_custom_call" | custom-call | tf_op jit(solution)/shard_map/pallas_call | solution.py:96
  (208 shorter events, 29.9 us)
Async XLA Ops:
  2.6 9.9 %copy-start.4 = (f32[1,256,256]{2,1,0:T(8,128)S(1)}, f32[1,256,256]{2,1,0:T(8,128)}, u32[]{:S(2)}) copy-start(f32[1,256,256]{2,1,0:T(8,128)} %param.15) | copy-start | bytes 786436
  2.6 9.9 %copy-start.5 = (bf16[1,1,384,256]{3,2,1,0:T(8,128)(2,1)S(1)}, bf16[1,1,384,256]{3,2,1,0:T(8,128)(2,1)}, u32[]{:S(2)}) copy-start(bf16[1,1,384,256]{3,2,1,0:T(8,128)(2,1)} %param.9) | copy-start | bytes 589828
  2.6 9.8 %copy-start.1 = (bf16[1,1,768,384]{3,2,1,0:T(8,128)(2,1)S(1)}, bf16[1,1,768,384]{3,2,1,0:T(8,128)(2,1)}, u32[]{:S(2)}) copy-start(bf16[1,1,768,384]{3,2,1,0:T(8,128)(2,1)} %param.11) | copy-start | bytes 1769476
  2.6 9.8 %copy-start.3 = (bf16[1,1,384,384]{3,2,1,0:T(8,128)(2,1)S(1)}, bf16[1,1,384,384]{3,2,1,0:T(8,128)(2,1)}, u32[]{:S(2)}) copy-start(bf16[1,1,384,384]{3,2,1,0:T(8,128)(2,1)} %param.8) | copy-start | bytes 884740
  2.8 22.0 %collective-permute-start = (f32[896,128]{0,1:T(8,128)S(1)}, f32[896,128]{0,1:T(8,128)S(1)}, u32[]{:S(2)}, u32[]{:S(2)}) collective-permute-start(f32[896,128]{0,1:T(8,128)S(1)} %copy.10), channel_id=1, source_target_pairs={{0,4},{4,0},{1,5},{5,1},{2,6},{6,2},{3,7},{7,3},{8,12},{12,8},{9,1... | collective-permute-start | bytes 1376264 | tf_op jit(solution)/shard_map/ppermute | solution.py:125
  14.9 9.9 %all-to-all-start = ((f32[8,32,256]{2,1,0:T(8,128)}), f32[8,32,256]{2,1,0:T(8,128)S(1)}, u32[]{:S(2)}, u32[]{:S(2)}) async-start(f32[8,32,256]{2,1,0:T(8,128)} %bitcast.6), calls=%async_computation | async-start | bytes 524288 | tf_op jit(solution)/shard_map/all_to_all | solution.py:142
  30.0 5.3 %collective-permute-start.1 = (f32[32,256]{1,0:T(8,128)S(1)}, f32[32,256]{1,0:T(8,128)S(1)}, u32[]{:S(2)}, u32[]{:S(2)}) collective-permute-start(f32[32,256]{1,0:T(8,128)S(1)} %convolution_add_fusion.2), channel_id=1, source_target_pairs={{0,8},{8,0},{16,24},{24,16},{32,40},{40,32},{48,56},{56,48},{64,72... | collective-permute-start | bytes 98312 | tf_op jit(solution)/shard_map/ppermute | solution.py:20
  31.9 6.5 %collective-permute-start.2 = (f32[256,128]{0,1:T(8,128)S(1)}, f32[256,128]{0,1:T(8,128)S(1)}, u32[]{:S(2)}, u32[]{:S(2)}) collective-permute-start(f32[256,128]{0,1:T(8,128)S(1)} %pad_maximum_fusion.1), channel_id=1, source_target_pairs={{0,8},{8,0},{16,24},{24,16},{32,40},{40,32},{48,56},{56,48},{64,72... | collective-permute-start | bytes 393224 | tf_op jit(solution)/shard_map/ppermute | solution.py:20
  39.0 10.1 %collective-permute-start.4 = (f32[256,128]{0,1:T(8,128)S(1)}, f32[256,128]{0,1:T(8,128)S(1)}, u32[]{:S(2)}, u32[]{:S(2)}) collective-permute-start(f32[256,128]{0,1:T(8,128)S(1)} %pad_maximum_fusion.2), channel_id=1, source_target_pairs={{0,24},{8,16},{16,8},{24,0},{32,56},{40,48},{48,40},{56,32},{64,88... | collective-permute-start | bytes 393224 | tf_op jit(solution)/shard_map/ppermute | solution.py:20
  41.4 6.5 %collective-permute-start.3 = (f32[32,256]{1,0:T(8,128)S(1)}, f32[32,256]{1,0:T(8,128)S(1)}, u32[]{:S(2)}, u32[]{:S(2)}) collective-permute-start(f32[32,256]{1,0:T(8,128)S(1)} %maximum_add_fusion), channel_id=1, source_target_pairs={{0,24},{8,16},{16,8},{24,0},{32,56},{40,48},{48,40},{56,32},{64,88... | collective-permute-start | bytes 98312 | tf_op jit(solution)/shard_map/ppermute | solution.py:20
  49.8 9.6 %collective-permute-start.6 = (f32[256,128]{0,1:T(8,128)S(1)}, f32[256,128]{0,1:T(8,128)S(1)}, u32[]{:S(2)}, u32[]{:S(2)}) collective-permute-start(f32[256,128]{0,1:T(8,128)S(1)} %pad_maximum_fusion.3), channel_id=1, source_target_pairs={{0,32},{8,40},{16,48},{24,56},{32,0},{40,8},{48,16},{56,24},{64,96... | collective-permute-start | bytes 393224 | tf_op jit(solution)/shard_map/ppermute | solution.py:20
  52.2 5.3 %copy-start.23 = (f32[32,256]{1,0:T(8,128)}, f32[32,256]{1,0:T(8,128)S(1)}, u32[]{:S(2)}) copy-start(f32[32,256]{1,0:T(8,128)S(1)} %maximum_add_fusion.1) | copy-start | bytes 98308
  52.2 5.3 %collective-permute-start.5 = (f32[32,256]{1,0:T(8,128)S(1)}, f32[32,256]{1,0:T(8,128)S(1)}, u32[]{:S(2)}, u32[]{:S(2)}) collective-permute-start(f32[32,256]{1,0:T(8,128)S(1)} %maximum_add_fusion.1), channel_id=1, source_target_pairs={{0,32},{8,40},{16,48},{24,56},{32,0},{40,8},{48,16},{56,24},{64,96... | collective-permute-start | bytes 98312 | tf_op jit(solution)/shard_map/ppermute | solution.py:20
  60.6 5.3 %copy-start.27 = (f32[128,128]{0,1:T(8,128)S(1)}, f32[128,128]{0,1:T(8,128)}, u32[]{:S(2)}) copy-start(f32[128,128]{0,1:T(8,128)} %get-tuple-element.37) | copy-start | bytes 196612
  60.6 5.3 %copy-start.37 = (f32[32,128]{1,0:T(8,128)S(1)}, f32[32,128]{1,0:T(8,128)}, u32[]{:S(2)}) copy-start(f32[32,128]{1,0:T(8,128)} %get-tuple-element.74) | copy-start | bytes 49156
  60.6 5.3 %copy-start.38 = (f32[32,128]{1,0:T(8,128)S(1)}, f32[32,128]{1,0:T(8,128)}, u32[]{:S(2)}) copy-start(f32[32,128]{1,0:T(8,128)} %get-tuple-element.75) | copy-start | bytes 49156
  60.6 14.8 %collective-permute-start.8 = (f32[256,128]{0,1:T(8,128)S(1)}, f32[256,128]{0,1:T(8,128)S(1)}, u32[]{:S(2)}, u32[]{:S(2)}) collective-permute-start(f32[256,128]{0,1:T(8,128)S(1)} %pad_maximum_fusion.4), channel_id=1, source_target_pairs={{0,64},{8,72},{16,80},{24,88},{32,96},{40,104},{48,112},{56,120},{... | collective-permute-start | bytes 393224 | tf_op jit(solution)/shard_map/ppermute | solution.py:20
  67.1 6.4 %copy-start.25 = (f32[32,256]{1,0:T(8,128)}, f32[32,256]{1,0:T(8,128)S(1)}, u32[]{:S(2)}) copy-start(f32[32,256]{1,0:T(8,128)S(1)} %maximum_add_fusion.2) | copy-start | bytes 98308
  67.1 2.7 %copy-start.24 = (f32[32,256]{1,0:T(8,128)S(1)}, f32[32,256]{1,0:T(8,128)}, u32[]{:S(2)}) copy-start(f32[32,256]{1,0:T(8,128)} %copy-done.23) | copy-start | bytes 98308
  67.1 6.4 %collective-permute-start.7 = (f32[32,256]{1,0:T(8,128)S(1)}, f32[32,256]{1,0:T(8,128)S(1)}, u32[]{:S(2)}, u32[]{:S(2)}) collective-permute-start(f32[32,256]{1,0:T(8,128)S(1)} %maximum_add_fusion.2), channel_id=1, source_target_pairs={{0,64},{8,72},{16,80},{24,88},{32,96},{40,104},{48,112},{56,120},{... | collective-permute-start | bytes 98312 | tf_op jit(solution)/shard_map/ppermute | solution.py:20
  77.2 9.7 %copy-start.28 = (f32[128,128]{0,1:T(8,128)S(1)}, f32[128,128]{0,1:T(8,128)}, u32[]{:S(2)}) copy-start(f32[128,128]{0,1:T(8,128)} %get-tuple-element.42) | copy-start | bytes 196612
  77.2 9.7 %copy-start.29 = (f32[128,128]{0,1:T(8,128)S(1)}, f32[128,128]{0,1:T(8,128)}, u32[]{:S(2)}) copy-start(f32[128,128]{0,1:T(8,128)} %slice.509) | copy-start | bytes 196612
  77.2 23.4 %collective-permute-start.10 = (f32[256,128]{0,1:T(8,128)S(1)}, f32[256,128]{0,1:T(8,128)S(1)}, u32[]{:S(2)}, u32[]{:S(2)}) collective-permute-start(f32[256,128]{0,1:T(8,128)S(1)} %pad_maximum_fusion.5), channel_id=1, source_target_pairs={{0,128},{8,136},{16,144},{24,152},{32,160},{40,168},{48,176},{56,1... | collective-permute-start | bytes 393224 | tf_op jit(solution)/shard_map/ppermute | solution.py:20
  88.8 2.1 %copy-start.26 = (f32[32,256]{1,0:T(8,128)S(1)}, f32[32,256]{1,0:T(8,128)}, u32[]{:S(2)}) copy-start(f32[32,256]{1,0:T(8,128)} %copy-done.25) | copy-start | bytes 98308
  88.8 9.9 %collective-permute-start.9 = (f32[32,256]{1,0:T(8,128)}, f32[32,256]{1,0:T(8,128)S(1)}, u32[]{:S(2)}, u32[]{:S(2)}) collective-permute-start(f32[32,256]{1,0:T(8,128)} %maximum_add_fusion.3), channel_id=1, source_target_pairs={{0,128},{8,136},{16,144},{24,152},{32,160},{40,168},{48,176},{56,1... | collective-permute-start | bytes 98312 | tf_op jit(solution)/shard_map/ppermute | solution.py:20
  101.2 6.6 %copy-start.41 = (f32[32,128]{1,0:T(8,128)S(1)}, f32[32,128]{1,0:T(8,128)}, u32[]{:S(2)}) copy-start(f32[32,128]{1,0:T(8,128)} %get-tuple-element.66) | copy-start | bytes 49156
  101.2 6.6 %copy-start.42 = (f32[32,128]{1,0:T(8,128)S(1)}, f32[32,128]{1,0:T(8,128)}, u32[]{:S(2)}) copy-start(f32[32,128]{1,0:T(8,128)} %get-tuple-element.67) | copy-start | bytes 49156
  101.2 6.6 %copy-start.43 = (f32[32,128]{1,0:T(8,128)S(1)}, f32[32,128]{1,0:T(8,128)}, u32[]{:S(2)}) copy-start(f32[32,128]{1,0:T(8,128)} %get-tuple-element.68) | copy-start | bytes 49156
  101.2 6.6 %copy-start.44 = (f32[32,128]{1,0:T(8,128)S(1)}, f32[32,128]{1,0:T(8,128)}, u32[]{:S(2)}) copy-start(f32[32,128]{1,0:T(8,128)} %get-tuple-element.69) | copy-start | bytes 49156
  101.2 16.9 %collective-permute-start.12 = (f32[128,128]{0,1:T(8,128)S(1)}, f32[128,128]{0,1:T(8,128)S(1)}, u32[]{:S(2)}, u32[]{:S(2)}) collective-permute-start(f32[128,128]{0,1:T(8,128)S(1)} %slice_add_fusion), channel_id=1, source_target_pairs={{0,384},{8,392},{16,400},{24,408},{32,416},{40,424},{48,432},{56,4... | collective-permute-start | bytes 196616 | tf_op jit(solution)/shard_map/ppermute | solution.py:20
  108.8 8.8 %collective-permute-start.11 = (f32[32,256]{1,0:T(8,128)}, f32[32,256]{1,0:T(8,128)S(1)}, u32[]{:S(2)}, u32[]{:S(2)}) collective-permute-start(f32[32,256]{1,0:T(8,128)} %maximum_add_fusion.4), channel_id=1, source_target_pairs={{0,384},{8,392},{16,400},{24,408},{32,416},{40,424},{48,432},{56,4... | collective-permute-start | bytes 98312 | tf_op jit(solution)/shard_map/ppermute | solution.py:20
  113.3 5.8 %copy-start.22 = (f32[32,256]{1,0:T(8,128)S(1)}, f32[32,256]{1,0:T(8,128)}, u32[]{:S(2)}) copy-start(f32[32,256]{1,0:T(8,128)} %copy-done.21) | copy-start | bytes 98308
  (29 other events, 27.3 us)

commit v4 on v3

v4 whole, which is shorter than its diff:
```python
import functools

import jax
import jax.numpy as jnp
from jax import lax
from jax.experimental import pallas as pl
from jax.experimental.pallas import tpu as pltpu
from jax.sharding import Mesh, PartitionSpec as P

TILE = 128
HIGHEST = lax.Precision.HIGHEST
SWAP = (1, 3, 4, 8, 16, 48)


def dot(a, b, dims=((1,), (0,)), precision=HIGHEST):
    return lax.dot_general(
        a, b, (dims, ((), ())), precision=precision, preferred_element_type=jnp.float32
    )


def swap(value, j, count):
    return lax.ppermute(value, "pair", [(n, n ^ SWAP[j]) for n in range(count)])


def pick(bits_ref, at):
    return bits_ref[at : at + 1, :1] == 1


def level_kernel(inverse_ref, couple_ref, level_ref):
    height = inverse_ref.shape[0]
    gain = -dot(inverse_ref[...], couple_ref[...])
    level_ref[:height] = gain
    level_ref[height : height + TILE] = -dot(gain.T, gain)
    level_ref[height + TILE : 2 * height + TILE] = inverse_ref[:, :TILE]
    level_ref[2 * height + TILE :] = inverse_ref[:, TILE:]


def join_maps(right, first, second, maps_ref, weights_ref, step_ref):
    early = first[:TILE]
    product = dot(second, early)
    turn = product[TILE:]
    maps_ref[:TILE] = product[:TILE]
    flipped = early.T
    maps_ref[TILE:] = first[TILE:] + dot(flipped, turn)
    weights_ref[:TILE, :TILE] = second[:TILE].T
    weights_ref[:TILE, TILE:] = turn
    weights_ref[TILE:, :TILE] = jnp.zeros_like(turn)
    weights_ref[TILE:, TILE:] = early
    if step_ref is not None:
        step_ref[:TILE] = jnp.where(right, flipped, turn.T)
        step_ref[TILE:] = jnp.where(right, 0.0, second[:TILE])


def pair_kernel(bits_ref, level_ref, sibling_ref, maps_ref, weights_ref):
    odd = pick(bits_ref, 0)
    own, other = level_ref[TILE : 3 * TILE], sibling_ref[TILE : 3 * TILE]
    join_maps(
        None, jnp.where(odd, other, own), jnp.where(odd, own, other), maps_ref, weights_ref, None
    )


def maps_kernel(j, bits_ref, own_ref, other_ref, maps_ref, weights_ref, step_ref):
    right = pick(bits_ref, j)
    own, other = own_ref[...], other_ref[...]
    join_maps(
        right, jnp.where(right, other, own), jnp.where(right, own, other),
        maps_ref, weights_ref, step_ref,
    )


def join_state(first, second, weights):
    mixed = jnp.concatenate([first[:, :TILE], second[:, TILE:]], axis=1)
    kept = jnp.concatenate([second[:, :TILE], first[:, TILE:]], axis=1)
    return kept + dot(mixed, weights)


def start_kernel(
    bits_ref, parts_ref, level_ref, sibling_ref, weights_ref, later_ref,
    owns_ref, states_ref, state_ref,
):
    odd = pick(bits_ref, 0)
    reps, height = parts_ref.shape[0] // 2, parts_ref.shape[2]
    own_gain, other_gain = level_ref[:height], sibling_ref[:height]
    gains = (jnp.where(odd, other_gain, own_gain), jnp.where(odd, own_gain, other_gain))
    states = []
    for c in range(2):
        own = parts_ref[c * reps]
        for r in range(1, reps):
            own = own + parts_ref[c * reps + r]
        owns_ref[c] = own
        states.append(jnp.concatenate([own[:, TILE:], -dot(own, gains[c])], axis=1))
        states_ref[c] = states[c]
    state_ref[...] = join_state(states[0], states[1], weights_ref[...])


def state_kernel(j, bits_ref, own_ref, other_ref, weights_ref, *refs):
    right = pick(bits_ref, j)
    own, other = own_ref[...], other_ref[...]
    refs[-1][...] = join_state(
        jnp.where(right, other, own), jnp.where(right, own, other), weights_ref[...]
    )


def descend_kernel(rounds, bits_ref, level_ref, sibling_ref, weights_ref, owns_ref, states_ref, *refs):
    sent, got = refs[:rounds], refs[rounds : 2 * rounds]
    answers, steps = refs[2 * rounds : 3 * rounds], refs[3 * rounds : -1]
    shares_ref = refs[-1]
    odd = pick(bits_ref, 0)
    height = owns_ref.shape[2]
    pushes = []
    for j in range(rounds):
        answer = answers[j][answers[j].shape[0] - TILE :]
        other = got[j][...]
        pushes.append(
            jnp.where(
                pick(bits_ref, j + 1),
                other[:, :TILE],
                other[:, TILE:] + dot(sent[j][:, :TILE], answer),
            )
        )
    before = jnp.zeros_like(pushes[0])
    after = before
    for j in reversed(range(rounds)):
        right, push = pick(bits_ref, j + 1), pushes[j]
        if j < rounds - 1:
            push = push + dot(jnp.concatenate([before, after], axis=1), steps[j][...])
        before, after = jnp.where(right, push, before), jnp.where(right, after, push)
    own, other = level_ref[...], sibling_ref[...]
    levels = (jnp.where(odd, other, own), jnp.where(odd, own, other))
    maps = [level[TILE : 3 * TILE] for level in levels]
    entry = states_ref[0, :, :TILE]
    middle_before = entry + dot(before, maps[0][:TILE], ((1,), (1,)))
    middle_after = (
        states_ref[1, :, TILE:]
        + dot(entry, maps[1][TILE:])
        + dot(before, weights_ref[:TILE, TILE:], ((1,), (1,)))
        + dot(after, maps[1][:TILE])
    )
    reps = shares_ref.shape[0] // 2
    ends = ((before, middle_after), (middle_before, after))
    for c in range(2):
        level = levels[c]
        forward = owns_ref[c] + dot(ends[c][0], level[:height], ((1,), (1,)))
        forward = jnp.concatenate(
            [forward[:, :TILE], forward[:, TILE:] - ends[c][1]], axis=1
        )
        left = dot(forward, level[height + TILE : 2 * height + TILE])
        share = jnp.concatenate([left, dot(forward, level[2 * height + TILE :])], axis=1)
        for r in range(reps):
            shares_ref[c * reps + r] = share


def live_columns(tiles_ref, rows, columns):
    return lax.broadcasted_iota(jnp.int32, (rows, columns), 1) < TILE * tiles_ref[...]


def subtree_forward_kernel(
    subtree_inverse_ref, rhs_ref, tiles_ref, update_ref, rows_ref, level_rhs_ref,
    forward_ref, rest_ref,
):
    columns, sub_rows = forward_ref.shape
    live = live_columns(tiles_ref, columns, sub_rows)
    masked = jnp.where(live, rhs_ref[...].astype(jnp.float32).T, 0.0).astype(jnp.bfloat16)
    solved = dot(masked, subtree_inverse_ref[...], ((1,), (1,)), None)
    forward = jnp.where(live, solved, 0.0).astype(jnp.bfloat16)
    forward_ref[...] = forward
    contrib = dot(forward, update_ref[...], ((1,), (1,)), None)
    totals = []
    for s in range(level_rhs_ref.shape[0] // TILE):
        total = jnp.zeros((columns, TILE), jnp.float32)
        for t in range(rows_ref.shape[1]):
            here = rows_ref[:, t : t + 1] == s
            total = total + jnp.where(here, contrib[:, t * TILE : (t + 1) * TILE], 0.0)
        totals.append(total)
    rest_ref[...] = 0.25 * level_rhs_ref[...].T - jnp.concatenate(totals, axis=1)


def part_kernel(rest_ref, inverse_ref, later_ref, part_ref):
    part_ref[...] = dot(rest_ref[...], inverse_ref[...], ((1,), (1,)))


def subtree_backward_kernel(
    solution_ref, forward_ref, subtree_inverse_ref, tiles_ref, update_ref, rows_ref,
    level_ref, final_ref,
):
    columns, sub_rows = forward_ref.shape
    live = live_columns(tiles_ref, columns, sub_rows)
    level_ref[...] = solution_ref[...].T
    picked = []
    for t in range(rows_ref.shape[1]):
        tile = solution_ref[:, :TILE]
        for s in range(1, solution_ref.shape[1] // TILE):
            here = rows_ref[:, t : t + 1] == s
            tile = jnp.where(here, solution_ref[:, s * TILE : (s + 1) * TILE], tile)
        picked.append(tile.astype(jnp.bfloat16))
    pulled = dot(jnp.concatenate(picked, axis=1), update_ref[...], precision=None)
    residue = forward_ref[...].astype(jnp.float32) - jnp.where(live, pulled, 0.0)
    final = dot(residue.astype(jnp.bfloat16), subtree_inverse_ref[...], precision=None)
    final_ref[...] = jnp.where(live, final, 0.0).T


def local_call(kernel, out_shape, *operands, later=()):
    vmem = pl.BlockSpec(memory_space=pltpu.VMEM)
    return pl.pallas_call(
        kernel,
        out_shape=out_shape,
        in_specs=[vmem] * len(operands) + [pl.BlockSpec(memory_space=pl.ANY)] * len(later),
        out_specs=[vmem] * len(out_shape),
        compiler_params=pltpu.CompilerParams(vmem_limit_bytes=8 * 2**20),
    )(*operands, *later)


def f32(*shape):
    return jax.ShapeDtypeStruct(shape, jnp.float32)


def shards(
    sub_inverse, sub_rhs, sub_tiles, update, update_rows, level_inverse, coupling, level_rhs
):
    count, place = lax.axis_size("pair"), lax.axis_index("pair")
    group = ("core", "rep")
    members = lax.axis_size(group)
    subtree_inverse, rhs_sub, block, rows = sub_inverse[0, 0], sub_rhs[0, 0], update[0, 0], update_rows[0]
    inverse, couple, rhs_level = level_inverse[0], coupling[0], level_rhs[0]
    sub_rows, width, height = subtree_inverse.shape[0], rhs_level.shape[1], inverse.shape[0]
    rounds = len(SWAP)
    spot = 2 * place + lax.axis_index("core")
    bits = (spot >> lax.broadcasted_iota(jnp.int32, (8, 128), 0)) & 1
    (level,) = local_call(level_kernel, [f32(2 * height + height + TILE, TILE)], inverse, couple)
    sibling = lax.ppermute(level, "core", [(0, 1), (1, 0)])
    forward_sub, rest = local_call(
        subtree_forward_kernel,
        [jax.ShapeDtypeStruct((width, sub_rows), jnp.bfloat16), f32(width, height)],
        subtree_inverse, rhs_sub, sub_tiles, block, rows, rhs_level,
    )
    maps, pair_weights = local_call(
        pair_kernel, [f32(2 * TILE, TILE), f32(2 * TILE, 2 * TILE)], bits, level, sibling
    )
    (part,) = local_call(part_kernel, [f32(width, height)], rest, inverse, later=(maps,))
    columns = width // members
    parts = lax.all_to_all(part.reshape(members, columns, height), group, 0, 0)
    answers, weights, steps, chain = [], [], [], [maps]
    for j in range(rounds):
        if j == rounds - 1:
            answers.append(swap(maps[TILE:], j, count))
            break
        answers.append(swap(maps, j, count))
        maps, weight, step = local_call(
            functools.partial(maps_kernel, j + 1),
            [f32(2 * TILE, TILE), f32(2 * TILE, 2 * TILE), f32(2 * TILE, TILE)],
            bits, maps, answers[j],
        )
        weights.append(weight)
        steps.append(step)
        chain.append(maps)
    owns, states, state = local_call(
        start_kernel,
        [f32(2, columns, height), f32(2, columns, 2 * TILE), f32(columns, 2 * TILE)],
        bits, parts, level, sibling, pair_weights, later=(chain[1],),
    )
    sent, got = [], []
    for j in range(rounds):
        sent.append(state)
        got.append(swap(state, j, count))
        if j < rounds - 1:
            (state,) = local_call(
                functools.partial(state_kernel, j + 1),
                [f32(columns, 2 * TILE)],
                bits, state, got[j], weights[j], later=(chain[j + 2],) if j < 2 else (),
            )
    (shares,) = local_call(
        functools.partial(descend_kernel, rounds),
        [f32(members, columns, height)],
        bits, level, sibling, pair_weights, owns, states, *sent, *got, *answers, *steps,
    )
    spread = lax.all_to_all(shares, group, 0, 0)
    solution, final = local_call(
        subtree_backward_kernel,
        [f32(height, width), f32(sub_rows, width)],
        spread.reshape(width, -1), forward_sub, subtree_inverse, sub_tiles, block, rows,
    )
    return (solution[None], final[None, None])


def solution(mesh):
    chain, reps = mesh.devices.shape
    split = Mesh(mesh.devices.reshape(chain // 2, 2, reps), ("pair", "core", "rep"))
    both = ("pair", "core")
    return jax.shard_map(
        shards,
        mesh=split,
        in_specs=(
            P(both, "rep", None, None),
            P(both, "rep", None, None),
            P(both, "rep"),
            P(both, "rep", None, None),
            P(both, "rep", None),
            P(both, None, None),
            P(both, None, None),
            P(both, None, None),
        ),
        out_specs=(P(both, None, None), P(both, "rep", None, None)),
        check_vma=False,
    )
```

time: 143 us -> 122 us (0.85)
  matrix products: 17.8 us -> 0 us
  local copies, waits for them, and re-layouts: 21.4 us -> 5.48 us
  Pallas kernels: 3.34 us -> 11.7 us
  waiting for transfers between devices: 23.5 us -> 30.8 us
    dot_general x41 -> x0, matrix products: 17.8 us -> none  [dot(): lax.dot_general(a, b, (dims, ((), ())), precision=precision, preferred_el...]
    ppermute x12, waiting for transfers between devices: 17 us -> 26.5 us  [swap(): return lax.ppermute(value, 'pair', [(n, n ^ SWAP[j]) for n in range(count)])]
    slice x29 -> x1, local copies, waits for them, and re-layouts: 8.73 us -> 0.01 us  [shards(): answers.append(swap(maps[TILE:], j, count))]
    pallas_call x2 -> x17, Pallas kernels: 3.34 us -> 11.7 us  [local_call(): pl.pallas_call(kernel, out_shape=out_shape, in_specs=[vmem] * len(operand...]
    transpose x19 -> x0, local copies, waits for them, and re-layouts: 3.74 us -> none  [the longest x11 1.75 us: join_maps(): upper = jnp.concatenate([second[:TILE].T, product[TILE:]], axis=1)]
    all_to_all x1, waiting for transfers between devices: 6.52 us -> 2.94 us  [shards(): parts = lax.all_to_all(part.reshape(members, columns, height), group, 0, 0)]
    ppermute x12, starting transfers between devices: 44 us -> 41.3 us  [swap(): return lax.ppermute(value, 'pair', [(n, n ^ SWAP[j]) for n in range(count)])]
    unnamed x97 -> x40, local copies, waits for them, and re-layouts: 7.75 us -> 5.41 us
  transfers between devices with their start and end apart: 14 -> 14, of which waited for: 7 -> 9; matrix products, arithmetic and copies ran while one was open for 14% -> 0% of each run, Pallas kernels for 1% -> 4%
where the time goes in v4:
time: 122 us; the launch traced here: 121 us
  starting transfers between devices  55.8 us (46%)
  waiting for transfers between devices  30.8 us (25%)
  blocking collectives  16 us (13%)
  Pallas kernels  11.7 us (10%)
  local copies, waits for them, and re-layouts  5.48 us (4%)
  between operations  1.71 us (1%)
    ppermute x12, starting transfers between devices, swap(): return lax.ppermute(value, 'pair', [(n, n ^ SWAP[j]) for n in range(count)])  41.3 us
    ppermute x12, waiting for transfers between devices, swap(): return lax.ppermute(value, 'pair', [(n, n ^ SWAP[j]) for n in range(count)])  26.5 us
    all_to_all x1, blocking collectives, shards(): spread = lax.all_to_all(shares, group, 0, 0)  16 us
    pallas_call x17, Pallas kernels, local_call(): pl.pallas_call(kernel, out_shape=out_shape, in_specs=[vmem] * len(operand...  11.7 us
    ppermute x1, starting transfers between devices, shards(): sibling = lax.ppermute(level, 'core', [(0, 1), (1, 0)])  8.79 us
    all_to_all x1, starting transfers between devices, shards(): parts = lax.all_to_all(part.reshape(members, columns, height), group, 0, 0)  5.69 us
    unnamed x40, local copies, waits for them, and re-layouts  5.41 us
    all_to_all x1, waiting for transfers between devices, shards(): parts = lax.all_to_all(part.reshape(members, columns, height), group, 0, 0)  2.94 us
  transfers between devices with their start and end apart: 14, of which 9 were waited for; matrix products, arithmetic and copies ran while one was open for 0% of the time, Pallas kernels for 4%

profile of v4, /device:TPU:1, one launch (start us, length us, event | category | flops | bytes accessed | tf_op | source)
XLA Modules:
  0.0 121.5 jit_solution(535507077416215257)
XLA Ops:
  0.6 0.9 copy-done.2
  1.6 0.9 copy-done.18
  2.5 0.8 shard_map.95.level_ref
  3.3 8.8 %collective-permute-start = (f32[896,128]{1,0:T(8,128)S(1)}, f32[896,128]{1,0:T(8,128)S(1)}, u32[]{:S(2)}, u32[]{:S(2)}) collective-permute-start(f32[896,128]{1,0:T(8,128)S(1)} %shard_map.95.level_ref), channel_id=1, source_target_pairs={{0,4},{4,0},{1,5},{5,1},{2,6},{6,2},{3,7},{7,3},{8,12},{12,8},{9,1... | collective-permute-start | bytes 1376264 | tf_op jit(solution)/shard_map/ppermute | solution.py:230
  12.1 1.4 %collective-permute-done.sibling_ref = f32[896,128]{1,0:T(8,128)S(1)} collective-permute-done((f32[896,128]{1,0:T(8,128)S(1)}, f32[896,128]{1,0:T(8,128)S(1)}, u32[]{:S(2)}, u32[]{:S(2)}) %collective-permute-start) | collective-permute-done | bytes 458784 | tf_op jit(solution)/shard_map/ppermute | solution.py:230
  14.2 2.1 %collective-permute-start.1 = (f32[256,128]{1,0:T(8,128)S(1)}, f32[256,128]{1,0:T(8,128)S(1)}, u32[]{:S(2)}, u32[]{:S(2)}) collective-permute-start(f32[256,128]{1,0:T(8,128)S(1)} %get-tuple-element.28.later_ref.own_ref), channel_id=1, source_target_pairs={{0,8},{8,0},{16,24},{24,16},{32,40},{40,32},{48,56},{56,48},{64,72... | collective-permute-start | bytes 393224 | tf_op jit(solution)/shard_map/ppermute | solution.py:22
  16.2 4.7 %collective-permute-done.1.other_ref.refs_12_ = f32[256,128]{1,0:T(8,128)S(1)} collective-permute-done((f32[256,128]{1,0:T(8,128)S(1)}, f32[256,128]{1,0:T(8,128)S(1)}, u32[]{:S(2)}, u32[]{:S(2)}) %collective-permute-start.1) | collective-permute-done | bytes 131104 | tf_op jit(solution)/shard_map/ppermute | solution.py:22
  22.1 2.0 %collective-permute-start.3 = (f32[256,128]{1,0:T(8,128)S(1)}, f32[256,128]{1,0:T(8,128)S(1)}, u32[]{:S(2)}, u32[]{:S(2)}) collective-permute-start(f32[256,128]{1,0:T(8,128)S(1)} %get-tuple-element.29.later_ref.own_ref), channel_id=1, source_target_pairs={{0,24},{8,16},{16,8},{24,0},{32,56},{40,48},{48,40},{56,32},{64,88... | collective-permute-start | bytes 393224 | tf_op jit(solution)/shard_map/ppermute | solution.py:22
  24.2 5.0 %collective-permute-done.3.other_ref.refs_13_ = f32[256,128]{1,0:T(8,128)S(1)} collective-permute-done((f32[256,128]{1,0:T(8,128)S(1)}, f32[256,128]{1,0:T(8,128)S(1)}, u32[]{:S(2)}, u32[]{:S(2)}) %collective-permute-start.3) | collective-permute-done | bytes 131104 | tf_op jit(solution)/shard_map/ppermute | solution.py:22
  29.8 0.7 copy-done.6
  31.1 1.9 %collective-permute-start.5 = (f32[256,128]{1,0:T(8,128)S(1)}, f32[256,128]{1,0:T(8,128)S(1)}, u32[]{:S(2)}, u32[]{:S(2)}) collective-permute-start(f32[256,128]{1,0:T(8,128)S(1)} %get-tuple-element.34.refs_0_.own_ref), channel_id=1, source_target_pairs={{0,32},{8,40},{16,48},{24,56},{32,0},{40,8},{48,16},{56,24},{64,96... | collective-permute-start | bytes 393224 | tf_op jit(solution)/shard_map/ppermute | solution.py:22
  34.3 0.7 shard_map.97
  35.3 1.1 shard_map.98
  36.4 5.7 %all-to-all-start = ((f32[8,32,256]{2,1,0:T(8,128)}), f32[8,32,256]{2,1,0:T(8,128)S(1)}, u32[]{:S(2)}, u32[]{:S(2)}) async-start(f32[8,32,256]{2,1,0:T(8,128)} %bitcast.7), calls=%async_computation | async-start | bytes 524288 | tf_op jit(solution)/shard_map/all_to_all | solution.py:241
  43.3 2.4 %collective-permute-start.8 = (f32[256,128]{1,0:T(8,128)S(1)}, f32[256,128]{1,0:T(8,128)S(1)}, u32[]{:S(2)}, u32[]{:S(2)}) collective-permute-start(f32[256,128]{1,0:T(8,128)S(1)} %get-tuple-element.36.refs_0_.own_ref), channel_id=1, source_target_pairs={{0,64},{8,72},{16,80},{24,88},{32,96},{40,104},{48,112},{56,120},{... | collective-permute-start | bytes 393224 | tf_op jit(solution)/shard_map/ppermute | solution.py:22
  45.7 2.9 %all-to-all-done.parts_ref = f32[8,32,256]{2,1,0:T(8,128)S(1)} async-done(((f32[8,32,256]{2,1,0:T(8,128)}), f32[8,32,256]{2,1,0:T(8,128)S(1)}, u32[]{:S(2)}, u32[]{:S(2)}) %all-to-all-start) | async-done | bytes 262176 | tf_op jit(solution)/shard_map/all_to_all | solution.py:241
  49.2 2.1 %collective-permute-start.2 = (f32[32,256]{1,0:T(8,128)S(1)}, f32[32,256]{1,0:T(8,128)S(1)}, u32[]{:S(2)}, u32[]{:S(2)}) collective-permute-start(f32[32,256]{1,0:T(8,128)S(1)} %get-tuple-element.32.own_ref.refs_0_), channel_id=1, source_target_pairs={{0,8},{8,0},{16,24},{24,16},{32,40},{40,32},{48,56},{56,48},{64,72... | collective-permute-start | bytes 98312 | tf_op jit(solution)/shard_map/ppermute | solution.py:22
  51.2 2.7 %collective-permute-done.8.other_ref.refs_15_ = f32[256,128]{1,0:T(8,128)S(1)} collective-permute-done((f32[256,128]{1,0:T(8,128)S(1)}, f32[256,128]{1,0:T(8,128)S(1)}, u32[]{:S(2)}, u32[]{:S(2)}) %collective-permute-start.8) | collective-permute-done | bytes 131104 | tf_op jit(solution)/shard_map/ppermute | solution.py:22
  54.6 7.1 %collective-permute-start.10 = (f32[256,128]{1,0:T(8,128)S(1)}, f32[256,128]{1,0:T(8,128)S(1)}, u32[]{:S(2)}, u32[]{:S(2)}) collective-permute-start(f32[256,128]{1,0:T(8,128)S(1)} %get-tuple-element.39.own_ref), channel_id=1, source_target_pairs={{0,128},{8,136},{16,144},{24,152},{32,160},{40,168},{48,176},{56,1... | collective-permute-start | bytes 393224 | tf_op jit(solution)/shard_map/ppermute | solution.py:22
  61.9 4.6 %collective-permute-start.4 = (f32[32,256]{1,0:T(8,128)S(1)}, f32[32,256]{1,0:T(8,128)S(1)}, u32[]{:S(2)}, u32[]{:S(2)}) collective-permute-start(f32[32,256]{1,0:T(8,128)S(1)} %shard_map.102.own_ref.refs_1_), channel_id=1, source_target_pairs={{0,24},{8,16},{16,8},{24,0},{32,56},{40,48},{48,40},{56,32},{64,88... | collective-permute-start | bytes 98312 | tf_op jit(solution)/shard_map/ppermute | solution.py:22
  66.6 1.3 %collective-permute-done.4.other_ref.refs_7_ = f32[32,256]{1,0:T(8,128)S(1)} collective-permute-done((f32[32,256]{1,0:T(8,128)S(1)}, f32[32,256]{1,0:T(8,128)S(1)}, u32[]{:S(2)}, u32[]{:S(2)}) %collective-permute-start.4) | collective-permute-done | bytes 32800 | tf_op jit(solution)/shard_map/ppermute | solution.py:22
  68.1 1.9 %collective-permute-start.6 = (f32[32,256]{1,0:T(8,128)S(1)}, f32[32,256]{1,0:T(8,128)S(1)}, u32[]{:S(2)}, u32[]{:S(2)}) collective-permute-start(f32[32,256]{1,0:T(8,128)S(1)} %shard_map.104.own_ref.refs_2_), channel_id=1, source_target_pairs={{0,32},{8,40},{16,48},{24,56},{32,0},{40,8},{48,16},{56,24},{64,96... | collective-permute-start | bytes 98312 | tf_op jit(solution)/shard_map/ppermute | solution.py:22
  70.0 3.2 %collective-permute-done.6.other_ref.refs_8_ = f32[32,256]{1,0:T(8,128)S(1)} collective-permute-done((f32[32,256]{1,0:T(8,128)S(1)}, f32[32,256]{1,0:T(8,128)S(1)}, u32[]{:S(2)}, u32[]{:S(2)}) %collective-permute-start.6) | collective-permute-done | bytes 32800 | tf_op jit(solution)/shard_map/ppermute | solution.py:22
  73.5 2.3 %collective-permute-start.7 = (f32[32,256]{1,0:T(8,128)S(1)}, f32[32,256]{1,0:T(8,128)S(1)}, u32[]{:S(2)}, u32[]{:S(2)}) collective-permute-start(f32[32,256]{1,0:T(8,128)S(1)} %shard_map.105.own_ref.refs_3_), channel_id=1, source_target_pairs={{0,64},{8,72},{16,80},{24,88},{32,96},{40,104},{48,112},{56,120},{... | collective-permute-start | bytes 98312 | tf_op jit(solution)/shard_map/ppermute | solution.py:22
  75.8 3.3 %collective-permute-done.7.other_ref.refs_9_ = f32[32,256]{1,0:T(8,128)S(1)} collective-permute-done((f32[32,256]{1,0:T(8,128)S(1)}, f32[32,256]{1,0:T(8,128)S(1)}, u32[]{:S(2)}, u32[]{:S(2)}) %collective-permute-start.7) | collective-permute-done | bytes 32800 | tf_op jit(solution)/shard_map/ppermute | solution.py:22
  79.3 5.2 %collective-permute-start.9 = (f32[32,256]{1,0:T(8,128)S(1)}, f32[32,256]{1,0:T(8,128)S(1)}, u32[]{:S(2)}, u32[]{:S(2)}) collective-permute-start(f32[32,256]{1,0:T(8,128)S(1)} %shard_map.107.own_ref.refs_4_), channel_id=1, source_target_pairs={{0,128},{8,136},{16,144},{24,152},{32,160},{40,168},{48,176},{56,1... | collective-permute-start | bytes 98312 | tf_op jit(solution)/shard_map/ppermute | solution.py:22
  85.1 7.5 %collective-permute-start.12 = (f32[128,128]{1,0:T(8,128)S(1)}, f32[128,128]{1,0:T(8,128)S(1)}, u32[]{:S(2)}, u32[]{:S(2)}) collective-permute-start(f32[128,128]{1,0:T(8,128)S(1)} %slice.3), channel_id=1, source_target_pairs={{0,384},{8,392},{16,400},{24,408},{32,416},{40,424},{48,432},{56,4... | collective-permute-start | bytes 196616 | tf_op jit(solution)/shard_map/ppermute | solution.py:22
  92.9 2.2 %collective-permute-start.11 = (f32[32,256]{1,0:T(8,128)S(1)}, f32[32,256]{1,0:T(8,128)S(1)}, u32[]{:S(2)}, u32[]{:S(2)}) collective-permute-start(f32[32,256]{1,0:T(8,128)S(1)} %shard_map.109.refs_5_), channel_id=1, source_target_pairs={{0,384},{8,392},{16,400},{24,408},{32,416},{40,424},{48,432},{56,4... | collective-permute-start | bytes 98312 | tf_op jit(solution)/shard_map/ppermute | solution.py:22
  95.2 6.3 %collective-permute-done.11.refs_11_ = f32[32,256]{1,0:T(8,128)S(1)} collective-permute-done((f32[32,256]{1,0:T(8,128)S(1)}, f32[32,256]{1,0:T(8,128)S(1)}, u32[]{:S(2)}, u32[]{:S(2)}) %collective-permute-start.11) | collective-permute-done | bytes 32800 | tf_op jit(solution)/shard_map/ppermute | solution.py:22
  101.5 2.5 %shard_map.110 = f32[8,32,256]{2,1,0:T(8,128)S(1)} custom-call(s32[8,128]{1,0:T(8,128)S(1)} %iota.7.bits_ref, f32[896,128]{1,0:T(8,128)S(1)} %shard_map.95.level_ref, f32[896,128]{1,0:T(8,128)S(1)} %collective-permute-done.sibling_ref, f32[256,256]{1,0:T(8,128)S(1)} %get-tuple-element.26.weights_ref, f32[2,32,256]{2,1,0:T(8,128)S(1)} %get-tuple-element.30.owns_ref, ...), custom_call_target="tpu_custom_call" | custom-call | tf_op jit(solution)/shard_map/pallas_call | solution.py:204
  104.1 16.0 %all_to_all.10 = f32[8,32,256]{2,1,0:T(8,128)S(1)} all-to-all(f32[8,32,256]{2,1,0:T(8,128)S(1)} %shard_map.110), channel_id=1, replica_groups=mesh['pair'=64,'core'=2,'rep'=4] {'core','rep'}, dimensions={0} | all-to-all | bytes 524288 | tf_op jit(solution)/shard_map/all_to_all | solution.py:276
  120.0 1.5 %shard_map.111 = (f32[256,256]{1,0:T(8,128)}, f32[384,256]{1,0:T(8,128)}) custom-call(f32[256,256]{1,0:T(8,128)S(1)} %bitcast.17, bf16[256,384]{1,0:T(8,128)(2,1)S(1)} %copy-done.11, bf16[384,384]{1,0:T(8,128)(2,1)S(1)} %bitcast.14, s32[1,1]{1,0:T(1,128)S(6)} %copy.10.tiles_ref, bf16[768,384]{1,0:T(8,128)(2,1)S(1)} %bitcast.12, s32[1,6]{1,0:T(1,128)S(1)} %bitcast.22), custom_call_target="tpu_custom_call" | custom-call | tf_op jit(solution)/shard_map/pallas_call | solution.py:204
  (57 shorter events, 8.1 us)
Async XLA Ops:
  0.6 1.0 copy-start.2
  1.6 0.9 copy-start.18
  3.3 10.2 %collective-permute-start = (f32[896,128]{1,0:T(8,128)S(1)}, f32[896,128]{1,0:T(8,128)S(1)}, u32[]{:S(2)}, u32[]{:S(2)}) collective-permute-start(f32[896,128]{1,0:T(8,128)S(1)} %shard_map.95.level_ref), channel_id=1, source_target_pairs={{0,4},{4,0},{1,5},{5,1},{2,6},{6,2},{3,7},{7,3},{8,12},{12,8},{9,1... | collective-permute-start | bytes 1376264 | tf_op jit(solution)/shard_map/ppermute | solution.py:230
  13.6 20.1 %copy-start = (bf16[1,1,768,384]{3,2,1,0:T(8,128)(2,1)S(1)}, bf16[1,1,768,384]{3,2,1,0:T(8,128)(2,1)}, u32[]{:S(2)}) copy-start(bf16[1,1,768,384]{3,2,1,0:T(8,128)(2,1)} %param.11) | copy-start | bytes 1769476
  13.6 20.1 %copy-start.8 = (f32[1,256,256]{2,1,0:T(8,128)S(1)}, f32[1,256,256]{2,1,0:T(8,128)}, u32[]{:S(2)}) copy-start(f32[1,256,256]{2,1,0:T(8,128)} %param.15) | copy-start | bytes 786436
  14.2 19.5 %copy-start.1 = (bf16[1,1,384,384]{3,2,1,0:T(8,128)(2,1)S(1)}, bf16[1,1,384,384]{3,2,1,0:T(8,128)(2,1)}, u32[]{:S(2)}) copy-start(bf16[1,1,384,384]{3,2,1,0:T(8,128)(2,1)} %param.8) | copy-start | bytes 884740
  14.2 6.7 %collective-permute-start.1 = (f32[256,128]{1,0:T(8,128)S(1)}, f32[256,128]{1,0:T(8,128)S(1)}, u32[]{:S(2)}, u32[]{:S(2)}) collective-permute-start(f32[256,128]{1,0:T(8,128)S(1)} %get-tuple-element.28.later_ref.own_ref), channel_id=1, source_target_pairs={{0,8},{8,0},{16,24},{24,16},{32,40},{40,32},{48,56},{56,48},{64,72... | collective-permute-start | bytes 393224 | tf_op jit(solution)/shard_map/ppermute | solution.py:22
  22.1 11.5 %copy-start.4 = (f32[256,256]{1,0:T(8,128)}, f32[256,256]{1,0:T(8,128)S(1)}, u32[]{:S(2)}) copy-start(f32[256,256]{1,0:T(8,128)S(1)} %get-tuple-element.33.weights_ref) | copy-start | bytes 786436
  22.1 11.6 %copy-start.9 = (bf16[1,1,384,256]{3,2,1,0:T(8,128)(2,1)S(1)}, bf16[1,1,384,256]{3,2,1,0:T(8,128)(2,1)}, u32[]{:S(2)}) copy-start(bf16[1,1,384,256]{3,2,1,0:T(8,128)(2,1)} %param.9) | copy-start | bytes 589828
  22.1 7.0 %collective-permute-start.3 = (f32[256,128]{1,0:T(8,128)S(1)}, f32[256,128]{1,0:T(8,128)S(1)}, u32[]{:S(2)}, u32[]{:S(2)}) collective-permute-start(f32[256,128]{1,0:T(8,128)S(1)} %get-tuple-element.29.later_ref.own_ref), channel_id=1, source_target_pairs={{0,24},{8,16},{16,8},{24,0},{32,56},{40,48},{48,40},{56,32},{64,88... | collective-permute-start | bytes 393224 | tf_op jit(solution)/shard_map/ppermute | solution.py:22
  29.8 0.7 copy-start.6
  31.1 11.0 %collective-permute-start.5 = (f32[256,128]{1,0:T(8,128)S(1)}, f32[256,128]{1,0:T(8,128)S(1)}, u32[]{:S(2)}, u32[]{:S(2)}) collective-permute-start(f32[256,128]{1,0:T(8,128)S(1)} %get-tuple-element.34.refs_0_.own_ref), channel_id=1, source_target_pairs={{0,32},{8,40},{16,48},{24,56},{32,0},{40,8},{48,16},{56,24},{64,96... | collective-permute-start | bytes 393224 | tf_op jit(solution)/shard_map/ppermute | solution.py:22
  33.7 0.7 copy-start.19
  34.3 0.9 copy-start.3
  35.0 1.4 %copy-start.10 = (bf16[256,384]{1,0:T(8,128)(2,1)}, bf16[256,384]{1,0:T(8,128)(2,1)S(1)}, u32[]{:S(2)}) copy-start(bf16[256,384]{1,0:T(8,128)(2,1)S(1)} %get-tuple-element.47.forward_ref) | copy-start | bytes 589828
  36.4 12.3 %all-to-all-start = ((f32[8,32,256]{2,1,0:T(8,128)}), f32[8,32,256]{2,1,0:T(8,128)S(1)}, u32[]{:S(2)}, u32[]{:S(2)}) async-start(f32[8,32,256]{2,1,0:T(8,128)} %bitcast.7), calls=%async_computation | async-start | bytes 524288 | tf_op jit(solution)/shard_map/all_to_all | solution.py:241
  42.7 0.7 copy-start.16
  43.3 10.6 %collective-permute-start.8 = (f32[256,128]{1,0:T(8,128)S(1)}, f32[256,128]{1,0:T(8,128)S(1)}, u32[]{:S(2)}, u32[]{:S(2)}) collective-permute-start(f32[256,128]{1,0:T(8,128)S(1)} %get-tuple-element.36.refs_0_.own_ref), channel_id=1, source_target_pairs={{0,64},{8,72},{16,80},{24,88},{32,96},{40,104},{48,112},{56,120},{... | collective-permute-start | bytes 393224 | tf_op jit(solution)/shard_map/ppermute | solution.py:22
  49.2 12.5 %copy-start.5 = (f32[256,256]{1,0:T(8,128)S(1)}, f32[256,256]{1,0:T(8,128)}, u32[]{:S(2)}) copy-start(f32[256,256]{1,0:T(8,128)} %copy-done.4) | copy-start | bytes 786436
  49.2 12.5 %collective-permute-start.2 = (f32[32,256]{1,0:T(8,128)S(1)}, f32[32,256]{1,0:T(8,128)S(1)}, u32[]{:S(2)}, u32[]{:S(2)}) collective-permute-start(f32[32,256]{1,0:T(8,128)S(1)} %get-tuple-element.32.own_ref.refs_0_), channel_id=1, source_target_pairs={{0,8},{8,0},{16,24},{24,16},{32,40},{40,32},{48,56},{56,48},{64,72... | collective-permute-start | bytes 98312 | tf_op jit(solution)/shard_map/ppermute | solution.py:22
  54.5 13.3 %copy-start.7 = (f32[256,256]{1,0:T(8,128)S(1)}, f32[256,256]{1,0:T(8,128)}, u32[]{:S(2)}) copy-start(f32[256,256]{1,0:T(8,128)} %copy-done.6) | copy-start | bytes 786436
  54.6 30.0 %collective-permute-start.10 = (f32[256,128]{1,0:T(8,128)S(1)}, f32[256,128]{1,0:T(8,128)S(1)}, u32[]{:S(2)}, u32[]{:S(2)}) collective-permute-start(f32[256,128]{1,0:T(8,128)S(1)} %get-tuple-element.39.own_ref), channel_id=1, source_target_pairs={{0,128},{8,136},{16,144},{24,152},{32,160},{40,168},{48,176},{56,1... | collective-permute-start | bytes 393224 | tf_op jit(solution)/shard_map/ppermute | solution.py:22
  61.9 5.9 %collective-permute-start.4 = (f32[32,256]{1,0:T(8,128)S(1)}, f32[32,256]{1,0:T(8,128)S(1)}, u32[]{:S(2)}, u32[]{:S(2)}) collective-permute-start(f32[32,256]{1,0:T(8,128)S(1)} %shard_map.102.own_ref.refs_1_), channel_id=1, source_target_pairs={{0,24},{8,16},{16,8},{24,0},{32,56},{40,48},{48,40},{56,32},{64,88... | collective-permute-start | bytes 98312 | tf_op jit(solution)/shard_map/ppermute | solution.py:22
  68.1 5.1 %collective-permute-start.6 = (f32[32,256]{1,0:T(8,128)S(1)}, f32[32,256]{1,0:T(8,128)S(1)}, u32[]{:S(2)}, u32[]{:S(2)}) collective-permute-start(f32[32,256]{1,0:T(8,128)S(1)} %shard_map.104.own_ref.refs_2_), channel_id=1, source_target_pairs={{0,32},{8,40},{16,48},{24,56},{32,0},{40,8},{48,16},{56,24},{64,96... | collective-permute-start | bytes 98312 | tf_op jit(solution)/shard_map/ppermute | solution.py:22
  73.5 5.6 %collective-permute-start.7 = (f32[32,256]{1,0:T(8,128)S(1)}, f32[32,256]{1,0:T(8,128)S(1)}, u32[]{:S(2)}, u32[]{:S(2)}) collective-permute-start(f32[32,256]{1,0:T(8,128)S(1)} %shard_map.105.own_ref.refs_3_), channel_id=1, source_target_pairs={{0,64},{8,72},{16,80},{24,88},{32,96},{40,104},{48,112},{56,120},{... | collective-permute-start | bytes 98312 | tf_op jit(solution)/shard_map/ppermute | solution.py:22
  79.3 13.4 %collective-permute-start.9 = (f32[32,256]{1,0:T(8,128)S(1)}, f32[32,256]{1,0:T(8,128)S(1)}, u32[]{:S(2)}, u32[]{:S(2)}) collective-permute-start(f32[32,256]{1,0:T(8,128)S(1)} %shard_map.107.own_ref.refs_4_), channel_id=1, source_target_pairs={{0,128},{8,136},{16,144},{24,152},{32,160},{40,168},{48,176},{56,1... | collective-permute-start | bytes 98312 | tf_op jit(solution)/shard_map/ppermute | solution.py:22
  85.1 16.4 %copy-start.17 = (f32[256,128]{1,0:T(8,128)S(1)}, f32[256,128]{1,0:T(8,128)}, u32[]{:S(2)}) copy-start(f32[256,128]{1,0:T(8,128)} %copy-done.16) | copy-start | bytes 393220
  85.1 16.4 %collective-permute-start.12 = (f32[128,128]{1,0:T(8,128)S(1)}, f32[128,128]{1,0:T(8,128)S(1)}, u32[]{:S(2)}, u32[]{:S(2)}) collective-permute-start(f32[128,128]{1,0:T(8,128)S(1)} %slice.3), channel_id=1, source_target_pairs={{0,384},{8,392},{16,400},{24,408},{32,416},{40,424},{48,432},{56,4... | collective-permute-start | bytes 196616 | tf_op jit(solution)/shard_map/ppermute | solution.py:22
  92.7 8.9 %copy-start.13 = (f32[256,128]{1,0:T(8,128)S(1)}, f32[256,128]{1,0:T(8,128)}, u32[]{:S(2)}) copy-start(f32[256,128]{1,0:T(8,128)} %copy-done.12) | copy-start | bytes 393220
  92.7 8.9 %copy-start.15 = (f32[256,128]{1,0:T(8,128)S(1)}, f32[256,128]{1,0:T(8,128)}, u32[]{:S(2)}) copy-start(f32[256,128]{1,0:T(8,128)} %copy-done.14) | copy-start | bytes 393220
  92.9 8.6 %collective-permute-start.11 = (f32[32,256]{1,0:T(8,128)S(1)}, f32[32,256]{1,0:T(8,128)S(1)}, u32[]{:S(2)}, u32[]{:S(2)}) collective-permute-start(f32[32,256]{1,0:T(8,128)S(1)} %shard_map.109.refs_5_), channel_id=1, source_target_pairs={{0,384},{8,392},{16,400},{24,408},{32,416},{40,424},{48,432},{56,4... | collective-permute-start | bytes 98312 | tf_op jit(solution)/shard_map/ppermute | solution.py:22
  104.0 16.0 %copy-start.11 = (bf16[256,384]{1,0:T(8,128)(2,1)S(1)}, bf16[256,384]{1,0:T(8,128)(2,1)}, u32[]{:S(2)}) copy-start(bf16[256,384]{1,0:T(8,128)(2,1)} %copy-done.10) | copy-start | bytes 589828
  (2 other events, 1.3 us)

commit v5 on v4

--- a/solution.py
+++ b/solution.py
@@ -12,6 +12,10 @@
 SWAP = (1, 3, 4, 8, 16, 48)
 
 
+MAPS_WEIGHT = 40
+STATE_WEIGHT = 3
+
+
 def dot(a, b, dims=((1,), (0,)), precision=HIGHEST):
     return lax.dot_general(
         a, b, (dims, ((), ())), precision=precision, preferred_element_type=jnp.float32
@@ -26,7 +30,19 @@
     return bits_ref[at : at + 1, :1] == 1
 
 
-def level_kernel(inverse_ref, couple_ref, level_ref):
+def fetch(sems, *pairs):
+    copies = [
+        pltpu.make_async_copy(source, target, sems.at[i])
+        for i, (source, target) in enumerate(pairs)
+    ]
+    for copy in copies:
+        copy.start()
+    return copies
+
+
+def level_kernel(inverse_hbm, couple_hbm, level_ref, inverse_ref, couple_ref, sems):
+    for copy in fetch(sems, (inverse_hbm, inverse_ref), (couple_hbm, couple_ref)):
+        copy.wait()
     height = inverse_ref.shape[0]
     gain = -dot(inverse_ref[...], couple_ref[...])
     level_ref[:height] = gain
@@ -51,7 +67,7 @@
         step_ref[TILE:] = jnp.where(right, 0.0, second[:TILE])
 
 
-def pair_kernel(bits_ref, level_ref, sibling_ref, maps_ref, weights_ref):
+def pair_kernel(bits_ref, level_ref, sibling_ref, later_ref, maps_ref, weights_ref):
     odd = pick(bits_ref, 0)
     own, other = level_ref[TILE : 3 * TILE], sibling_ref[TILE : 3 * TILE]
     join_maps(
@@ -59,7 +75,7 @@
     )
 
 
-def maps_kernel(j, bits_ref, own_ref, other_ref, maps_ref, weights_ref, step_ref):
+def maps_kernel(j, bits_ref, own_ref, other_ref, later_ref, maps_ref, weights_ref, step_ref):
     right = pick(bits_ref, j)
     own, other = own_ref[...], other_ref[...]
     join_maps(
@@ -155,16 +171,31 @@
 
 
 def subtree_forward_kernel(
-    subtree_inverse_ref, rhs_ref, tiles_ref, update_ref, rows_ref, level_rhs_ref,
+    tiles_hbm, rhs_hbm, subtree_inverse_hbm, update_hbm, rows_hbm, level_rhs_hbm, later_ref,
     forward_ref, rest_ref,
+    tiles_ref, rhs_ref, subtree_inverse_ref, update_ref, rows_ref, level_rhs_ref, sems,
 ):
+    copies = fetch(
+        sems,
+        (tiles_hbm, tiles_ref),
+        (rhs_hbm, rhs_ref),
+        (subtree_inverse_hbm, subtree_inverse_ref),
+        (update_hbm, update_ref),
+        (rows_hbm, rows_ref),
+        (level_rhs_hbm, level_rhs_ref),
+    )
     columns, sub_rows = forward_ref.shape
+    copies[0].wait()
     live = live_columns(tiles_ref, columns, sub_rows)
+    copies[1].wait()
     masked = jnp.where(live, rhs_ref[...].astype(jnp.float32).T, 0.0).astype(jnp.bfloat16)
+    copies[2].wait()
     solved = dot(masked, subtree_inverse_ref[...], ((1,), (1,)), None)
     forward = jnp.where(live, solved, 0.0).astype(jnp.bfloat16)
     forward_ref[...] = forward
+    copies[3].wait()
     contrib = dot(forward, update_ref[...], ((1,), (1,)), None)
+    copies[4].wait()
     totals = []
     for s in range(level_rhs_ref.shape[0] // TILE):
         total = jnp.zeros((columns, TILE), jnp.float32)
@@ -172,20 +203,35 @@
             here = rows_ref[:, t : t + 1] == s
             total = total + jnp.where(here, contrib[:, t * TILE : (t + 1) * TILE], 0.0)
         totals.append(total)
+    copies[5].wait()
     rest_ref[...] = 0.25 * level_rhs_ref[...].T - jnp.concatenate(totals, axis=1)
 
 
-def part_kernel(rest_ref, inverse_ref, later_ref, part_ref):
-    part_ref[...] = dot(rest_ref[...], inverse_ref[...], ((1,), (1,)))
+def part_kernel(rest_ref, level_ref, later_ref, part_ref):
+    left = level_ref[3 * TILE : 3 * TILE + rest_ref.shape[1]]
+    right = level_ref[3 * TILE + rest_ref.shape[1] :]
+    part_ref[...] = dot(rest_ref[:, :TILE], left, ((1,), (1,))) + dot(
+        rest_ref[:, TILE:], right, ((1,), (1,))
+    )
 
 
 def subtree_backward_kernel(
-    solution_ref, forward_ref, subtree_inverse_ref, tiles_ref, update_ref, rows_ref,
+    solution_ref, forward_ref, tiles_hbm, rows_hbm, update_hbm, subtree_inverse_hbm,
     level_ref, final_ref,
+    tiles_ref, rows_ref, update_ref, subtree_inverse_ref, sems,
 ):
+    copies = fetch(
+        sems,
+        (tiles_hbm, tiles_ref),
+        (rows_hbm, rows_ref),
+        (update_hbm, update_ref),
+        (subtree_inverse_hbm, subtree_inverse_ref),
+    )
     columns, sub_rows = forward_ref.shape
+    level_ref[...] = solution_ref[...].T
+    copies[0].wait()
     live = live_columns(tiles_ref, columns, sub_rows)
-    level_ref[...] = solution_ref[...].T
+    copies[1].wait()
     picked = []
     for t in range(rows_ref.shape[1]):
         tile = solution_ref[:, :TILE]
@@ -193,21 +239,32 @@
             here = rows_ref[:, t : t + 1] == s
             tile = jnp.where(here, solution_ref[:, s * TILE : (s + 1) * TILE], tile)
         picked.append(tile.astype(jnp.bfloat16))
+    copies[2].wait()
     pulled = dot(jnp.concatenate(picked, axis=1), update_ref[...], precision=None)
     residue = forward_ref[...].astype(jnp.float32) - jnp.where(live, pulled, 0.0)
+    copies[3].wait()
     final = dot(residue.astype(jnp.bfloat16), subtree_inverse_ref[...], precision=None)
     final_ref[...] = jnp.where(live, final, 0.0).T
 
 
-def local_call(kernel, out_shape, *operands, later=()):
+def local_call(kernel, out_shape, *operands, fetched=(), later=(), weight=0, limit=8 * 2**20):
     vmem = pl.BlockSpec(memory_space=pltpu.VMEM)
+    scratch = [pltpu.VMEM(part.shape, part.dtype) for part in fetched]
+    if fetched:
+        scratch.append(pltpu.SemaphoreType.DMA((len(fetched),)))
     return pl.pallas_call(
         kernel,
         out_shape=out_shape,
-        in_specs=[vmem] * len(operands) + [pl.BlockSpec(memory_space=pl.ANY)] * len(later),
+        in_specs=[vmem] * len(operands)
+        + [pl.BlockSpec(memory_space=pltpu.HBM)] * len(fetched)
+        + [pl.BlockSpec(memory_space=pl.ANY)] * len(later),
         out_specs=[vmem] * len(out_shape),
-        compiler_params=pltpu.CompilerParams(vmem_limit_bytes=8 * 2**20),
-    )(*operands, *later)
+        scratch_shapes=scratch,
+        cost_estimate=pl.CostEstimate(
+            flops=weight * 10**9, bytes_accessed=weight * 2**20, transcendentals=0
+        ),
+        compiler_params=pltpu.CompilerParams(vmem_limit_bytes=limit),
+    )(*operands, *fetched, *later)
 
 
 def f32(*shape):
@@ -226,47 +283,55 @@
     rounds = len(SWAP)
     spot = 2 * place + lax.axis_index("core")
     bits = (spot >> lax.broadcasted_iota(jnp.int32, (8, 128), 0)) & 1
-    (level,) = local_call(level_kernel, [f32(2 * height + height + TILE, TILE)], inverse, couple)
+    (level,) = local_call(
+        level_kernel, [f32(3 * height + TILE, TILE)], fetched=(inverse, couple)
+    )
     sibling = lax.ppermute(level, "core", [(0, 1), (1, 0)])
     forward_sub, rest = local_call(
         subtree_forward_kernel,
         [jax.ShapeDtypeStruct((width, sub_rows), jnp.bfloat16), f32(width, height)],
-        subtree_inverse, rhs_sub, sub_tiles, block, rows, rhs_level,
+        fetched=(sub_tiles, rhs_sub, subtree_inverse, block, rows, rhs_level), later=(level,),
     )
     maps, pair_weights = local_call(
-        pair_kernel, [f32(2 * TILE, TILE), f32(2 * TILE, 2 * TILE)], bits, level, sibling
-    )
-    (part,) = local_call(part_kernel, [f32(width, height)], rest, inverse, later=(maps,))
+        pair_kernel, [f32(2 * TILE, TILE), f32(2 * TILE, 2 * TILE)], bits, level, sibling,
+        later=(rest,),
+    )
+    (part,) = local_call(part_kernel, [f32(width, height)], rest, level, later=(maps,))
     columns = width // members
     parts = lax.all_to_all(part.reshape(members, columns, height), group, 0, 0)
-    answers, weights, steps, chain = [], [], [], [maps]
-    for j in range(rounds):
-        if j == rounds - 1:
-            answers.append(swap(maps[TILE:], j, count))
-            break
+    answers, weights, steps = [], [], []
+
+    def advance_maps(j, maps, *later):
         answers.append(swap(maps, j, count))
         maps, weight, step = local_call(
             functools.partial(maps_kernel, j + 1),
             [f32(2 * TILE, TILE), f32(2 * TILE, 2 * TILE), f32(2 * TILE, TILE)],
-            bits, maps, answers[j],
+            bits, maps, answers[j], later=later, weight=MAPS_WEIGHT,
         )
         weights.append(weight)
         steps.append(step)
-        chain.append(maps)
+        return maps
+
+    maps = advance_maps(0, maps, part)
     owns, states, state = local_call(
         start_kernel,
         [f32(2, columns, height), f32(2, columns, 2 * TILE), f32(columns, 2 * TILE)],
-        bits, parts, level, sibling, pair_weights, later=(chain[1],),
+        bits, parts, level, sibling, pair_weights, later=(maps,),
     )
     sent, got = [], []
     for j in range(rounds):
         sent.append(state)
         got.append(swap(state, j, count))
+        if j < rounds - 2:
+            maps = advance_maps(j + 1, maps, state)
+        elif j == rounds - 2:
+            answers.append(swap(maps[TILE:], j + 1, count))
         if j < rounds - 1:
             (state,) = local_call(
                 functools.partial(state_kernel, j + 1),
                 [f32(columns, 2 * TILE)],
-                bits, state, got[j], weights[j], later=(chain[j + 2],) if j < 2 else (),
+                bits, state, got[j], weights[j], later=(maps,) if j < 2 else (),
+                weight=STATE_WEIGHT,
             )
     (shares,) = local_call(
         functools.partial(descend_kernel, rounds),
@@ -277,7 +342,8 @@
     solution, final = local_call(
         subtree_backward_kernel,
         [f32(height, width), f32(sub_rows, width)],
-        spread.reshape(width, -1), forward_sub, subtree_inverse, sub_tiles, block, rows,
+        spread.reshape(width, -1), forward_sub,
+        fetched=(sub_tiles, rows, block, subtree_inverse), limit=66 * 10**6,
     )
     return (solution[None], final[None, None])
 

time: 122 us -> 112 us (0.918)
  waiting for transfers between devices: 30.8 us -> 25 us
  starting transfers between devices: 55.8 us -> 51.4 us
  Pallas kernels: 11.7 us -> 15.4 us
  blocking collectives: 16 us -> 12.5 us
    ppermute x12, waiting for transfers between devices: 26.5 us -> 21.4 us  [swap(): return lax.ppermute(value, 'pair', [(n, n ^ SWAP[j]) for n in range(count)])]
    pallas_call x17, Pallas kernels: 11.7 us -> 15.4 us  [local_call(): pl.pallas_call(kernel, out_shape=out_shape, in_specs=[vmem] * len(operand...]
    all_to_all x1, blocking collectives: 16 us -> 12.5 us  [shards(): spread = lax.all_to_all(shares, group, 0, 0)]
    all_to_all x1, starting transfers between devices: 5.69 us -> 3.36 us  [shards(): parts = lax.all_to_all(part.reshape(members, columns, height), group, 0, 0)]
    ppermute x12, starting transfers between devices: 41.3 us -> 39.2 us  [swap(): return lax.ppermute(value, 'pair', [(n, n ^ SWAP[j]) for n in range(count)])]
    ppermute x1, waiting for transfers between devices: 1.4 us -> 0.01 us  [shards(): sibling = lax.ppermute(level, 'core', [(0, 1), (1, 0)])]
    unnamed x40 -> x16, local copies, waits for them, and re-layouts: 5.41 us -> 5.11 us
  transfers between devices with their start and end apart: 14 -> 14, of which waited for: 9 -> 7; matrix products, arithmetic and copies ran while one was open for 0% -> 0% of each run, Pallas kernels for 4% -> 7%
where the time goes in v5:
time: 112 us; the launch traced here: 111 us
  starting transfers between devices  51.4 us (46%)
  waiting for transfers between devices  25 us (22%)
  Pallas kernels  15.4 us (14%)
  blocking collectives  12.5 us (11%)
  local copies, waits for them, and re-layouts  5.19 us (5%)
  between operations  1.62 us (1%)
    ppermute x12, starting transfers between devices, swap(): return lax.ppermute(value, 'pair', [(n, n ^ SWAP[j]) for n in range(count)])  39.2 us
    ppermute x12, waiting for transfers between devices, swap(): return lax.ppermute(value, 'pair', [(n, n ^ SWAP[j]) for n in range(count)])  21.4 us
    pallas_call x17, Pallas kernels, local_call(): pl.pallas_call(kernel, out_shape=out_shape, in_specs=[vmem] * len(operand...  15.4 us
    all_to_all x1, blocking collectives, shards(): spread = lax.all_to_all(shares, group, 0, 0)  12.5 us
    ppermute x1, starting transfers between devices, shards(): sibling = lax.ppermute(level, 'core', [(0, 1), (1, 0)])  8.79 us
    unnamed x16, local copies, waits for them, and re-layouts  5.11 us
    all_to_all x1, waiting for transfers between devices, shards(): parts = lax.all_to_all(part.reshape(members, columns, height), group, 0, 0)  3.6 us
    all_to_all x1, starting transfers between devices, shards(): parts = lax.all_to_all(part.reshape(members, columns, height), group, 0, 0)  3.36 us
  transfers between devices with their start and end apart: 14, of which 7 were waited for; matrix products, arithmetic and copies ran while one was open for 0% of the time, Pallas kernels for 7%

profile of v5, /device:TPU:1, one launch (start us, length us, event | category | flops | bytes accessed | tf_op | source)
XLA Modules:
  0.0 111.1 jit_solution(576101928998392016)
XLA Ops:
  0.7 1.0 copy-done.3
  1.7 0.9 copy-done.6
  2.6 1.0 shard_map.95.later_ref.level_ref
  3.6 8.8 %collective-permute-start = (f32[896,128]{1,0:T(8,128)S(1)}, f32[896,128]{1,0:T(8,128)S(1)}, u32[]{:S(2)}, u32[]{:S(2)}) collective-permute-start(f32[896,128]{1,0:T(8,128)S(1)} %shard_map.95.later_ref.level_ref), channel_id=1, source_target_pairs={{0,4},{4,0},{1,5},{5,1},{2,6},{6,2},{3,7},{7,3},{8,12},{12,8},{9,1... | collective-permute-start | bytes 1376264 | tf_op jit(solution)/shard_map/ppermute | solution.py:289
  13.1 0.9 copy-done.2
  14.0 0.9 copy-done.4
  15.0 0.7 copy-done.7
  15.6 1.8 %shard_map.96 = (bf16[256,384]{1,0:T(8,128)(2,1)S(1)}, f32[256,256]{1,0:T(8,128)S(1)}) custom-call(s32[1,1]{1,0:T(1,128)S(6)} %copy.10.tiles_hbm, bf16[384,256]{1,0:T(8,128)(2,1)S(1)} %bitcast.17, bf16[384,384]{1,0:T(8,128)(2,1)S(1)} %bitcast.14, bf16[768,384]{1,0:T(8,128)(2,1)S(1)} %bitcast.12, s32[1,6]{1,0:T(1,128)S(1)} %bitcast.20, ...), custom_call_target="tpu_custom_call" | custom-call | tf_op jit(solution)/shard_map/pallas_call | solution.py:255
  17.4 0.7 copy-done.5
  18.7 1.9 %collective-permute-start.1 = (f32[256,128]{1,0:T(8,128)S(1)}, f32[256,128]{1,0:T(8,128)S(1)}, u32[]{:S(2)}, u32[]{:S(2)}) collective-permute-start(f32[256,128]{1,0:T(8,128)S(1)} %get-tuple-element.28.later_ref.own_ref), channel_id=1, source_target_pairs={{0,8},{8,0},{16,24},{24,16},{32,40},{40,32},{48,56},{56,48},{64,72... | collective-permute-start | bytes 393224 | tf_op jit(solution)/shard_map/ppermute | solution.py:26
  20.7 1.3 %shard_map.98.later_ref = f32[256,256]{1,0:T(8,128)} custom-call(f32[256,256]{1,0:T(8,128)S(1)} %get-tuple-element.26.later_ref.rest_ref, f32[896,128]{1,0:T(8,128)S(1)} %shard_map.95.later_ref.level_ref, f32[256,128]{1,0:T(8,128)S(1)} %get-tuple-element.28.later_ref.own_ref), custom_call_target="tpu_custom_call" | custom-call | tf_op jit(solution)/shard_map/pallas_call | solution.py:255
  21.9 3.4 %all-to-all-start = ((f32[8,32,256]{2,1,0:T(8,128)}), f32[8,32,256]{2,1,0:T(8,128)S(1)}, u32[]{:S(2)}, u32[]{:S(2)}) async-start(f32[8,32,256]{2,1,0:T(8,128)} %bitcast.7), calls=%async_computation | async-start | bytes 524288 | tf_op jit(solution)/shard_map/all_to_all | solution.py:301
  26.3 1.9 %collective-permute-start.3 = (f32[256,128]{1,0:T(8,128)S(1)}, f32[256,128]{1,0:T(8,128)S(1)}, u32[]{:S(2)}, u32[]{:S(2)}) collective-permute-start(f32[256,128]{1,0:T(8,128)S(1)} %get-tuple-element.29.later_ref.own_ref), channel_id=1, source_target_pairs={{0,24},{8,16},{16,8},{24,0},{32,56},{40,48},{48,40},{56,32},{64,88... | collective-permute-start | bytes 393224 | tf_op jit(solution)/shard_map/ppermute | solution.py:26
  28.2 3.6 %all-to-all-done.parts_ref = f32[8,32,256]{2,1,0:T(8,128)S(1)} async-done(((f32[8,32,256]{2,1,0:T(8,128)}), f32[8,32,256]{2,1,0:T(8,128)S(1)}, u32[]{:S(2)}, u32[]{:S(2)}) %all-to-all-start) | async-done | bytes 262176 | tf_op jit(solution)/shard_map/all_to_all | solution.py:301
  32.3 3.6 %collective-permute-start.2 = (f32[32,256]{1,0:T(8,128)S(1)}, f32[32,256]{1,0:T(8,128)S(1)}, u32[]{:S(2)}, u32[]{:S(2)}) collective-permute-start(f32[32,256]{1,0:T(8,128)S(1)} %get-tuple-element.32.later_ref.own_ref.refs_0_), channel_id=1, source_target_pairs={{0,8},{8,0},{16,24},{24,16},{32,40},{40,32},{48,56},{56,48},{64,72... | collective-permute-start | bytes 98312 | tf_op jit(solution)/shard_map/ppermute | solution.py:26
  36.6 1.9 %collective-permute-start.5 = (f32[256,128]{1,0:T(8,128)S(1)}, f32[256,128]{1,0:T(8,128)S(1)}, u32[]{:S(2)}, u32[]{:S(2)}) collective-permute-start(f32[256,128]{1,0:T(8,128)S(1)} %get-tuple-element.34.refs_0_.own_ref), channel_id=1, source_target_pairs={{0,32},{8,40},{16,48},{24,56},{32,0},{40,8},{48,16},{56,24},{64,96... | collective-permute-start | bytes 393224 | tf_op jit(solution)/shard_map/ppermute | solution.py:26
  38.8 1.9 %collective-permute-start.4 = (f32[32,256]{1,0:T(8,128)S(1)}, f32[32,256]{1,0:T(8,128)S(1)}, u32[]{:S(2)}, u32[]{:S(2)}) collective-permute-start(f32[32,256]{1,0:T(8,128)S(1)} %shard_map.102.later_ref.own_ref.refs_1_), channel_id=1, source_target_pairs={{0,24},{8,16},{16,8},{24,0},{32,56},{40,48},{48,40},{56,32},{64,88... | collective-permute-start | bytes 98312 | tf_op jit(solution)/shard_map/ppermute | solution.py:26
  40.7 2.2 %collective-permute-done.5.other_ref.refs_14_ = f32[256,128]{1,0:T(8,128)S(1)} collective-permute-done((f32[256,128]{1,0:T(8,128)S(1)}, f32[256,128]{1,0:T(8,128)S(1)}, u32[]{:S(2)}, u32[]{:S(2)}) %collective-permute-start.5) | collective-permute-done | bytes 131104 | tf_op jit(solution)/shard_map/ppermute | solution.py:26
  43.4 1.2 %collective-permute-done.4.other_ref.refs_7_ = f32[32,256]{1,0:T(8,128)S(1)} collective-permute-done((f32[32,256]{1,0:T(8,128)S(1)}, f32[32,256]{1,0:T(8,128)S(1)}, u32[]{:S(2)}, u32[]{:S(2)}) %collective-permute-start.4) | collective-permute-done | bytes 32800 | tf_op jit(solution)/shard_map/ppermute | solution.py:26
  44.9 3.4 %collective-permute-start.6 = (f32[32,256]{1,0:T(8,128)S(1)}, f32[32,256]{1,0:T(8,128)S(1)}, u32[]{:S(2)}, u32[]{:S(2)}) collective-permute-start(f32[32,256]{1,0:T(8,128)S(1)} %shard_map.104.own_ref.later_ref.refs_2_), channel_id=1, source_target_pairs={{0,32},{8,40},{16,48},{24,56},{32,0},{40,8},{48,16},{56,24},{64,96... | collective-permute-start | bytes 98312 | tf_op jit(solution)/shard_map/ppermute | solution.py:26
  48.3 1.9 %collective-permute-start.8 = (f32[256,128]{1,0:T(8,128)S(1)}, f32[256,128]{1,0:T(8,128)S(1)}, u32[]{:S(2)}, u32[]{:S(2)}) collective-permute-start(f32[256,128]{1,0:T(8,128)S(1)} %get-tuple-element.36.refs_0_.own_ref), channel_id=1, source_target_pairs={{0,64},{8,72},{16,80},{24,88},{32,96},{40,104},{48,112},{56,120},{... | collective-permute-start | bytes 393224 | tf_op jit(solution)/shard_map/ppermute | solution.py:26
  50.5 4.3 %collective-permute-start.7 = (f32[32,256]{1,0:T(8,128)S(1)}, f32[32,256]{1,0:T(8,128)S(1)}, u32[]{:S(2)}, u32[]{:S(2)}) collective-permute-start(f32[32,256]{1,0:T(8,128)S(1)} %shard_map.105.own_ref.later_ref.refs_3_), channel_id=1, source_target_pairs={{0,64},{8,72},{16,80},{24,88},{32,96},{40,104},{48,112},{56,120},{... | collective-permute-start | bytes 98312 | tf_op jit(solution)/shard_map/ppermute | solution.py:26
  54.7 3.4 %collective-permute-done.8.other_ref.refs_15_ = f32[256,128]{1,0:T(8,128)S(1)} collective-permute-done((f32[256,128]{1,0:T(8,128)S(1)}, f32[256,128]{1,0:T(8,128)S(1)}, u32[]{:S(2)}, u32[]{:S(2)}) %collective-permute-start.8) | collective-permute-done | bytes 131104 | tf_op jit(solution)/shard_map/ppermute | solution.py:26
  58.7 2.7 %collective-permute-start.10 = (f32[256,128]{1,0:T(8,128)S(1)}, f32[256,128]{1,0:T(8,128)S(1)}, u32[]{:S(2)}, u32[]{:S(2)}) collective-permute-start(f32[256,128]{1,0:T(8,128)S(1)} %get-tuple-element.39.own_ref), channel_id=1, source_target_pairs={{0,128},{8,136},{16,144},{24,152},{32,160},{40,168},{48,176},{56,1... | collective-permute-start | bytes 393224 | tf_op jit(solution)/shard_map/ppermute | solution.py:26
  61.7 6.5 %collective-permute-start.9 = (f32[32,256]{1,0:T(8,128)S(1)}, f32[32,256]{1,0:T(8,128)S(1)}, u32[]{:S(2)}, u32[]{:S(2)}) collective-permute-start(f32[32,256]{1,0:T(8,128)S(1)} %shard_map.107.own_ref.refs_4_), channel_id=1, source_target_pairs={{0,128},{8,136},{16,144},{24,152},{32,160},{40,168},{48,176},{56,1... | collective-permute-start | bytes 98312 | tf_op jit(solution)/shard_map/ppermute | solution.py:26
  68.2 8.9 %collective-permute-done.10.other_ref.refs_16_ = f32[256,128]{1,0:T(8,128)S(1)} collective-permute-done((f32[256,128]{1,0:T(8,128)S(1)}, f32[256,128]{1,0:T(8,128)S(1)}, u32[]{:S(2)}, u32[]{:S(2)}) %collective-permute-start.10) | collective-permute-done | bytes 131104 | tf_op jit(solution)/shard_map/ppermute | solution.py:26
  77.7 5.9 %collective-permute-start.12 = (f32[128,128]{1,0:T(8,128)S(1)}, f32[128,128]{1,0:T(8,128)S(1)}, u32[]{:S(2)}, u32[]{:S(2)}) collective-permute-start(f32[128,128]{1,0:T(8,128)S(1)} %slice.3), channel_id=1, source_target_pairs={{0,384},{8,392},{16,400},{24,408},{32,416},{40,424},{48,432},{56,4... | collective-permute-start | bytes 196616 | tf_op jit(solution)/shard_map/ppermute | solution.py:26
  83.8 3.3 %collective-permute-start.11 = (f32[32,256]{1,0:T(8,128)S(1)}, f32[32,256]{1,0:T(8,128)S(1)}, u32[]{:S(2)}, u32[]{:S(2)}) collective-permute-start(f32[32,256]{1,0:T(8,128)S(1)} %shard_map.109.refs_5_), channel_id=1, source_target_pairs={{0,384},{8,392},{16,400},{24,408},{32,416},{40,424},{48,432},{56,4... | collective-permute-start | bytes 98312 | tf_op jit(solution)/shard_map/ppermute | solution.py:26
  87.1 5.2 %collective-permute-done.11.refs_11_ = f32[32,256]{1,0:T(8,128)S(1)} collective-permute-done((f32[32,256]{1,0:T(8,128)S(1)}, f32[32,256]{1,0:T(8,128)S(1)}, u32[]{:S(2)}, u32[]{:S(2)}) %collective-permute-start.11) | collective-permute-done | bytes 32800 | tf_op jit(solution)/shard_map/ppermute | solution.py:26
  92.4 2.5 %shard_map.110 = f32[8,32,256]{2,1,0:T(8,128)S(1)} custom-call(s32[8,128]{1,0:T(8,128)S(1)} %iota.7.bits_ref, f32[896,128]{1,0:T(8,128)S(1)} %shard_map.95.later_ref.level_ref, f32[896,128]{1,0:T(8,128)S(1)} %collective-permute-done.sibling_ref, f32[256,256]{1,0:T(8,128)S(1)} %get-tuple-element.27.weights_ref, f32[2,32,256]{2,1,0:T(8,128)S(1)} %get-tuple-element.30.owns_ref, ...), custom_call_target="tpu_custom_call" | custom-call | tf_op jit(solution)/shard_map/pallas_call | solution.py:255
  94.9 12.5 %all_to_all.10 = f32[8,32,256]{2,1,0:T(8,128)} all-to-all(f32[8,32,256]{2,1,0:T(8,128)S(1)} %shard_map.110), channel_id=1, replica_groups=mesh['pair'=64,'core'=2,'rep'=4] {'core','rep'}, dimensions={0} | all-to-all | bytes 524288 | tf_op jit(solution)/shard_map/all_to_all | solution.py:341
  107.4 3.6 %shard_map.111 = (f32[256,256]{1,0:T(8,128)}, f32[384,256]{1,0:T(8,128)}) custom-call(f32[256,256]{1,0:T(8,128)} %bitcast.21, bf16[256,384]{1,0:T(8,128)(2,1)} %copy-done.5, s32[1,1]{1,0:T(1,128)S(6)} %copy.10.tiles_hbm, s32[1,6]{1,0:T(1,128)} %bitcast.19, bf16[768,384]{1,0:T(8,128)(2,1)} %bitcast.11, bf16[384,384]{1,0:T(8,128)(2,1)} %bitcast.13), custom_call_target="tpu_custom_call" | custom-call | tf_op jit(solution)/shard_map/pallas_call | solution.py:255
  (33 shorter events, 5.7 us)
Async XLA Ops:
  0.6 12.4 %copy-start = (bf16[1,1,768,384]{3,2,1,0:T(8,128)(2,1)S(1)}, bf16[1,1,768,384]{3,2,1,0:T(8,128)(2,1)}, u32[]{:S(2)}) copy-start(bf16[1,1,768,384]{3,2,1,0:T(8,128)(2,1)} %param.11) | copy-start | bytes 1769476
  0.6 1.0 copy-start.3
  1.7 0.9 copy-start.6
  2.6 10.5 %copy-start.1 = (bf16[1,1,384,384]{3,2,1,0:T(8,128)(2,1)S(1)}, bf16[1,1,384,384]{3,2,1,0:T(8,128)(2,1)}, u32[]{:S(2)}) copy-start(bf16[1,1,384,384]{3,2,1,0:T(8,128)(2,1)} %param.8) | copy-start | bytes 884740
  3.6 14.5 %collective-permute-start = (f32[896,128]{1,0:T(8,128)S(1)}, f32[896,128]{1,0:T(8,128)S(1)}, u32[]{:S(2)}, u32[]{:S(2)}) collective-permute-start(f32[896,128]{1,0:T(8,128)S(1)} %shard_map.95.later_ref.level_ref), channel_id=1, source_target_pairs={{0,4},{4,0},{1,5},{5,1},{2,6},{6,2},{3,7},{7,3},{8,12},{12,8},{9,1... | collective-permute-start | bytes 1376264 | tf_op jit(solution)/shard_map/ppermute | solution.py:289
  13.1 1.0 copy-start.2
  14.0 0.9 copy-start.4
  15.0 0.7 copy-start.7
  17.4 0.7 copy-start.5
  18.7 7.0 %collective-permute-start.1 = (f32[256,128]{1,0:T(8,128)S(1)}, f32[256,128]{1,0:T(8,128)S(1)}, u32[]{:S(2)}, u32[]{:S(2)}) collective-permute-start(f32[256,128]{1,0:T(8,128)S(1)} %get-tuple-element.28.later_ref.own_ref), channel_id=1, source_target_pairs={{0,8},{8,0},{16,24},{24,16},{32,40},{40,32},{48,56},{56,48},{64,72... | collective-permute-start | bytes 393224 | tf_op jit(solution)/shard_map/ppermute | solution.py:26
  21.9 9.9 %all-to-all-start = ((f32[8,32,256]{2,1,0:T(8,128)}), f32[8,32,256]{2,1,0:T(8,128)S(1)}, u32[]{:S(2)}, u32[]{:S(2)}) async-start(f32[8,32,256]{2,1,0:T(8,128)} %bitcast.7), calls=%async_computation | async-start | bytes 524288 | tf_op jit(solution)/shard_map/all_to_all | solution.py:301
  26.3 9.7 %collective-permute-start.3 = (f32[256,128]{1,0:T(8,128)S(1)}, f32[256,128]{1,0:T(8,128)S(1)}, u32[]{:S(2)}, u32[]{:S(2)}) collective-permute-start(f32[256,128]{1,0:T(8,128)S(1)} %get-tuple-element.29.later_ref.own_ref), channel_id=1, source_target_pairs={{0,24},{8,16},{16,8},{24,0},{32,56},{40,48},{48,40},{56,32},{64,88... | collective-permute-start | bytes 393224 | tf_op jit(solution)/shard_map/ppermute | solution.py:26
  32.3 6.2 %collective-permute-start.2 = (f32[32,256]{1,0:T(8,128)S(1)}, f32[32,256]{1,0:T(8,128)S(1)}, u32[]{:S(2)}, u32[]{:S(2)}) collective-permute-start(f32[32,256]{1,0:T(8,128)S(1)} %get-tuple-element.32.later_ref.own_ref.refs_0_), channel_id=1, source_target_pairs={{0,8},{8,0},{16,24},{24,16},{32,40},{40,32},{48,56},{56,48},{64,72... | collective-permute-start | bytes 98312 | tf_op jit(solution)/shard_map/ppermute | solution.py:26
  36.6 6.3 %collective-permute-start.5 = (f32[256,128]{1,0:T(8,128)S(1)}, f32[256,128]{1,0:T(8,128)S(1)}, u32[]{:S(2)}, u32[]{:S(2)}) collective-permute-start(f32[256,128]{1,0:T(8,128)S(1)} %get-tuple-element.34.refs_0_.own_ref), channel_id=1, source_target_pairs={{0,32},{8,40},{16,48},{24,56},{32,0},{40,8},{48,16},{56,24},{64,96... | collective-permute-start | bytes 393224 | tf_op jit(solution)/shard_map/ppermute | solution.py:26
  38.8 5.9 %collective-permute-start.4 = (f32[32,256]{1,0:T(8,128)S(1)}, f32[32,256]{1,0:T(8,128)S(1)}, u32[]{:S(2)}, u32[]{:S(2)}) collective-permute-start(f32[32,256]{1,0:T(8,128)S(1)} %shard_map.102.later_ref.own_ref.refs_1_), channel_id=1, source_target_pairs={{0,24},{8,16},{16,8},{24,0},{32,56},{40,48},{48,40},{56,32},{64,88... | collective-permute-start | bytes 98312 | tf_op jit(solution)/shard_map/ppermute | solution.py:26
  44.9 5.3 %collective-permute-start.6 = (f32[32,256]{1,0:T(8,128)S(1)}, f32[32,256]{1,0:T(8,128)S(1)}, u32[]{:S(2)}, u32[]{:S(2)}) collective-permute-start(f32[32,256]{1,0:T(8,128)S(1)} %shard_map.104.own_ref.later_ref.refs_2_), channel_id=1, source_target_pairs={{0,32},{8,40},{16,48},{24,56},{32,0},{40,8},{48,16},{56,24},{64,96... | collective-permute-start | bytes 98312 | tf_op jit(solution)/shard_map/ppermute | solution.py:26
  48.3 9.9 %collective-permute-start.8 = (f32[256,128]{1,0:T(8,128)S(1)}, f32[256,128]{1,0:T(8,128)S(1)}, u32[]{:S(2)}, u32[]{:S(2)}) collective-permute-start(f32[256,128]{1,0:T(8,128)S(1)} %get-tuple-element.36.refs_0_.own_ref), channel_id=1, source_target_pairs={{0,64},{8,72},{16,80},{24,88},{32,96},{40,104},{48,112},{56,120},{... | collective-permute-start | bytes 393224 | tf_op jit(solution)/shard_map/ppermute | solution.py:26
  50.5 11.0 %collective-permute-start.7 = (f32[32,256]{1,0:T(8,128)S(1)}, f32[32,256]{1,0:T(8,128)S(1)}, u32[]{:S(2)}, u32[]{:S(2)}) collective-permute-start(f32[32,256]{1,0:T(8,128)S(1)} %shard_map.105.own_ref.later_ref.refs_3_), channel_id=1, source_target_pairs={{0,64},{8,72},{16,80},{24,88},{32,96},{40,104},{48,112},{56,120},{... | collective-permute-start | bytes 98312 | tf_op jit(solution)/shard_map/ppermute | solution.py:26
  58.7 18.3 %collective-permute-start.10 = (f32[256,128]{1,0:T(8,128)S(1)}, f32[256,128]{1,0:T(8,128)S(1)}, u32[]{:S(2)}, u32[]{:S(2)}) collective-permute-start(f32[256,128]{1,0:T(8,128)S(1)} %get-tuple-element.39.own_ref), channel_id=1, source_target_pairs={{0,128},{8,136},{16,144},{24,152},{32,160},{40,168},{48,176},{56,1... | collective-permute-start | bytes 393224 | tf_op jit(solution)/shard_map/ppermute | solution.py:26
  61.7 21.8 %collective-permute-start.9 = (f32[32,256]{1,0:T(8,128)S(1)}, f32[32,256]{1,0:T(8,128)S(1)}, u32[]{:S(2)}, u32[]{:S(2)}) collective-permute-start(f32[32,256]{1,0:T(8,128)S(1)} %shard_map.107.own_ref.refs_4_), channel_id=1, source_target_pairs={{0,128},{8,136},{16,144},{24,152},{32,160},{40,168},{48,176},{56,1... | collective-permute-start | bytes 98312 | tf_op jit(solution)/shard_map/ppermute | solution.py:26
  77.7 14.7 %collective-permute-start.12 = (f32[128,128]{1,0:T(8,128)S(1)}, f32[128,128]{1,0:T(8,128)S(1)}, u32[]{:S(2)}, u32[]{:S(2)}) collective-permute-start(f32[128,128]{1,0:T(8,128)S(1)} %slice.3), channel_id=1, source_target_pairs={{0,384},{8,392},{16,400},{24,408},{32,416},{40,424},{48,432},{56,4... | collective-permute-start | bytes 196616 | tf_op jit(solution)/shard_map/ppermute | solution.py:26
  83.8 8.6 %collective-permute-start.11 = (f32[32,256]{1,0:T(8,128)S(1)}, f32[32,256]{1,0:T(8,128)S(1)}, u32[]{:S(2)}, u32[]{:S(2)}) collective-permute-start(f32[32,256]{1,0:T(8,128)S(1)} %shard_map.109.refs_5_), channel_id=1, source_target_pairs={{0,384},{8,392},{16,400},{24,408},{32,416},{40,424},{48,432},{56,4... | collective-permute-start | bytes 98312 | tf_op jit(solution)/shard_map/ppermute | solution.py:26

commit v6 on v4

--- a/solution.py
+++ b/solution.py
@@ -8,8 +8,14 @@
 from jax.sharding import Mesh, PartitionSpec as P
 
 TILE = 128
+HALF = TILE // 2
 HIGHEST = lax.Precision.HIGHEST
 SWAP = (1, 3, 4, 8, 16, 48)
+
+
+PACKED = 3
+MAPS_WEIGHT = 10
+STATE_WEIGHT = 1
 
 
 def dot(a, b, dims=((1,), (0,)), precision=HIGHEST):
@@ -26,22 +32,49 @@
     return bits_ref[at : at + 1, :1] == 1
 
 
-def level_kernel(inverse_ref, couple_ref, level_ref):
-    height = inverse_ref.shape[0]
-    gain = -dot(inverse_ref[...], couple_ref[...])
-    level_ref[:height] = gain
-    level_ref[height : height + TILE] = -dot(gain.T, gain)
-    level_ref[height + TILE : 2 * height + TILE] = inverse_ref[:, :TILE]
-    level_ref[2 * height + TILE :] = inverse_ref[:, TILE:]
-
-
-def join_maps(right, first, second, maps_ref, weights_ref, step_ref):
+def fetch(sems, *pairs):
+    copies = [
+        pltpu.make_async_copy(source, target, sems.at[i])
+        for i, (source, target) in enumerate(pairs)
+    ]
+    for copy in copies:
+        copy.start()
+    return copies
+
+
+def corners():
+    row = lax.broadcasted_iota(jnp.int32, (HALF, TILE), 0)
+    lane = lax.broadcasted_iota(jnp.int32, (HALF, TILE), 1)
+    return row, lane
+
+
+def pack(square):
+    row, lane = corners()
+    top, bottom = square[:HALF], square[HALF:]
+    body = jnp.where((lane >= HALF) & (row > lane - HALF), pltpu.roll(top, HALF, 1), bottom)
+    diagonal = jnp.sum(jnp.where(row == lane, top, 0.0), axis=0, keepdims=True)
+    return jnp.concatenate([body, jnp.broadcast_to(diagonal, (8, TILE))], axis=0)
+
+
+def unpack(packed):
+    row, lane = corners()
+    body, diagonal = packed[:HALF], packed[HALF : HALF + 1]
+    first = jnp.where((lane < HALF) & (row > lane), pltpu.roll(body, HALF, 1), 0.0)
+    first = jnp.where(row == lane, 0.5 * diagonal, first)
+    last = jnp.where((lane < HALF) | (row < lane - HALF), body, 0.0)
+    last = jnp.where(row == lane - HALF, 0.5 * body, last)
+    half = jnp.concatenate([first, last], axis=0)
+    return half + half.T
+
+
+def join_maps(right, first, second, maps_ref, weights_ref, step_ref=None):
     early = first[:TILE]
     product = dot(second, early)
     turn = product[TILE:]
+    flipped = early.T
+    answer = first[TILE:] + dot(flipped, turn)
     maps_ref[:TILE] = product[:TILE]
-    flipped = early.T
-    maps_ref[TILE:] = first[TILE:] + dot(flipped, turn)
+    maps_ref[TILE:] = answer
     weights_ref[:TILE, :TILE] = second[:TILE].T
     weights_ref[:TILE, TILE:] = turn
     weights_ref[TILE:, :TILE] = jnp.zeros_like(turn)
@@ -49,23 +82,33 @@
     if step_ref is not None:
         step_ref[:TILE] = jnp.where(right, flipped, turn.T)
         step_ref[TILE:] = jnp.where(right, 0.0, second[:TILE])
+    return product[:TILE], answer
 
 
 def pair_kernel(bits_ref, level_ref, sibling_ref, maps_ref, weights_ref):
     odd = pick(bits_ref, 0)
     own, other = level_ref[TILE : 3 * TILE], sibling_ref[TILE : 3 * TILE]
     join_maps(
-        None, jnp.where(odd, other, own), jnp.where(odd, own, other), maps_ref, weights_ref, None
-    )
-
-
-def maps_kernel(j, bits_ref, own_ref, other_ref, maps_ref, weights_ref, step_ref):
-    right = pick(bits_ref, j)
+        odd, jnp.where(odd, other, own), jnp.where(odd, own, other), maps_ref, weights_ref
+    )
+
+
+def maps_kernel(j, later, bits_ref, own_ref, other_ref, *refs):
+    maps_ref, weights_ref, step_ref, answer_ref, *message = refs[later:]
+    right = pick(bits_ref, j + 1)
     own, other = own_ref[...], other_ref[...]
-    join_maps(
+    if j >= PACKED:
+        other = jnp.concatenate([other[:TILE], unpack(other[TILE:])], axis=0)
+    answer_ref[...] = other[TILE:]
+    ahead, answer = join_maps(
         right, jnp.where(right, other, own), jnp.where(right, own, other),
         maps_ref, weights_ref, step_ref,
     )
+    if j + 1 >= PACKED:
+        packed = pack(answer)
+        if j + 2 < len(SWAP):
+            packed = jnp.concatenate([ahead, packed], axis=0)
+        message[0][...] = packed
 
 
 def join_state(first, second, weights):
@@ -75,7 +118,7 @@
 
 
 def start_kernel(
-    bits_ref, parts_ref, level_ref, sibling_ref, weights_ref, later_ref,
+    bits_ref, parts_ref, level_ref, sibling_ref, weights_ref,
     owns_ref, states_ref, state_ref,
 ):
     odd = pick(bits_ref, 0)
@@ -109,7 +152,7 @@
     height = owns_ref.shape[2]
     pushes = []
     for j in range(rounds):
-        answer = answers[j][answers[j].shape[0] - TILE :]
+        answer = answers[j][...] if j < rounds - 1 else unpack(answers[j][...])
         other = got[j][...]
         pushes.append(
             jnp.where(
@@ -154,17 +197,44 @@
     return lax.broadcasted_iota(jnp.int32, (rows, columns), 1) < TILE * tiles_ref[...]
 
 
-def subtree_forward_kernel(
-    subtree_inverse_ref, rhs_ref, tiles_ref, update_ref, rows_ref, level_rhs_ref,
-    forward_ref, rest_ref,
+def first_kernel(
+    inverse_hbm, couple_hbm, rhs_hbm, tiles_hbm, subtree_inverse_hbm, update_hbm, rows_hbm,
+    level_rhs_hbm,
+    level_ref, forward_ref, part_ref,
+    inverse_ref, couple_ref, rhs_ref, tiles_ref, subtree_inverse_ref, update_ref, rows_ref,
+    level_rhs_ref, sems,
 ):
+    copies = fetch(
+        sems,
+        (inverse_hbm, inverse_ref),
+        (couple_hbm, couple_ref),
+        (rhs_hbm, rhs_ref),
+        (tiles_hbm, tiles_ref),
+        (subtree_inverse_hbm, subtree_inverse_ref),
+        (update_hbm, update_ref),
+        (rows_hbm, rows_ref),
+        (level_rhs_hbm, level_rhs_ref),
+    )
+    height = inverse_ref.shape[0]
+    copies[0].wait()
+    copies[1].wait()
+    gain = -dot(inverse_ref[...], couple_ref[...])
+    level_ref[:height] = gain
+    level_ref[height : height + TILE] = -dot(gain.T, gain)
+    level_ref[height + TILE : 2 * height + TILE] = inverse_ref[:, :TILE]
+    level_ref[2 * height + TILE :] = inverse_ref[:, TILE:]
     columns, sub_rows = forward_ref.shape
+    copies[2].wait()
+    copies[3].wait()
     live = live_columns(tiles_ref, columns, sub_rows)
     masked = jnp.where(live, rhs_ref[...].astype(jnp.float32).T, 0.0).astype(jnp.bfloat16)
+    copies[4].wait()
     solved = dot(masked, subtree_inverse_ref[...], ((1,), (1,)), None)
     forward = jnp.where(live, solved, 0.0).astype(jnp.bfloat16)
     forward_ref[...] = forward
+    copies[5].wait()
     contrib = dot(forward, update_ref[...], ((1,), (1,)), None)
+    copies[6].wait()
     totals = []
     for s in range(level_rhs_ref.shape[0] // TILE):
         total = jnp.zeros((columns, TILE), jnp.float32)
@@ -172,11 +242,9 @@
             here = rows_ref[:, t : t + 1] == s
             total = total + jnp.where(here, contrib[:, t * TILE : (t + 1) * TILE], 0.0)
         totals.append(total)
-    rest_ref[...] = 0.25 * level_rhs_ref[...].T - jnp.concatenate(totals, axis=1)
-
-
-def part_kernel(rest_ref, inverse_ref, later_ref, part_ref):
-    part_ref[...] = dot(rest_ref[...], inverse_ref[...], ((1,), (1,)))
+    copies[7].wait()
+    rest = 0.25 * level_rhs_ref[...].T - jnp.concatenate(totals, axis=1)
+    part_ref[...] = dot(rest, inverse_ref[...], ((1,), (1,)))
 
 
 def subtree_backward_kernel(
@@ -199,15 +267,24 @@
     final_ref[...] = jnp.where(live, final, 0.0).T
 
 
-def local_call(kernel, out_shape, *operands, later=()):
+def local_call(kernel, out_shape, *operands, fetched=(), later=(), weight=0, limit=8 * 2**20):
     vmem = pl.BlockSpec(memory_space=pltpu.VMEM)
+    scratch = [pltpu.VMEM(part.shape, part.dtype) for part in fetched]
+    if fetched:
+        scratch.append(pltpu.SemaphoreType.DMA((len(fetched),)))
     return pl.pallas_call(
         kernel,
         out_shape=out_shape,
-        in_specs=[vmem] * len(operands) + [pl.BlockSpec(memory_space=pl.ANY)] * len(later),
+        in_specs=[vmem] * len(operands)
+        + [pl.BlockSpec(memory_space=pltpu.HBM)] * len(fetched)
+        + [pl.BlockSpec(memory_space=pl.ANY)] * len(later),
         out_specs=[vmem] * len(out_shape),
-        compiler_params=pltpu.CompilerParams(vmem_limit_bytes=8 * 2**20),
-    )(*operands, *later)
+        scratch_shapes=scratch,
+        cost_estimate=pl.CostEstimate(
+            flops=weight * 10**9, bytes_accessed=weight * 2**20, transcendentals=0
+        ),
+        compiler_params=pltpu.CompilerParams(vmem_limit_bytes=limit),
+    )(*operands, *fetched, *later)
 
 
 def f32(*shape):
@@ -226,47 +303,60 @@
     rounds = len(SWAP)
     spot = 2 * place + lax.axis_index("core")
     bits = (spot >> lax.broadcasted_iota(jnp.int32, (8, 128), 0)) & 1
-    (level,) = local_call(level_kernel, [f32(2 * height + height + TILE, TILE)], inverse, couple)
+    level, forward_sub, part = local_call(
+        first_kernel,
+        [
+            f32(3 * height + TILE, TILE),
+            jax.ShapeDtypeStruct((width, sub_rows), jnp.bfloat16),
+            f32(width, height),
+        ],
+        fetched=(inverse, couple, rhs_sub, sub_tiles, subtree_inverse, block, rows, rhs_level),
+        limit=66 * 10**6,
+    )
     sibling = lax.ppermute(level, "core", [(0, 1), (1, 0)])
-    forward_sub, rest = local_call(
-        subtree_forward_kernel,
-        [jax.ShapeDtypeStruct((width, sub_rows), jnp.bfloat16), f32(width, height)],
-        subtree_inverse, rhs_sub, sub_tiles, block, rows, rhs_level,
-    )
     maps, pair_weights = local_call(
         pair_kernel, [f32(2 * TILE, TILE), f32(2 * TILE, 2 * TILE)], bits, level, sibling
     )
-    (part,) = local_call(part_kernel, [f32(width, height)], rest, inverse, later=(maps,))
     columns = width // members
     parts = lax.all_to_all(part.reshape(members, columns, height), group, 0, 0)
-    answers, weights, steps, chain = [], [], [], [maps]
-    for j in range(rounds):
-        if j == rounds - 1:
-            answers.append(swap(maps[TILE:], j, count))
-            break
-        answers.append(swap(maps, j, count))
-        maps, weight, step = local_call(
-            functools.partial(maps_kernel, j + 1),
-            [f32(2 * TILE, TILE), f32(2 * TILE, 2 * TILE), f32(2 * TILE, TILE)],
-            bits, maps, answers[j],
+    answers, weights, steps = [], [], []
+
+    def advance_maps(j, maps, message, *later):
+        other = swap(message, j, count)
+        shapes = [
+            f32(2 * TILE, TILE), f32(2 * TILE, 2 * TILE), f32(2 * TILE, TILE), f32(TILE, TILE)
+        ]
+        if j + 1 >= PACKED:
+            shapes.append(f32(HALF + 8 + (TILE if j + 2 < rounds else 0), TILE))
+        maps, weight, step, answer, *message = local_call(
+            functools.partial(maps_kernel, j, len(later)),
+            shapes, bits, maps, other, later=later, weight=MAPS_WEIGHT,
         )
         weights.append(weight)
         steps.append(step)
-        chain.append(maps)
+        answers.append(answer)
+        return maps, message[0] if message else maps
+
+    maps, message = advance_maps(0, maps, maps, parts)
     owns, states, state = local_call(
         start_kernel,
         [f32(2, columns, height), f32(2, columns, 2 * TILE), f32(columns, 2 * TILE)],
-        bits, parts, level, sibling, pair_weights, later=(chain[1],),
+        bits, parts, level, sibling, pair_weights,
     )
     sent, got = [], []
     for j in range(rounds):
         sent.append(state)
         got.append(swap(state, j, count))
+        if j < rounds - 2:
+            maps, message = advance_maps(j + 1, maps, message, state)
+        elif j == rounds - 2:
+            answers.append(swap(message, j + 1, count))
         if j < rounds - 1:
             (state,) = local_call(
                 functools.partial(state_kernel, j + 1),
                 [f32(columns, 2 * TILE)],
-                bits, state, got[j], weights[j], later=(chain[j + 2],) if j < 2 else (),
+                bits, state, got[j], weights[j], later=(maps,) if j < 1 else (),
+                weight=STATE_WEIGHT,
             )
     (shares,) = local_call(
         functools.partial(descend_kernel, rounds),

time: 122 us -> 107 us (0.88)
  waiting for transfers between devices: 30.8 us -> 18.6 us
  local copies, waits for them, and re-layouts: 5.48 us -> 0.73 us
  starting transfers between devices: 55.8 us -> 51.9 us
  Pallas kernels: 11.7 us -> 14.6 us
  blocking collectives: 16 us -> 18.7 us
    ppermute x12, waiting for transfers between devices: 26.5 us -> 14.7 us  [swap(): return lax.ppermute(value, 'pair', [(n, n ^ SWAP[j]) for n in range(count)])]
    unnamed x40 -> x10, local copies, waits for them, and re-layouts: 5.41 us -> 0.66 us
    pallas_call x17 -> x15, Pallas kernels: 11.7 us -> 14.6 us  [local_call(): pl.pallas_call(kernel, out_shape=out_shape, in_specs=[vmem] * len(operand...]
    all_to_all x1, blocking collectives: 16 us -> 18.7 us  [shards(): spread = lax.all_to_all(shares, group, 0, 0)]
    all_to_all x1, starting transfers between devices: 5.69 us -> 3.38 us  [shards(): parts = lax.all_to_all(part.reshape(members, columns, height), group, 0, 0)]
    ppermute x12, starting transfers between devices: 41.3 us -> 39.6 us  [swap(): return lax.ppermute(value, 'pair', [(n, n ^ SWAP[j]) for n in range(count)])]
    ppermute x1, waiting for transfers between devices: 1.4 us -> 0.01 us  [shards(): sibling = lax.ppermute(level, 'core', [(0, 1), (1, 0)])]
  transfers between devices with their start and end apart: 14 -> 14, of which waited for: 9 -> 7; matrix products, arithmetic and copies ran while one was open for 0% -> 0% of each run, Pallas kernels for 4% -> 5%
where the time goes in v6:
time: 107 us; the launch traced here: 106 us
  starting transfers between devices  51.9 us (49%)
  blocking collectives  18.7 us (17%)
  waiting for transfers between devices  18.6 us (17%)
  Pallas kernels  14.6 us (14%)
  between operations  1.58 us (1%)
    ppermute x12, starting transfers between devices, swap(): return lax.ppermute(value, 'pair', [(n, n ^ SWAP[j]) for n in range(count)])  39.6 us
    all_to_all x1, blocking collectives, shards(): spread = lax.all_to_all(shares, group, 0, 0)  18.7 us
    ppermute x12, waiting for transfers between devices, swap(): return lax.ppermute(value, 'pair', [(n, n ^ SWAP[j]) for n in range(count)])  14.7 us
    pallas_call x15, Pallas kernels, local_call(): pl.pallas_call(kernel, out_shape=out_shape, in_specs=[vmem] * len(operand...  14.6 us
    ppermute x1, starting transfers between devices, shards(): sibling = lax.ppermute(level, 'core', [(0, 1), (1, 0)])  8.92 us
    all_to_all x1, waiting for transfers between devices, shards(): parts = lax.all_to_all(part.reshape(members, columns, height), group, 0, 0)  3.94 us
    all_to_all x1, starting transfers between devices, shards(): parts = lax.all_to_all(part.reshape(members, columns, height), group, 0, 0)  3.38 us
  transfers between devices with their start and end apart: 14, of which 7 were waited for; matrix products, arithmetic and copies ran while one was open for 0% of the time, Pallas kernels for 5%

profile of v6, /device:TPU:1, one launch (start us, length us, event | category | flops | bytes accessed | tf_op | source)
XLA Modules:
  0.0 106.1 jit_solution(12774983889465585932)
XLA Ops:
  1.3 4.5 %shard_map.95 = (f32[896,128]{1,0:T(8,128)}, bf16[256,384]{1,0:T(8,128)(2,1)}, f32[256,256]{1,0:T(8,128)}) custom-call(f32[256,256]{1,0:T(8,128)} %bitcast.19, f32[256,128]{1,0:T(8,128)} %bitcast.22, bf16[384,256]{1,0:T(8,128)(2,1)} %bitcast.21, s32[1,1]{1,0:T(1,128)S(6)} %copy.10.tiles_hbm.tiles_ref, bf16[384,384]{1,0:T(8,128)(2,1)} %bitcast.13, ...), custom_call_target="tpu_custom_call" | custom-call | tf_op jit(solution)/shard_map/pallas_call | solution.py:275
  5.8 8.9 %collective-permute-start = (f32[896,128]{1,0:T(8,128)}, f32[896,128]{1,0:T(8,128)S(1)}, u32[]{:S(2)}, u32[]{:S(2)}) collective-permute-start(f32[896,128]{1,0:T(8,128)} %get-tuple-element.34.level_ref), channel_id=1, source_target_pairs={{0,4},{4,0},{1,5},{5,1},{2,6},{6,2},{3,7},{7,3},{8,12},{12,8},{9,1... | collective-permute-start | bytes 1376264 | tf_op jit(solution)/shard_map/ppermute | solution.py:316
  14.7 3.4 %all-to-all-start = ((f32[8,32,256]{2,1,0:T(8,128)}), f32[8,32,256]{2,1,0:T(8,128)S(1)}, u32[]{:S(2)}, u32[]{:S(2)}) async-start(f32[8,32,256]{2,1,0:T(8,128)} %bitcast.18), calls=%async_computation | async-start | bytes 524288 | tf_op jit(solution)/shard_map/all_to_all | solution.py:321
  18.2 0.6 shard_map.96
  18.8 1.9 %collective-permute-start.2 = (f32[256,128]{1,0:T(8,128)S(1)}, f32[256,128]{1,0:T(8,128)S(1)}, u32[]{:S(2)}, u32[]{:S(2)}) collective-permute-start(f32[256,128]{1,0:T(8,128)S(1)} %get-tuple-element.40.own_ref), channel_id=1, source_target_pairs={{0,8},{8,0},{16,24},{24,16},{32,40},{40,32},{48,56},{56,48},{64,72... | collective-permute-start | bytes 393224 | tf_op jit(solution)/shard_map/ppermute | solution.py:28
  20.7 3.9 %all-to-all-done.parts_ref.refs_0_ = f32[8,32,256]{2,1,0:T(8,128)S(1)} async-done(((f32[8,32,256]{2,1,0:T(8,128)}), f32[8,32,256]{2,1,0:T(8,128)S(1)}, u32[]{:S(2)}, u32[]{:S(2)}) %all-to-all-start) | async-done | bytes 262176 | tf_op jit(solution)/shard_map/all_to_all | solution.py:321
  24.6 1.1 %collective-permute-done.2.other_ref = f32[256,128]{1,0:T(8,128)S(1)} collective-permute-done((f32[256,128]{1,0:T(8,128)S(1)}, f32[256,128]{1,0:T(8,128)S(1)}, u32[]{:S(2)}, u32[]{:S(2)}) %collective-permute-start.2) | collective-permute-done | bytes 131104 | tf_op jit(solution)/shard_map/ppermute | solution.py:28
  25.7 0.6 shard_map.98
  26.3 1.9 %collective-permute-start.3 = (f32[256,128]{1,0:T(8,128)S(1)}, f32[256,128]{1,0:T(8,128)S(1)}, u32[]{:S(2)}, u32[]{:S(2)}) collective-permute-start(f32[256,128]{1,0:T(8,128)S(1)} %get-tuple-element.42.own_ref), channel_id=1, source_target_pairs={{0,24},{8,16},{16,8},{24,0},{32,56},{40,48},{48,40},{56,32},{64,88... | collective-permute-start | bytes 393224 | tf_op jit(solution)/shard_map/ppermute | solution.py:28
  28.7 2.1 %collective-permute-start.1 = (f32[32,256]{1,0:T(8,128)S(1)}, f32[32,256]{1,0:T(8,128)S(1)}, u32[]{:S(2)}, u32[]{:S(2)}) collective-permute-start(f32[32,256]{1,0:T(8,128)S(1)} %get-tuple-element.39.refs_0_.own_ref), channel_id=1, source_target_pairs={{0,8},{8,0},{16,24},{24,16},{32,40},{40,32},{48,56},{56,48},{64,72... | collective-permute-start | bytes 98312 | tf_op jit(solution)/shard_map/ppermute | solution.py:28
  30.8 2.7 %collective-permute-done.3.other_ref = f32[256,128]{1,0:T(8,128)S(1)} collective-permute-done((f32[256,128]{1,0:T(8,128)S(1)}, f32[256,128]{1,0:T(8,128)S(1)}, u32[]{:S(2)}, u32[]{:S(2)}) %collective-permute-start.3) | collective-permute-done | bytes 131104 | tf_op jit(solution)/shard_map/ppermute | solution.py:28
  33.5 0.6 shard_map.99
  34.1 1.9 %collective-permute-start.6 = (f32[256,128]{1,0:T(8,128)S(1)}, f32[256,128]{1,0:T(8,128)S(1)}, u32[]{:S(2)}, u32[]{:S(2)}) collective-permute-start(f32[256,128]{1,0:T(8,128)S(1)} %get-tuple-element.43.refs_0_.own_ref), channel_id=1, source_target_pairs={{0,32},{8,40},{16,48},{24,56},{32,0},{40,8},{48,16},{56,24},{64,96... | collective-permute-start | bytes 393224 | tf_op jit(solution)/shard_map/ppermute | solution.py:28
  36.3 2.2 %collective-permute-start.4 = (f32[32,256]{1,0:T(8,128)S(1)}, f32[32,256]{1,0:T(8,128)S(1)}, u32[]{:S(2)}, u32[]{:S(2)}) collective-permute-start(f32[32,256]{1,0:T(8,128)S(1)} %shard_map.100.own_ref.refs_0_.refs_1_), channel_id=1, source_target_pairs={{0,24},{8,16},{16,8},{24,0},{32,56},{40,48},{48,40},{56,32},{64,88... | collective-permute-start | bytes 98312 | tf_op jit(solution)/shard_map/ppermute | solution.py:28
  38.6 3.6 %collective-permute-done.4.other_ref.refs_7_ = f32[32,256]{1,0:T(8,128)S(1)} collective-permute-done((f32[32,256]{1,0:T(8,128)S(1)}, f32[32,256]{1,0:T(8,128)S(1)}, u32[]{:S(2)}, u32[]{:S(2)}) %collective-permute-start.4) | collective-permute-done | bytes 32800 | tf_op jit(solution)/shard_map/ppermute | solution.py:28
  42.4 3.4 %collective-permute-start.5 = (f32[32,256]{1,0:T(8,128)S(1)}, f32[32,256]{1,0:T(8,128)S(1)}, u32[]{:S(2)}, u32[]{:S(2)}) collective-permute-start(f32[32,256]{1,0:T(8,128)S(1)} %shard_map.101.own_ref.refs_0_.refs_2_), channel_id=1, source_target_pairs={{0,32},{8,40},{16,48},{24,56},{32,0},{40,8},{48,16},{56,24},{64,96... | collective-permute-start | bytes 98312 | tf_op jit(solution)/shard_map/ppermute | solution.py:28
  45.8 0.7 shard_map.102
  46.5 1.9 %collective-permute-start.8 = (f32[200,128]{1,0:T(8,128)S(1)}, f32[200,128]{1,0:T(8,128)S(1)}, u32[]{:S(2)}, u32[]{:S(2)}) collective-permute-start(f32[200,128]{1,0:T(8,128)S(1)} %get-tuple-element.47), channel_id=1, source_target_pairs={{0,64},{8,72},{16,80},{24,88},{32,96},{40,104},{48,112},{56,120},{... | collective-permute-start | bytes 307208 | tf_op jit(solution)/shard_map/ppermute | solution.py:28
  48.7 4.3 %collective-permute-start.7 = (f32[32,256]{1,0:T(8,128)S(1)}, f32[32,256]{1,0:T(8,128)S(1)}, u32[]{:S(2)}, u32[]{:S(2)}) collective-permute-start(f32[32,256]{1,0:T(8,128)S(1)} %shard_map.103.own_ref.refs_0_.refs_3_), channel_id=1, source_target_pairs={{0,64},{8,72},{16,80},{24,88},{32,96},{40,104},{48,112},{56,120},{... | collective-permute-start | bytes 98312 | tf_op jit(solution)/shard_map/ppermute | solution.py:28
  53.0 0.7 collective-permute-done.8.other_ref
  53.6 0.7 shard_map.104
  54.4 5.0 %collective-permute-start.10 = (f32[200,128]{1,0:T(8,128)S(1)}, f32[200,128]{1,0:T(8,128)S(1)}, u32[]{:S(2)}, u32[]{:S(2)}) collective-permute-start(f32[200,128]{1,0:T(8,128)S(1)} %get-tuple-element.50), channel_id=1, source_target_pairs={{0,128},{8,136},{16,144},{24,152},{32,160},{40,168},{48,176},{56,1... | collective-permute-start | bytes 307208 | tf_op jit(solution)/shard_map/ppermute | solution.py:28
  59.7 4.6 %collective-permute-start.9 = (f32[32,256]{1,0:T(8,128)S(1)}, f32[32,256]{1,0:T(8,128)S(1)}, u32[]{:S(2)}, u32[]{:S(2)}) collective-permute-start(f32[32,256]{1,0:T(8,128)S(1)} %shard_map.105.own_ref.refs_4_), channel_id=1, source_target_pairs={{0,128},{8,136},{16,144},{24,152},{32,160},{40,168},{48,176},{56,1... | collective-permute-start | bytes 98312 | tf_op jit(solution)/shard_map/ppermute | solution.py:28
  64.2 1.8 %collective-permute-done.10.other_ref = f32[200,128]{1,0:T(8,128)S(1)} collective-permute-done((f32[200,128]{1,0:T(8,128)S(1)}, f32[200,128]{1,0:T(8,128)S(1)}, u32[]{:S(2)}, u32[]{:S(2)}) %collective-permute-start.10) | collective-permute-done | bytes 102432 | tf_op jit(solution)/shard_map/ppermute | solution.py:28
  66.1 1.3 %shard_map.106 = (f32[256,128]{1,0:T(8,128)}, f32[256,256]{1,0:T(8,128)S(1)}, f32[256,128]{1,0:T(8,128)S(1)}, f32[128,128]{1,0:T(8,128)S(1)}, f32[72,128]{1,0:T(8,128)S(1)}) custom-call(s32[8,128]{1,0:T(8,128)S(1)} %iota.7.bits_ref, f32[256,128]{1,0:T(8,128)S(1)} %get-tuple-element.49.own_ref, f32[200,128]{1,0:T(8,128)S(1)} %collective-permute-done.10.other_ref, ...), custom_call_target="tpu_custom_call" | custom-call | flops 10000000000 | bytes 10485760 | tf_op jit(solution)/shard_map/pallas_call | solution.py:275
  67.3 6.5 %collective-permute-start.12 = (f32[72,128]{1,0:T(8,128)S(1)}, f32[72,128]{1,0:T(8,128)S(1)}, u32[]{:S(2)}, u32[]{:S(2)}) collective-permute-start(f32[72,128]{1,0:T(8,128)S(1)} %get-tuple-element.57), channel_id=1, source_target_pairs={{0,384},{8,392},{16,400},{24,408},{32,416},{40,424},{48,432},{56,4... | collective-permute-start | bytes 110600 | tf_op jit(solution)/shard_map/ppermute | solution.py:28
  74.2 3.8 %collective-permute-start.11 = (f32[32,256]{1,0:T(8,128)S(1)}, f32[32,256]{1,0:T(8,128)S(1)}, u32[]{:S(2)}, u32[]{:S(2)}) collective-permute-start(f32[32,256]{1,0:T(8,128)S(1)} %shard_map.107.refs_5_), channel_id=1, source_target_pairs={{0,384},{8,392},{16,400},{24,408},{32,416},{40,424},{48,432},{56,4... | collective-permute-start | bytes 98312 | tf_op jit(solution)/shard_map/ppermute | solution.py:28
  78.0 4.8 %collective-permute-done.11.refs_11_ = f32[32,256]{1,0:T(8,128)S(1)} collective-permute-done((f32[32,256]{1,0:T(8,128)S(1)}, f32[32,256]{1,0:T(8,128)S(1)}, u32[]{:S(2)}, u32[]{:S(2)}) %collective-permute-start.11) | collective-permute-done | bytes 32800 | tf_op jit(solution)/shard_map/ppermute | solution.py:28
  82.8 2.5 %shard_map.108 = f32[8,32,256]{2,1,0:T(8,128)S(1)} custom-call(s32[8,128]{1,0:T(8,128)S(1)} %iota.7.bits_ref, f32[896,128]{1,0:T(8,128)S(1)} %copy-done, f32[896,128]{1,0:T(8,128)S(1)} %collective-permute-done.sibling_ref, f32[256,256]{1,0:T(8,128)S(1)} %get-tuple-element.35.weights_ref, f32[2,32,256]{2,1,0:T(8,128)S(1)} %get-tuple-element.37.owns_ref, ...), custom_call_target="tpu_custom_call" | custom-call | tf_op jit(solution)/shard_map/pallas_call | solution.py:275
  85.3 18.7 %all_to_all.10 = f32[8,32,256]{2,1,0:T(8,128)S(1)} all-to-all(f32[8,32,256]{2,1,0:T(8,128)S(1)} %shard_map.108), channel_id=1, replica_groups=mesh['pair'=64,'core'=2,'rep'=4] {'core','rep'}, dimensions={0} | all-to-all | bytes 524288 | tf_op jit(solution)/shard_map/all_to_all | solution.py:366
  104.0 0.6 copy-done.4
  104.6 1.5 %shard_map.109 = (f32[256,256]{1,0:T(8,128)}, f32[384,256]{1,0:T(8,128)}) custom-call(f32[256,256]{1,0:T(8,128)S(1)} %bitcast.15, bf16[256,384]{1,0:T(8,128)(2,1)S(1)} %copy-done.3, bf16[384,384]{1,0:T(8,128)(2,1)S(1)} %bitcast.14, s32[1,1]{1,0:T(1,128)S(6)} %copy.10.tiles_hbm.tiles_ref, bf16[768,384]{1,0:T(8,128)(2,1)S(1)} %bitcast.12, s32[1,6]{1,0:T(1,128)S(1)} %bitcast.17), custom_call_target="tpu_custom_call" | custom-call | tf_op jit(solution)/shard_map/pallas_call | solution.py:275
  (24 shorter events, 1.9 us)
Async XLA Ops:
  5.8 12.4 %copy-start = (f32[896,128]{1,0:T(8,128)S(1)}, f32[896,128]{1,0:T(8,128)}, u32[]{:S(2)}) copy-start(f32[896,128]{1,0:T(8,128)} %get-tuple-element.34.level_ref) | copy-start | bytes 1376260
  5.8 12.3 %collective-permute-start = (f32[896,128]{1,0:T(8,128)}, f32[896,128]{1,0:T(8,128)S(1)}, u32[]{:S(2)}, u32[]{:S(2)}) collective-permute-start(f32[896,128]{1,0:T(8,128)} %get-tuple-element.34.level_ref), channel_id=1, source_target_pairs={{0,4},{4,0},{1,5},{5,1},{2,6},{6,2},{3,7},{7,3},{8,12},{12,8},{9,1... | collective-permute-start | bytes 1376264 | tf_op jit(solution)/shard_map/ppermute | solution.py:316
  14.7 9.9 %all-to-all-start = ((f32[8,32,256]{2,1,0:T(8,128)}), f32[8,32,256]{2,1,0:T(8,128)S(1)}, u32[]{:S(2)}, u32[]{:S(2)}) async-start(f32[8,32,256]{2,1,0:T(8,128)} %bitcast.18), calls=%async_computation | async-start | bytes 524288 | tf_op jit(solution)/shard_map/all_to_all | solution.py:321
  18.8 7.0 %collective-permute-start.2 = (f32[256,128]{1,0:T(8,128)S(1)}, f32[256,128]{1,0:T(8,128)S(1)}, u32[]{:S(2)}, u32[]{:S(2)}) collective-permute-start(f32[256,128]{1,0:T(8,128)S(1)} %get-tuple-element.40.own_ref), channel_id=1, source_target_pairs={{0,8},{8,0},{16,24},{24,16},{32,40},{40,32},{48,56},{56,48},{64,72... | collective-permute-start | bytes 393224 | tf_op jit(solution)/shard_map/ppermute | solution.py:28
  26.3 7.3 %collective-permute-start.3 = (f32[256,128]{1,0:T(8,128)S(1)}, f32[256,128]{1,0:T(8,128)S(1)}, u32[]{:S(2)}, u32[]{:S(2)}) collective-permute-start(f32[256,128]{1,0:T(8,128)S(1)} %get-tuple-element.42.own_ref), channel_id=1, source_target_pairs={{0,24},{8,16},{16,8},{24,0},{32,56},{40,48},{48,40},{56,32},{64,88... | collective-permute-start | bytes 393224 | tf_op jit(solution)/shard_map/ppermute | solution.py:28
  28.7 7.3 %collective-permute-start.1 = (f32[32,256]{1,0:T(8,128)S(1)}, f32[32,256]{1,0:T(8,128)S(1)}, u32[]{:S(2)}, u32[]{:S(2)}) collective-permute-start(f32[32,256]{1,0:T(8,128)S(1)} %get-tuple-element.39.refs_0_.own_ref), channel_id=1, source_target_pairs={{0,8},{8,0},{16,24},{24,16},{32,40},{40,32},{48,56},{56,48},{64,72... | collective-permute-start | bytes 98312 | tf_op jit(solution)/shard_map/ppermute | solution.py:28
  34.1 11.7 %collective-permute-start.6 = (f32[256,128]{1,0:T(8,128)S(1)}, f32[256,128]{1,0:T(8,128)S(1)}, u32[]{:S(2)}, u32[]{:S(2)}) collective-permute-start(f32[256,128]{1,0:T(8,128)S(1)} %get-tuple-element.43.refs_0_.own_ref), channel_id=1, source_target_pairs={{0,32},{8,40},{16,48},{24,56},{32,0},{40,8},{48,16},{56,24},{64,96... | collective-permute-start | bytes 393224 | tf_op jit(solution)/shard_map/ppermute | solution.py:28
  36.3 5.9 %collective-permute-start.4 = (f32[32,256]{1,0:T(8,128)S(1)}, f32[32,256]{1,0:T(8,128)S(1)}, u32[]{:S(2)}, u32[]{:S(2)}) collective-permute-start(f32[32,256]{1,0:T(8,128)S(1)} %shard_map.100.own_ref.refs_0_.refs_1_), channel_id=1, source_target_pairs={{0,24},{8,16},{16,8},{24,0},{32,56},{40,48},{48,40},{56,32},{64,88... | collective-permute-start | bytes 98312 | tf_op jit(solution)/shard_map/ppermute | solution.py:28
  42.4 6.0 %collective-permute-start.5 = (f32[32,256]{1,0:T(8,128)S(1)}, f32[32,256]{1,0:T(8,128)S(1)}, u32[]{:S(2)}, u32[]{:S(2)}) collective-permute-start(f32[32,256]{1,0:T(8,128)S(1)} %shard_map.101.own_ref.refs_0_.refs_2_), channel_id=1, source_target_pairs={{0,32},{8,40},{16,48},{24,56},{32,0},{40,8},{48,16},{56,24},{64,96... | collective-permute-start | bytes 98312 | tf_op jit(solution)/shard_map/ppermute | solution.py:28
  46.5 7.1 %collective-permute-start.8 = (f32[200,128]{1,0:T(8,128)S(1)}, f32[200,128]{1,0:T(8,128)S(1)}, u32[]{:S(2)}, u32[]{:S(2)}) collective-permute-start(f32[200,128]{1,0:T(8,128)S(1)} %get-tuple-element.47), channel_id=1, source_target_pairs={{0,64},{8,72},{16,80},{24,88},{32,96},{40,104},{48,112},{56,120},{... | collective-permute-start | bytes 307208 | tf_op jit(solution)/shard_map/ppermute | solution.py:28
  48.7 10.7 %collective-permute-start.7 = (f32[32,256]{1,0:T(8,128)S(1)}, f32[32,256]{1,0:T(8,128)S(1)}, u32[]{:S(2)}, u32[]{:S(2)}) collective-permute-start(f32[32,256]{1,0:T(8,128)S(1)} %shard_map.103.own_ref.refs_0_.refs_3_), channel_id=1, source_target_pairs={{0,64},{8,72},{16,80},{24,88},{32,96},{40,104},{48,112},{56,120},{... | collective-permute-start | bytes 98312 | tf_op jit(solution)/shard_map/ppermute | solution.py:28
  54.4 11.7 %collective-permute-start.10 = (f32[200,128]{1,0:T(8,128)S(1)}, f32[200,128]{1,0:T(8,128)S(1)}, u32[]{:S(2)}, u32[]{:S(2)}) collective-permute-start(f32[200,128]{1,0:T(8,128)S(1)} %get-tuple-element.50), channel_id=1, source_target_pairs={{0,128},{8,136},{16,144},{24,152},{32,160},{40,168},{48,176},{56,1... | collective-permute-start | bytes 307208 | tf_op jit(solution)/shard_map/ppermute | solution.py:28
  59.7 14.3 %collective-permute-start.9 = (f32[32,256]{1,0:T(8,128)S(1)}, f32[32,256]{1,0:T(8,128)S(1)}, u32[]{:S(2)}, u32[]{:S(2)}) collective-permute-start(f32[32,256]{1,0:T(8,128)S(1)} %shard_map.105.own_ref.refs_4_), channel_id=1, source_target_pairs={{0,128},{8,136},{16,144},{24,152},{32,160},{40,168},{48,176},{56,1... | collective-permute-start | bytes 98312 | tf_op jit(solution)/shard_map/ppermute | solution.py:28
  67.3 15.4 %collective-permute-start.12 = (f32[72,128]{1,0:T(8,128)S(1)}, f32[72,128]{1,0:T(8,128)S(1)}, u32[]{:S(2)}, u32[]{:S(2)}) collective-permute-start(f32[72,128]{1,0:T(8,128)S(1)} %get-tuple-element.57), channel_id=1, source_target_pairs={{0,384},{8,392},{16,400},{24,408},{32,416},{40,424},{48,432},{56,4... | collective-permute-start | bytes 110600 | tf_op jit(solution)/shard_map/ppermute | solution.py:28
  74.2 8.6 %collective-permute-start.11 = (f32[32,256]{1,0:T(8,128)S(1)}, f32[32,256]{1,0:T(8,128)S(1)}, u32[]{:S(2)}, u32[]{:S(2)}) collective-permute-start(f32[32,256]{1,0:T(8,128)S(1)} %shard_map.107.refs_5_), channel_id=1, source_target_pairs={{0,384},{8,392},{16,400},{24,408},{32,416},{40,424},{48,432},{56,4... | collective-permute-start | bytes 98312 | tf_op jit(solution)/shard_map/ppermute | solution.py:28
  82.8 21.2 %copy-start.1 = (bf16[1,1,768,384]{3,2,1,0:T(8,128)(2,1)S(1)}, bf16[1,1,768,384]{3,2,1,0:T(8,128)(2,1)}, u32[]{:S(2)}) copy-start(bf16[1,1,768,384]{3,2,1,0:T(8,128)(2,1)} %param.11) | copy-start | bytes 1769476
  85.2 18.7 %copy-start.2 = (bf16[1,1,384,384]{3,2,1,0:T(8,128)(2,1)S(1)}, bf16[1,1,384,384]{3,2,1,0:T(8,128)(2,1)}, u32[]{:S(2)}) copy-start(bf16[1,1,384,384]{3,2,1,0:T(8,128)(2,1)} %param.8) | copy-start | bytes 884740
  85.3 18.7 %copy-start.3 = (bf16[256,384]{1,0:T(8,128)(2,1)S(1)}, bf16[256,384]{1,0:T(8,128)(2,1)}, u32[]{:S(2)}) copy-start(bf16[256,384]{1,0:T(8,128)(2,1)} %get-tuple-element.63.forward_ref) | copy-start | bytes 589828
  103.9 0.7 copy-start.4

commit v7 on v6

--- a/solution.py
+++ b/solution.py
@@ -9,13 +9,15 @@
 
 TILE = 128
 HALF = TILE // 2
+MARKS = 16
 HIGHEST = lax.Precision.HIGHEST
 SWAP = (1, 3, 4, 8, 16, 48)
 
 
 PACKED = 3
-MAPS_WEIGHT = 10
-STATE_WEIGHT = 1
+MAPS_WEIGHT = (3, 10, 0, 30, 30)
+STATE_WEIGHT = (30, 10, 30, 10, 30)
+BEHIND = (True, True, False, True)
 
 
 def dot(a, b, dims=((1,), (0,)), precision=HIGHEST):
@@ -73,8 +75,9 @@
     turn = product[TILE:]
     flipped = early.T
     answer = first[TILE:] + dot(flipped, turn)
-    maps_ref[:TILE] = product[:TILE]
-    maps_ref[TILE:] = answer
+    if maps_ref is not None:
+        maps_ref[:TILE] = product[:TILE]
+        maps_ref[TILE:] = answer
     weights_ref[:TILE, :TILE] = second[:TILE].T
     weights_ref[:TILE, TILE:] = turn
     weights_ref[TILE:, :TILE] = jnp.zeros_like(turn)
@@ -94,7 +97,7 @@
 
 
 def maps_kernel(j, later, bits_ref, own_ref, other_ref, *refs):
-    maps_ref, weights_ref, step_ref, answer_ref, *message = refs[later:]
+    weights_ref, step_ref, answer_ref, *rest = refs[later:]
     right = pick(bits_ref, j + 1)
     own, other = own_ref[...], other_ref[...]
     if j >= PACKED:
@@ -102,13 +105,13 @@
     answer_ref[...] = other[TILE:]
     ahead, answer = join_maps(
         right, jnp.where(right, other, own), jnp.where(right, own, other),
-        maps_ref, weights_ref, step_ref,
+        rest[0] if j + 2 < len(SWAP) else None, weights_ref, step_ref,
     )
     if j + 1 >= PACKED:
         packed = pack(answer)
         if j + 2 < len(SWAP):
             packed = jnp.concatenate([ahead, packed], axis=0)
-        message[0][...] = packed
+        rest[-1][...] = packed
 
 
 def join_state(first, second, weights):
@@ -146,55 +149,74 @@
 
 def descend_kernel(rounds, bits_ref, level_ref, sibling_ref, weights_ref, owns_ref, states_ref, *refs):
     sent, got = refs[:rounds], refs[rounds : 2 * rounds]
-    answers, steps = refs[2 * rounds : 3 * rounds], refs[3 * rounds : -1]
-    shares_ref = refs[-1]
+    answers, steps = refs[2 * rounds : 3 * rounds], refs[3 * rounds : 4 * rounds]
+    descent_ref = refs[-1]
     odd = pick(bits_ref, 0)
     height = owns_ref.shape[2]
     pushes = []
     for j in range(rounds):
-        answer = answers[j][...] if j < rounds - 1 else unpack(answers[j][...])
         other = got[j][...]
         pushes.append(
             jnp.where(
                 pick(bits_ref, j + 1),
                 other[:, :TILE],
-                other[:, TILE:] + dot(sent[j][:, :TILE], answer),
+                other[:, TILE:] + dot(sent[j][:, :TILE], answers[j][...]),
             )
         )
-    before = jnp.zeros_like(pushes[0])
-    after = before
+
+    def under(constant):
+        return jnp.concatenate([jnp.zeros((TILE, constant.shape[1]), jnp.float32), constant], axis=0)
+
+    row = lax.broadcasted_iota(jnp.int32, (TILE + owns_ref.shape[1], TILE), 0)
+    lane = lax.broadcasted_iota(jnp.int32, (TILE + owns_ref.shape[1], TILE), 1)
+    basis = jnp.where(row == lane, 1.0, 0.0)
+    right = pick(bits_ref, rounds + 1)
+    before, after = jnp.where(right, basis, 0.0), jnp.where(right, 0.0, basis)
     for j in reversed(range(rounds)):
-        right, push = pick(bits_ref, j + 1), pushes[j]
-        if j < rounds - 1:
-            push = push + dot(jnp.concatenate([before, after], axis=1), steps[j][...])
+        right = pick(bits_ref, j + 1)
+        push = under(pushes[j]) + dot(jnp.concatenate([before, after], axis=1), steps[j][...])
         before, after = jnp.where(right, push, before), jnp.where(right, after, push)
     own, other = level_ref[...], sibling_ref[...]
     levels = (jnp.where(odd, other, own), jnp.where(odd, own, other))
     maps = [level[TILE : 3 * TILE] for level in levels]
     entry = states_ref[0, :, :TILE]
-    middle_before = entry + dot(before, maps[0][:TILE], ((1,), (1,)))
+    middle_before = under(entry) + dot(before, maps[0][:TILE], ((1,), (1,)))
     middle_after = (
-        states_ref[1, :, TILE:]
-        + dot(entry, maps[1][TILE:])
+        under(states_ref[1, :, TILE:] + dot(entry, maps[1][TILE:]))
         + dot(before, weights_ref[:TILE, TILE:], ((1,), (1,)))
         + dot(after, maps[1][:TILE])
     )
-    reps = shares_ref.shape[0] // 2
     ends = ((before, middle_after), (middle_before, after))
     for c in range(2):
         level = levels[c]
-        forward = owns_ref[c] + dot(ends[c][0], level[:height], ((1,), (1,)))
+        forward = under(owns_ref[c]) + dot(ends[c][0], level[:height], ((1,), (1,)))
         forward = jnp.concatenate(
             [forward[:, :TILE], forward[:, TILE:] - ends[c][1]], axis=1
         )
-        left = dot(forward, level[height + TILE : 2 * height + TILE])
-        share = jnp.concatenate([left, dot(forward, level[2 * height + TILE :])], axis=1)
+        descent_ref[:, 2 * c * TILE : (2 * c + 1) * TILE] = dot(
+            forward, level[height + TILE : 2 * height + TILE]
+        )
+        descent_ref[:, (2 * c + 1) * TILE : (2 * c + 2) * TILE] = dot(
+            forward, level[2 * height + TILE :]
+        )
+
+
+def finish_kernel(rounds, bits_ref, sent_ref, got_ref, answer_ref, descent_ref, shares_ref):
+    other = got_ref[...]
+    push = jnp.where(
+        pick(bits_ref, rounds),
+        other[:, :TILE],
+        other[:, TILE:] + dot(sent_ref[:, :TILE], unpack(answer_ref[...])),
+    )
+    both = descent_ref[TILE:] + dot(push, descent_ref[:TILE])
+    reps, height = shares_ref.shape[0] // 2, shares_ref.shape[2]
+    for c in range(2):
         for r in range(reps):
-            shares_ref[c * reps + r] = share
-
-
-def live_columns(tiles_ref, rows, columns):
-    return lax.broadcasted_iota(jnp.int32, (rows, columns), 1) < TILE * tiles_ref[...]
+            shares_ref[c * reps + r] = both[:, c * height : (c + 1) * height]
+
+
+def live_columns(tiles, rows, columns):
+    return lax.broadcasted_iota(jnp.int32, (rows, columns), 1) < TILE * tiles
 
 
 def first_kernel(
@@ -223,15 +245,15 @@
     level_ref[height : height + TILE] = -dot(gain.T, gain)
     level_ref[height + TILE : 2 * height + TILE] = inverse_ref[:, :TILE]
     level_ref[2 * height + TILE :] = inverse_ref[:, TILE:]
-    columns, sub_rows = forward_ref.shape
+    columns, sub_rows = rhs_ref.shape[1], rhs_ref.shape[0]
     copies[2].wait()
     copies[3].wait()
-    live = live_columns(tiles_ref, columns, sub_rows)
+    live = live_columns(tiles_ref[...], columns, sub_rows)
     masked = jnp.where(live, rhs_ref[...].astype(jnp.float32).T, 0.0).astype(jnp.bfloat16)
     copies[4].wait()
     solved = dot(masked, subtree_inverse_ref[...], ((1,), (1,)), None)
     forward = jnp.where(live, solved, 0.0).astype(jnp.bfloat16)
-    forward_ref[...] = forward
+    forward_ref[:columns] = forward
     copies[5].wait()
     contrib = dot(forward, update_ref[...], ((1,), (1,)), None)
     copies[6].wait()
@@ -242,27 +264,33 @@
             here = rows_ref[:, t : t + 1] == s
             total = total + jnp.where(here, contrib[:, t * TILE : (t + 1) * TILE], 0.0)
         totals.append(total)
+    row = lax.broadcasted_iota(jnp.int32, (MARKS, sub_rows), 0)
+    lane = lax.broadcasted_iota(jnp.int32, (MARKS, sub_rows), 1)
+    marks = jnp.where(row == 0, tiles_ref[...], 0)
+    for t in range(rows_ref.shape[1]):
+        marks = jnp.where((row == 1) & (lane == t), rows_ref[:, t : t + 1], marks)
+    forward_ref[columns:] = marks.astype(jnp.float32).astype(jnp.bfloat16)
     copies[7].wait()
     rest = 0.25 * level_rhs_ref[...].T - jnp.concatenate(totals, axis=1)
     part_ref[...] = dot(rest, inverse_ref[...], ((1,), (1,)))
 
 
 def subtree_backward_kernel(
-    solution_ref, forward_ref, subtree_inverse_ref, tiles_ref, update_ref, rows_ref,
-    level_ref, final_ref,
+    solution_ref, forward_ref, subtree_inverse_ref, update_ref, level_ref, final_ref
 ):
-    columns, sub_rows = forward_ref.shape
-    live = live_columns(tiles_ref, columns, sub_rows)
+    columns, sub_rows = solution_ref.shape[0], forward_ref.shape[1]
+    marks = forward_ref[columns:].astype(jnp.float32).astype(jnp.int32)
+    live = live_columns(marks[:1, :1], columns, sub_rows)
     level_ref[...] = solution_ref[...].T
     picked = []
-    for t in range(rows_ref.shape[1]):
+    for t in range(update_ref.shape[0] // TILE):
         tile = solution_ref[:, :TILE]
         for s in range(1, solution_ref.shape[1] // TILE):
-            here = rows_ref[:, t : t + 1] == s
+            here = marks[1:2, t : t + 1] == s
             tile = jnp.where(here, solution_ref[:, s * TILE : (s + 1) * TILE], tile)
         picked.append(tile.astype(jnp.bfloat16))
     pulled = dot(jnp.concatenate(picked, axis=1), update_ref[...], precision=None)
-    residue = forward_ref[...].astype(jnp.float32) - jnp.where(live, pulled, 0.0)
+    residue = forward_ref[:columns].astype(jnp.float32) - jnp.where(live, pulled, 0.0)
     final = dot(residue.astype(jnp.bfloat16), subtree_inverse_ref[...], precision=None)
     final_ref[...] = jnp.where(live, final, 0.0).T
 
@@ -307,7 +335,7 @@
         first_kernel,
         [
             f32(3 * height + TILE, TILE),
-            jax.ShapeDtypeStruct((width, sub_rows), jnp.bfloat16),
+            jax.ShapeDtypeStruct((width + MARKS, sub_rows), jnp.bfloat16),
             f32(width, height),
         ],
         fetched=(inverse, couple, rhs_sub, sub_tiles, subtree_inverse, block, rows, rhs_level),
@@ -324,18 +352,20 @@
     def advance_maps(j, maps, message, *later):
         other = swap(message, j, count)
         shapes = [
-            f32(2 * TILE, TILE), f32(2 * TILE, 2 * TILE), f32(2 * TILE, TILE), f32(TILE, TILE)
+            f32(2 * TILE, 2 * TILE), f32(2 * TILE, TILE), f32(TILE, TILE)
         ]
+        if j + 2 < rounds:
+            shapes.append(f32(2 * TILE, TILE))
         if j + 1 >= PACKED:
             shapes.append(f32(HALF + 8 + (TILE if j + 2 < rounds else 0), TILE))
-        maps, weight, step, answer, *message = local_call(
+        weight, step, answer, *rest = local_call(
             functools.partial(maps_kernel, j, len(later)),
-            shapes, bits, maps, other, later=later, weight=MAPS_WEIGHT,
+            shapes, bits, maps, other, later=later, weight=MAPS_WEIGHT[j],
         )
         weights.append(weight)
         steps.append(step)
         answers.append(answer)
-        return maps, message[0] if message else maps
+        return rest[0], rest[-1]
 
     maps, message = advance_maps(0, maps, maps, parts)
     owns, states, state = local_call(
@@ -348,26 +378,33 @@
         sent.append(state)
         got.append(swap(state, j, count))
         if j < rounds - 2:
-            maps, message = advance_maps(j + 1, maps, message, state)
+            later = (state,) if BEHIND[j] else ()
+            maps, message = advance_maps(j + 1, maps, message, *later)
         elif j == rounds - 2:
             answers.append(swap(message, j + 1, count))
         if j < rounds - 1:
             (state,) = local_call(
                 functools.partial(state_kernel, j + 1),
                 [f32(columns, 2 * TILE)],
-                bits, state, got[j], weights[j], later=(maps,) if j < 1 else (),
-                weight=STATE_WEIGHT,
+                bits, state, got[j], weights[j],
+                weight=STATE_WEIGHT[j],
             )
+    (descent,) = local_call(
+        functools.partial(descend_kernel, rounds - 1),
+        [f32(TILE + columns, 2 * height)],
+        bits, level, sibling, pair_weights, owns, states,
+        *sent[:-1], *got[:-1], *answers[:-1], *steps,
+    )
     (shares,) = local_call(
-        functools.partial(descend_kernel, rounds),
+        functools.partial(finish_kernel, rounds),
         [f32(members, columns, height)],
-        bits, level, sibling, pair_weights, owns, states, *sent, *got, *answers, *steps,
+        bits, sent[-1], got[-1], answers[-1], descent,
     )
     spread = lax.all_to_all(shares, group, 0, 0)
     solution, final = local_call(
         subtree_backward_kernel,
         [f32(height, width), f32(sub_rows, width)],
-        spread.reshape(width, -1), forward_sub, subtree_inverse, sub_tiles, block, rows,
+        spread.reshape(width, -1), forward_sub, subtree_inverse, block,
     )
     return (solution[None], final[None, None])
 

time: 107 us -> 99.2 us (0.927)
  waiting for transfers between devices: 18.6 us -> 13 us
  blocking collectives: 18.7 us -> 15.3 us
  Pallas kernels: 14.6 us -> 15.7 us
    ppermute x12, waiting for transfers between devices: 14.7 us -> 9.03 us  [swap(): return lax.ppermute(value, 'pair', [(n, n ^ SWAP[j]) for n in range(count)])]
    all_to_all x1, blocking collectives: 18.7 us -> 15.3 us  [shards(): spread = lax.all_to_all(shares, group, 0, 0)]
    pallas_call x15 -> x16, Pallas kernels: 14.6 us -> 15.7 us  [local_call(): pl.pallas_call(kernel, out_shape=out_shape, in_specs=[vmem] * len(operand...]
  transfers between devices with their start and end apart: 14 -> 14, of which waited for: 7 -> 6; matrix products, arithmetic and copies ran while one was open for 0% -> 0% of each run, Pallas kernels for 5% -> 9%
where the time goes in v7:
time: 99.2 us; the launch traced here: 98.5 us
  starting transfers between devices  52.8 us (53%)
  Pallas kernels  15.7 us (16%)
  blocking collectives  15.3 us (15%)
  waiting for transfers between devices  13 us (13%)
  between operations  1.61 us (2%)
    ppermute x12, starting transfers between devices, swap(): return lax.ppermute(value, 'pair', [(n, n ^ SWAP[j]) for n in range(count)])  40.5 us
    pallas_call x16, Pallas kernels, local_call(): pl.pallas_call(kernel, out_shape=out_shape, in_specs=[vmem] * len(operand...  15.7 us
    all_to_all x1, blocking collectives, shards(): spread = lax.all_to_all(shares, group, 0, 0)  15.3 us
    ppermute x12, waiting for transfers between devices, swap(): return lax.ppermute(value, 'pair', [(n, n ^ SWAP[j]) for n in range(count)])  9.03 us
    ppermute x1, starting transfers between devices, shards(): sibling = lax.ppermute(level, 'core', [(0, 1), (1, 0)])  8.92 us
    all_to_all x1, waiting for transfers between devices, shards(): parts = lax.all_to_all(part.reshape(members, columns, height), group, 0, 0)  3.93 us
    all_to_all x1, starting transfers between devices, shards(): parts = lax.all_to_all(part.reshape(members, columns, height), group, 0, 0)  3.38 us
  transfers between devices with their start and end apart: 14, of which 6 were waited for; matrix products, arithmetic and copies ran while one was open for 0% of the time, Pallas kernels for 9%

profile of v7, /device:TPU:1, one launch (start us, length us, event | category | flops | bytes accessed | tf_op | source)
XLA Modules:
  0.0 98.5 jit_solution(17134387228633817073)
XLA Ops:
  1.3 4.5 %shard_map.95 = (f32[896,128]{1,0:T(8,128)}, bf16[272,384]{1,0:T(8,128)(2,1)}, f32[256,256]{1,0:T(8,128)}) custom-call(f32[256,256]{1,0:T(8,128)} %bitcast.17, f32[256,128]{1,0:T(8,128)} %bitcast.20, bf16[384,256]{1,0:T(8,128)(2,1)} %bitcast.19, s32[1,1]{1,0:T(1,128)S(6)} %copy.10.tiles_hbm, bf16[384,384]{1,0:T(8,128)(2,1)} %bitcast.13, ...), custom_call_target="tpu_custom_call" | custom-call | tf_op jit(solution)/shard_map/pallas_call | solution.py:303
  5.8 8.9 %collective-permute-start = (f32[896,128]{1,0:T(8,128)}, f32[896,128]{1,0:T(8,128)S(1)}, u32[]{:S(2)}, u32[]{:S(2)}) collective-permute-start(f32[896,128]{1,0:T(8,128)} %get-tuple-element.35.level_ref), channel_id=1, source_target_pairs={{0,4},{4,0},{1,5},{5,1},{2,6},{6,2},{3,7},{7,3},{8,12},{12,8},{9,1... | collective-permute-start | bytes 1376264 | tf_op jit(solution)/shard_map/ppermute | solution.py:344
  14.7 3.4 %all-to-all-start = ((f32[8,32,256]{2,1,0:T(8,128)}), f32[8,32,256]{2,1,0:T(8,128)S(1)}, u32[]{:S(2)}, u32[]{:S(2)}) async-start(f32[8,32,256]{2,1,0:T(8,128)} %bitcast.16), calls=%async_computation | async-start | bytes 524288 | tf_op jit(solution)/shard_map/all_to_all | solution.py:349
  18.2 0.6 shard_map.96
  18.8 1.9 %collective-permute-start.2 = (f32[256,128]{1,0:T(8,128)S(1)}, f32[256,128]{1,0:T(8,128)S(1)}, u32[]{:S(2)}, u32[]{:S(2)}) collective-permute-start(f32[256,128]{1,0:T(8,128)S(1)} %get-tuple-element.38.own_ref), channel_id=1, source_target_pairs={{0,8},{8,0},{16,24},{24,16},{32,40},{40,32},{48,56},{56,48},{64,72... | collective-permute-start | bytes 393224 | tf_op jit(solution)/shard_map/ppermute | solution.py:30
  20.7 3.9 %all-to-all-done.parts_ref.refs_0_ = f32[8,32,256]{2,1,0:T(8,128)S(1)} async-done(((f32[8,32,256]{2,1,0:T(8,128)}), f32[8,32,256]{2,1,0:T(8,128)S(1)}, u32[]{:S(2)}, u32[]{:S(2)}) %all-to-all-start) | async-done | bytes 262176 | tf_op jit(solution)/shard_map/all_to_all | solution.py:349
  24.6 0.5 shard_map.97
  25.1 1.9 %collective-permute-start.1 = (f32[32,256]{1,0:T(8,128)S(1)}, f32[32,256]{1,0:T(8,128)S(1)}, u32[]{:S(2)}, u32[]{:S(2)}) collective-permute-start(f32[32,256]{1,0:T(8,128)S(1)} %get-tuple-element.37.own_ref.refs_0_), channel_id=1, source_target_pairs={{0,8},{8,0},{16,24},{24,16},{32,40},{40,32},{48,56},{56,48},{64,72... | collective-permute-start | bytes 98312 | tf_op jit(solution)/shard_map/ppermute | solution.py:30
  27.1 0.6 shard_map.98
  27.6 1.9 %collective-permute-start.4 = (f32[256,128]{1,0:T(8,128)S(1)}, f32[256,128]{1,0:T(8,128)S(1)}, u32[]{:S(2)}, u32[]{:S(2)}) collective-permute-start(f32[256,128]{1,0:T(8,128)S(1)} %get-tuple-element.40.own_ref), channel_id=1, source_target_pairs={{0,24},{8,16},{16,8},{24,0},{32,56},{40,48},{48,40},{56,32},{64,88... | collective-permute-start | bytes 393224 | tf_op jit(solution)/shard_map/ppermute | solution.py:30
  30.0 4.4 %collective-permute-start.3 = (f32[32,256]{1,0:T(8,128)S(1)}, f32[32,256]{1,0:T(8,128)S(1)}, u32[]{:S(2)}, u32[]{:S(2)}) collective-permute-start(f32[32,256]{1,0:T(8,128)S(1)} %shard_map.99.own_ref.refs_0_.refs_1_), channel_id=1, source_target_pairs={{0,24},{8,16},{16,8},{24,0},{32,56},{40,48},{48,40},{56,32},{64,88... | collective-permute-start | bytes 98312 | tf_op jit(solution)/shard_map/ppermute | solution.py:30
  34.4 1.0 %collective-permute-done.4.other_ref = f32[256,128]{1,0:T(8,128)S(1)} collective-permute-done((f32[256,128]{1,0:T(8,128)S(1)}, f32[256,128]{1,0:T(8,128)S(1)}, u32[]{:S(2)}, u32[]{:S(2)}) %collective-permute-start.4) | collective-permute-done | bytes 131104 | tf_op jit(solution)/shard_map/ppermute | solution.py:30
  35.5 0.6 shard_map.100
  36.0 1.9 %collective-permute-start.6 = (f32[256,128]{1,0:T(8,128)S(1)}, f32[256,128]{1,0:T(8,128)S(1)}, u32[]{:S(2)}, u32[]{:S(2)}) collective-permute-start(f32[256,128]{1,0:T(8,128)S(1)} %get-tuple-element.42.own_ref), channel_id=1, source_target_pairs={{0,32},{8,40},{16,48},{24,56},{32,0},{40,8},{48,16},{56,24},{64,96... | collective-permute-start | bytes 393224 | tf_op jit(solution)/shard_map/ppermute | solution.py:30
  38.0 0.3 shard_map.101.own_ref.refs_2_
  38.2 3.4 %collective-permute-start.5 = (f32[32,256]{1,0:T(8,128)S(1)}, f32[32,256]{1,0:T(8,128)S(1)}, u32[]{:S(2)}, u32[]{:S(2)}) collective-permute-start(f32[32,256]{1,0:T(8,128)S(1)} %shard_map.101.own_ref.refs_2_), channel_id=1, source_target_pairs={{0,32},{8,40},{16,48},{24,56},{32,0},{40,8},{48,16},{56,24},{64,96... | collective-permute-start | bytes 98312 | tf_op jit(solution)/shard_map/ppermute | solution.py:30
  41.7 0.7 shard_map.102
  42.4 1.9 %collective-permute-start.8 = (f32[200,128]{1,0:T(8,128)S(1)}, f32[200,128]{1,0:T(8,128)S(1)}, u32[]{:S(2)}, u32[]{:S(2)}) collective-permute-start(f32[200,128]{1,0:T(8,128)S(1)} %get-tuple-element.45), channel_id=1, source_target_pairs={{0,64},{8,72},{16,80},{24,88},{32,96},{40,104},{48,112},{56,120},{... | collective-permute-start | bytes 307208 | tf_op jit(solution)/shard_map/ppermute | solution.py:30
  44.6 4.3 %collective-permute-start.7 = (f32[32,256]{1,0:T(8,128)S(1)}, f32[32,256]{1,0:T(8,128)S(1)}, u32[]{:S(2)}, u32[]{:S(2)}) collective-permute-start(f32[32,256]{1,0:T(8,128)S(1)} %shard_map.103.own_ref.refs_0_.refs_3_), channel_id=1, source_target_pairs={{0,64},{8,72},{16,80},{24,88},{32,96},{40,104},{48,112},{56,120},{... | collective-permute-start | bytes 98312 | tf_op jit(solution)/shard_map/ppermute | solution.py:30
  48.9 0.7 collective-permute-done.8.other_ref
  49.5 0.7 shard_map.104
  50.3 5.6 %collective-permute-start.10 = (f32[200,128]{1,0:T(8,128)S(1)}, f32[200,128]{1,0:T(8,128)S(1)}, u32[]{:S(2)}, u32[]{:S(2)}) collective-permute-start(f32[200,128]{1,0:T(8,128)S(1)} %get-tuple-element.48), channel_id=1, source_target_pairs={{0,128},{8,136},{16,144},{24,152},{32,160},{40,168},{48,176},{56,1... | collective-permute-start | bytes 307208 | tf_op jit(solution)/shard_map/ppermute | solution.py:30
  56.2 4.1 %collective-permute-start.9 = (f32[32,256]{1,0:T(8,128)S(1)}, f32[32,256]{1,0:T(8,128)S(1)}, u32[]{:S(2)}, u32[]{:S(2)}) collective-permute-start(f32[32,256]{1,0:T(8,128)S(1)} %shard_map.105.own_ref.refs_4_), channel_id=1, source_target_pairs={{0,128},{8,136},{16,144},{24,152},{32,160},{40,168},{48,176},{56,1... | collective-permute-start | bytes 98312 | tf_op jit(solution)/shard_map/ppermute | solution.py:30
  60.3 6.9 %collective-permute-done.10.other_ref = f32[200,128]{1,0:T(8,128)S(1)} collective-permute-done((f32[200,128]{1,0:T(8,128)S(1)}, f32[200,128]{1,0:T(8,128)S(1)}, u32[]{:S(2)}, u32[]{:S(2)}) %collective-permute-start.10) | collective-permute-done | bytes 102432 | tf_op jit(solution)/shard_map/ppermute | solution.py:30
  67.3 0.7 shard_map.106
  68.0 2.0 %collective-permute-start.12 = (f32[72,128]{1,0:T(8,128)S(1)}, f32[72,128]{1,0:T(8,128)S(1)}, u32[]{:S(2)}, u32[]{:S(2)}) collective-permute-start(f32[72,128]{1,0:T(8,128)S(1)} %get-tuple-element.50), channel_id=1, source_target_pairs={{0,384},{8,392},{16,400},{24,408},{32,416},{40,424},{48,432},{56,4... | collective-permute-start | bytes 110600 | tf_op jit(solution)/shard_map/ppermute | solution.py:30
  70.0 0.3 shard_map.107.sent_ref
  70.3 7.2 %collective-permute-start.11 = (f32[32,256]{1,0:T(8,128)S(1)}, f32[32,256]{1,0:T(8,128)S(1)}, u32[]{:S(2)}, u32[]{:S(2)}) collective-permute-start(f32[32,256]{1,0:T(8,128)S(1)} %shard_map.107.sent_ref), channel_id=1, source_target_pairs={{0,384},{8,392},{16,400},{24,408},{32,416},{40,424},{48,432},{56,4... | collective-permute-start | bytes 98312 | tf_op jit(solution)/shard_map/ppermute | solution.py:30
  77.5 3.6 %shard_map.108.descent_ref = f32[160,512]{1,0:T(8,128)S(1)} custom-call(s32[8,128]{1,0:T(8,128)S(1)} %iota.7.bits_ref, f32[896,128]{1,0:T(8,128)S(1)} %copy-done, f32[896,128]{1,0:T(8,128)S(1)} %collective-permute-done.sibling_ref, f32[256,256]{1,0:T(8,128)S(1)} %get-tuple-element.36.weights_ref, f32[2,32,256]{2,1,0:T(8,128)S(1)} %get-tuple-element.51.owns_ref, ...), custom_call_target="tpu_custom_call" | custom-call | tf_op jit(solution)/shard_map/pallas_call | solution.py:303
  81.1 0.6 shard_map.109
  81.7 15.3 %all_to_all.10 = f32[8,32,256]{2,1,0:T(8,128)S(1)} all-to-all(f32[8,32,256]{2,1,0:T(8,128)S(1)} %shard_map.109), channel_id=1, replica_groups=mesh['pair'=64,'core'=2,'rep'=4] {'core','rep'}, dimensions={0} | all-to-all | bytes 524288 | tf_op jit(solution)/shard_map/all_to_all | solution.py:403
  97.0 1.5 %shard_map.110 = (f32[256,256]{1,0:T(8,128)}, f32[384,256]{1,0:T(8,128)}) custom-call(f32[256,256]{1,0:T(8,128)S(1)} %bitcast.15, bf16[272,384]{1,0:T(8,128)(2,1)S(1)} %copy-done.3, bf16[384,384]{1,0:T(8,128)(2,1)S(1)} %bitcast.14, bf16[768,384]{1,0:T(8,128)(2,1)S(1)} %bitcast.12), custom_call_target="tpu_custom_call" | custom-call | tf_op jit(solution)/shard_map/pallas_call | solution.py:303
  (23 shorter events, 1.2 us)
Async XLA Ops:
  5.8 12.4 %copy-start = (f32[896,128]{1,0:T(8,128)S(1)}, f32[896,128]{1,0:T(8,128)}, u32[]{:S(2)}) copy-start(f32[896,128]{1,0:T(8,128)} %get-tuple-element.35.level_ref) | copy-start | bytes 1376260
  5.8 12.3 %collective-permute-start = (f32[896,128]{1,0:T(8,128)}, f32[896,128]{1,0:T(8,128)S(1)}, u32[]{:S(2)}, u32[]{:S(2)}) collective-permute-start(f32[896,128]{1,0:T(8,128)} %get-tuple-element.35.level_ref), channel_id=1, source_target_pairs={{0,4},{4,0},{1,5},{5,1},{2,6},{6,2},{3,7},{7,3},{8,12},{12,8},{9,1... | collective-permute-start | bytes 1376264 | tf_op jit(solution)/shard_map/ppermute | solution.py:344
  14.7 9.9 %all-to-all-start = ((f32[8,32,256]{2,1,0:T(8,128)}), f32[8,32,256]{2,1,0:T(8,128)S(1)}, u32[]{:S(2)}, u32[]{:S(2)}) async-start(f32[8,32,256]{2,1,0:T(8,128)} %bitcast.16), calls=%async_computation | async-start | bytes 524288 | tf_op jit(solution)/shard_map/all_to_all | solution.py:349
  18.8 8.3 %collective-permute-start.2 = (f32[256,128]{1,0:T(8,128)S(1)}, f32[256,128]{1,0:T(8,128)S(1)}, u32[]{:S(2)}, u32[]{:S(2)}) collective-permute-start(f32[256,128]{1,0:T(8,128)S(1)} %get-tuple-element.38.own_ref), channel_id=1, source_target_pairs={{0,8},{8,0},{16,24},{24,16},{32,40},{40,32},{48,56},{56,48},{64,72... | collective-permute-start | bytes 393224 | tf_op jit(solution)/shard_map/ppermute | solution.py:30
  25.1 4.7 %collective-permute-start.1 = (f32[32,256]{1,0:T(8,128)S(1)}, f32[32,256]{1,0:T(8,128)S(1)}, u32[]{:S(2)}, u32[]{:S(2)}) collective-permute-start(f32[32,256]{1,0:T(8,128)S(1)} %get-tuple-element.37.own_ref.refs_0_), channel_id=1, source_target_pairs={{0,8},{8,0},{16,24},{24,16},{32,40},{40,32},{48,56},{56,48},{64,72... | collective-permute-start | bytes 98312 | tf_op jit(solution)/shard_map/ppermute | solution.py:30
  27.6 7.8 %collective-permute-start.4 = (f32[256,128]{1,0:T(8,128)S(1)}, f32[256,128]{1,0:T(8,128)S(1)}, u32[]{:S(2)}, u32[]{:S(2)}) collective-permute-start(f32[256,128]{1,0:T(8,128)S(1)} %get-tuple-element.40.own_ref), channel_id=1, source_target_pairs={{0,24},{8,16},{16,8},{24,0},{32,56},{40,48},{48,40},{56,32},{64,88... | collective-permute-start | bytes 393224 | tf_op jit(solution)/shard_map/ppermute | solution.py:30
  30.0 7.9 %collective-permute-start.3 = (f32[32,256]{1,0:T(8,128)S(1)}, f32[32,256]{1,0:T(8,128)S(1)}, u32[]{:S(2)}, u32[]{:S(2)}) collective-permute-start(f32[32,256]{1,0:T(8,128)S(1)} %shard_map.99.own_ref.refs_0_.refs_1_), channel_id=1, source_target_pairs={{0,24},{8,16},{16,8},{24,0},{32,56},{40,48},{48,40},{56,32},{64,88... | collective-permute-start | bytes 98312 | tf_op jit(solution)/shard_map/ppermute | solution.py:30
  36.0 5.7 %collective-permute-start.6 = (f32[256,128]{1,0:T(8,128)S(1)}, f32[256,128]{1,0:T(8,128)S(1)}, u32[]{:S(2)}, u32[]{:S(2)}) collective-permute-start(f32[256,128]{1,0:T(8,128)S(1)} %get-tuple-element.42.own_ref), channel_id=1, source_target_pairs={{0,32},{8,40},{16,48},{24,56},{32,0},{40,8},{48,16},{56,24},{64,96... | collective-permute-start | bytes 393224 | tf_op jit(solution)/shard_map/ppermute | solution.py:30
  38.2 6.1 %collective-permute-start.5 = (f32[32,256]{1,0:T(8,128)S(1)}, f32[32,256]{1,0:T(8,128)S(1)}, u32[]{:S(2)}, u32[]{:S(2)}) collective-permute-start(f32[32,256]{1,0:T(8,128)S(1)} %shard_map.101.own_ref.refs_2_), channel_id=1, source_target_pairs={{0,32},{8,40},{16,48},{24,56},{32,0},{40,8},{48,16},{56,24},{64,96... | collective-permute-start | bytes 98312 | tf_op jit(solution)/shard_map/ppermute | solution.py:30
  42.4 7.1 %collective-permute-start.8 = (f32[200,128]{1,0:T(8,128)S(1)}, f32[200,128]{1,0:T(8,128)S(1)}, u32[]{:S(2)}, u32[]{:S(2)}) collective-permute-start(f32[200,128]{1,0:T(8,128)S(1)} %get-tuple-element.45), channel_id=1, source_target_pairs={{0,64},{8,72},{16,80},{24,88},{32,96},{40,104},{48,112},{56,120},{... | collective-permute-start | bytes 307208 | tf_op jit(solution)/shard_map/ppermute | solution.py:30
  44.6 11.3 %collective-permute-start.7 = (f32[32,256]{1,0:T(8,128)S(1)}, f32[32,256]{1,0:T(8,128)S(1)}, u32[]{:S(2)}, u32[]{:S(2)}) collective-permute-start(f32[32,256]{1,0:T(8,128)S(1)} %shard_map.103.own_ref.refs_0_.refs_3_), channel_id=1, source_target_pairs={{0,64},{8,72},{16,80},{24,88},{32,96},{40,104},{48,112},{56,120},{... | collective-permute-start | bytes 98312 | tf_op jit(solution)/shard_map/ppermute | solution.py:30
  50.3 17.0 %collective-permute-start.10 = (f32[200,128]{1,0:T(8,128)S(1)}, f32[200,128]{1,0:T(8,128)S(1)}, u32[]{:S(2)}, u32[]{:S(2)}) collective-permute-start(f32[200,128]{1,0:T(8,128)S(1)} %get-tuple-element.48), channel_id=1, source_target_pairs={{0,128},{8,136},{16,144},{24,152},{32,160},{40,168},{48,176},{56,1... | collective-permute-start | bytes 307208 | tf_op jit(solution)/shard_map/ppermute | solution.py:30
  56.2 13.8 %collective-permute-start.9 = (f32[32,256]{1,0:T(8,128)S(1)}, f32[32,256]{1,0:T(8,128)S(1)}, u32[]{:S(2)}, u32[]{:S(2)}) collective-permute-start(f32[32,256]{1,0:T(8,128)S(1)} %shard_map.105.own_ref.refs_4_), channel_id=1, source_target_pairs={{0,128},{8,136},{16,144},{24,152},{32,160},{40,168},{48,176},{56,1... | collective-permute-start | bytes 98312 | tf_op jit(solution)/shard_map/ppermute | solution.py:30
  68.0 13.1 %collective-permute-start.12 = (f32[72,128]{1,0:T(8,128)S(1)}, f32[72,128]{1,0:T(8,128)S(1)}, u32[]{:S(2)}, u32[]{:S(2)}) collective-permute-start(f32[72,128]{1,0:T(8,128)S(1)} %get-tuple-element.50), channel_id=1, source_target_pairs={{0,384},{8,392},{16,400},{24,408},{32,416},{40,424},{48,432},{56,4... | collective-permute-start | bytes 110600 | tf_op jit(solution)/shard_map/ppermute | solution.py:30
  70.3 10.8 %collective-permute-start.11 = (f32[32,256]{1,0:T(8,128)S(1)}, f32[32,256]{1,0:T(8,128)S(1)}, u32[]{:S(2)}, u32[]{:S(2)}) collective-permute-start(f32[32,256]{1,0:T(8,128)S(1)} %shard_map.107.sent_ref), channel_id=1, source_target_pairs={{0,384},{8,392},{16,400},{24,408},{32,416},{40,424},{48,432},{56,4... | collective-permute-start | bytes 98312 | tf_op jit(solution)/shard_map/ppermute | solution.py:30
  81.1 15.9 %copy-start.1 = (bf16[1,1,768,384]{3,2,1,0:T(8,128)(2,1)S(1)}, bf16[1,1,768,384]{3,2,1,0:T(8,128)(2,1)}, u32[]{:S(2)}) copy-start(bf16[1,1,768,384]{3,2,1,0:T(8,128)(2,1)} %param.11) | copy-start | bytes 1769476
  81.7 15.3 %copy-start.2 = (bf16[1,1,384,384]{3,2,1,0:T(8,128)(2,1)S(1)}, bf16[1,1,384,384]{3,2,1,0:T(8,128)(2,1)}, u32[]{:S(2)}) copy-start(bf16[1,1,384,384]{3,2,1,0:T(8,128)(2,1)} %param.8) | copy-start | bytes 884740
  81.7 15.3 %copy-start.3 = (bf16[272,384]{1,0:T(8,128)(2,1)S(1)}, bf16[272,384]{1,0:T(8,128)(2,1)}, u32[]{:S(2)}) copy-start(bf16[272,384]{1,0:T(8,128)(2,1)} %get-tuple-element.63.forward_ref) | copy-start | bytes 626692

commit v8 on v7

--- a/solution.py
+++ b/solution.py
@@ -14,10 +14,9 @@
 SWAP = (1, 3, 4, 8, 16, 48)
 
 
-PACKED = 3
-MAPS_WEIGHT = (3, 10, 0, 30, 30)
-STATE_WEIGHT = (30, 10, 30, 10, 30)
-BEHIND = (True, True, False, True)
+APART = 2
+MAPS_WEIGHT = (3, 10)
+STATE_WEIGHT = (30, 10)
 
 
 def dot(a, b, dims=((1,), (0,)), precision=HIGHEST):
@@ -69,49 +68,85 @@
     return half + half.T
 
 
-def join_maps(right, first, second, maps_ref, weights_ref, step_ref=None):
+def join_maps(first, second):
     early = first[:TILE]
     product = dot(second, early)
     turn = product[TILE:]
-    flipped = early.T
-    answer = first[TILE:] + dot(flipped, turn)
-    if maps_ref is not None:
-        maps_ref[:TILE] = product[:TILE]
-        maps_ref[TILE:] = answer
+    answer = first[TILE:] + dot(early.T, turn)
+    return jnp.concatenate([product[:TILE], answer], axis=0), turn
+
+
+def fill_weights(first, second, turn, weights_ref):
     weights_ref[:TILE, :TILE] = second[:TILE].T
     weights_ref[:TILE, TILE:] = turn
     weights_ref[TILE:, :TILE] = jnp.zeros_like(turn)
-    weights_ref[TILE:, TILE:] = early
-    if step_ref is not None:
-        step_ref[:TILE] = jnp.where(right, flipped, turn.T)
-        step_ref[TILE:] = jnp.where(right, 0.0, second[:TILE])
-    return product[:TILE], answer
+    weights_ref[TILE:, TILE:] = first[:TILE]
+
+
+def fill_step(right, first, second, turn, step_ref):
+    step_ref[:TILE] = jnp.where(right, first[:TILE], turn).T
+    step_ref[TILE:] = jnp.where(right, 0.0, second[:TILE])
 
 
 def pair_kernel(bits_ref, level_ref, sibling_ref, maps_ref, weights_ref):
     odd = pick(bits_ref, 0)
     own, other = level_ref[TILE : 3 * TILE], sibling_ref[TILE : 3 * TILE]
-    join_maps(
-        odd, jnp.where(odd, other, own), jnp.where(odd, own, other), maps_ref, weights_ref
-    )
+    first, second = jnp.where(odd, other, own), jnp.where(odd, own, other)
+    maps_ref[...], turn = join_maps(first, second)
+    fill_weights(first, second, turn, weights_ref)
 
 
 def maps_kernel(j, later, bits_ref, own_ref, other_ref, *refs):
-    weights_ref, step_ref, answer_ref, *rest = refs[later:]
+    maps_ref, weights_ref, step_ref = refs[later:]
     right = pick(bits_ref, j + 1)
     own, other = own_ref[...], other_ref[...]
-    if j >= PACKED:
-        other = jnp.concatenate([other[:TILE], unpack(other[TILE:])], axis=0)
-    answer_ref[...] = other[TILE:]
-    ahead, answer = join_maps(
-        right, jnp.where(right, other, own), jnp.where(right, own, other),
-        rest[0] if j + 2 < len(SWAP) else None, weights_ref, step_ref,
-    )
-    if j + 1 >= PACKED:
-        packed = pack(answer)
-        if j + 2 < len(SWAP):
-            packed = jnp.concatenate([ahead, packed], axis=0)
-        rest[-1][...] = packed
+    first, second = jnp.where(right, other, own), jnp.where(right, own, other)
+    maps_ref[...], turn = join_maps(first, second)
+    fill_weights(first, second, turn, weights_ref)
+    fill_step(right, first, second, turn, step_ref)
+
+
+def message(maps, state, last):
+    parts = [pack(maps[TILE:]), state[:, :TILE], state[:, TILE:]]
+    return jnp.concatenate(parts if last else [maps[:TILE]] + parts, axis=0)
+
+
+def push_of(right, own, other, answer):
+    return jnp.where(
+        right, other[:, :TILE], other[:, TILE:] + dot(own[:, :TILE], answer)
+    )
+
+
+def round_kernel(j, last, bits_ref, maps_ref, state_ref, other_ref, *refs):
+    step_ref, push_ref, message_ref, next_state_ref, *next_maps_ref = refs
+    right = pick(bits_ref, j + 1)
+    columns = state_ref.shape[0]
+    offset = TILE + HALF + 8
+    own = maps_ref[...]
+    answer = unpack(other_ref[TILE:offset])
+    other = jnp.concatenate([other_ref[:TILE], answer], axis=0)
+    own_state = state_ref[...]
+    other_state = jnp.concatenate(
+        [other_ref[offset : offset + columns], other_ref[offset + columns :]], axis=1
+    )
+    first, second = jnp.where(right, other, own), jnp.where(right, own, other)
+    maps, turn = join_maps(first, second)
+    early = jnp.where(right, other_state, own_state)
+    late = jnp.where(right, own_state, other_state)
+    entry = early[:, :TILE]
+    state = jnp.concatenate(
+        [
+            late[:, :TILE] + dot(entry, second[:TILE], ((1,), (1,))),
+            early[:, TILE:] + dot(late[:, TILE:], first[:TILE]) + dot(entry, turn),
+        ],
+        axis=1,
+    )
+    message_ref[...] = message(maps, state, last)
+    next_state_ref[...] = state
+    if not last:
+        next_maps_ref[0][...] = maps
+    fill_step(right, first, second, turn, step_ref)
+    push_ref[...] = push_of(right, own_state, other_state, answer)
 
 
 def join_state(first, second, weights):
@@ -139,30 +174,26 @@
     state_ref[...] = join_state(states[0], states[1], weights_ref[...])
 
 
-def state_kernel(j, bits_ref, own_ref, other_ref, weights_ref, *refs):
-    right = pick(bits_ref, j)
+def state_kernel(j, bits_ref, own_ref, other_ref, answer_ref, weights_ref, *refs):
+    right = pick(bits_ref, j + 1)
     own, other = own_ref[...], other_ref[...]
-    refs[-1][...] = join_state(
+    state = join_state(
         jnp.where(right, other, own), jnp.where(right, own, other), weights_ref[...]
     )
+    if len(refs) == 2:
+        state_ref, push_ref = refs
+    else:
+        maps_ref, state_ref, push_ref, message_ref = refs
+        message_ref[...] = message(maps_ref[...], state, False)
+    state_ref[...] = state
+    push_ref[...] = push_of(right, own, other, answer_ref[TILE:])
 
 
 def descend_kernel(rounds, bits_ref, level_ref, sibling_ref, weights_ref, owns_ref, states_ref, *refs):
-    sent, got = refs[:rounds], refs[rounds : 2 * rounds]
-    answers, steps = refs[2 * rounds : 3 * rounds], refs[3 * rounds : 4 * rounds]
+    pushes, steps = refs[:rounds], refs[rounds : 2 * rounds]
     descent_ref = refs[-1]
     odd = pick(bits_ref, 0)
     height = owns_ref.shape[2]
-    pushes = []
-    for j in range(rounds):
-        other = got[j][...]
-        pushes.append(
-            jnp.where(
-                pick(bits_ref, j + 1),
-                other[:, :TILE],
-                other[:, TILE:] + dot(sent[j][:, :TILE], answers[j][...]),
-            )
-        )
 
     def under(constant):
         return jnp.concatenate([jnp.zeros((TILE, constant.shape[1]), jnp.float32), constant], axis=0)
@@ -174,7 +205,7 @@
     before, after = jnp.where(right, basis, 0.0), jnp.where(right, 0.0, basis)
     for j in reversed(range(rounds)):
         right = pick(bits_ref, j + 1)
-        push = under(pushes[j]) + dot(jnp.concatenate([before, after], axis=1), steps[j][...])
+        push = under(pushes[j][...]) + dot(jnp.concatenate([before, after], axis=1), steps[j][...])
         before, after = jnp.where(right, push, before), jnp.where(right, after, push)
     own, other = level_ref[...], sibling_ref[...]
     levels = (jnp.where(odd, other, own), jnp.where(odd, own, other))
@@ -201,13 +232,12 @@
         )
 
 
-def finish_kernel(rounds, bits_ref, sent_ref, got_ref, answer_ref, descent_ref, shares_ref):
-    other = got_ref[...]
-    push = jnp.where(
-        pick(bits_ref, rounds),
-        other[:, :TILE],
-        other[:, TILE:] + dot(sent_ref[:, :TILE], unpack(answer_ref[...])),
-    )
+def finish_kernel(rounds, bits_ref, state_ref, other_ref, descent_ref, shares_ref):
+    columns, offset = state_ref.shape[0], HALF + 8
+    other = jnp.concatenate(
+        [other_ref[offset : offset + columns], other_ref[offset + columns :]], axis=1
+    )
+    push = push_of(pick(bits_ref, rounds), state_ref[...], other, unpack(other_ref[:offset]))
     both = descent_ref[TILE:] + dot(push, descent_ref[:TILE])
     reps, height = shares_ref.shape[0] // 2, shares_ref.shape[2]
     for c in range(2):
@@ -347,58 +377,64 @@
     )
     columns = width // members
     parts = lax.all_to_all(part.reshape(members, columns, height), group, 0, 0)
-    answers, weights, steps = [], [], []
-
-    def advance_maps(j, maps, message, *later):
-        other = swap(message, j, count)
-        shapes = [
-            f32(2 * TILE, 2 * TILE), f32(2 * TILE, TILE), f32(TILE, TILE)
-        ]
-        if j + 2 < rounds:
-            shapes.append(f32(2 * TILE, TILE))
-        if j + 1 >= PACKED:
-            shapes.append(f32(HALF + 8 + (TILE if j + 2 < rounds else 0), TILE))
-        weight, step, answer, *rest = local_call(
+    pushes, steps = [], []
+    square = 2 * TILE
+
+    def advance_maps(j, maps, *later):
+        other = swap(maps, j, count)
+        maps, weights, step = local_call(
             functools.partial(maps_kernel, j, len(later)),
-            shapes, bits, maps, other, later=later, weight=MAPS_WEIGHT[j],
-        )
-        weights.append(weight)
+            [f32(square, TILE), f32(square, square), f32(square, TILE)],
+            bits, maps, other, later=later, weight=MAPS_WEIGHT[j],
+        )
         steps.append(step)
-        answers.append(answer)
-        return rest[0], rest[-1]
-
-    maps, message = advance_maps(0, maps, maps, parts)
+        return other, maps, weights
+
+    answer, maps, weights = advance_maps(0, maps, parts)
     owns, states, state = local_call(
         start_kernel,
-        [f32(2, columns, height), f32(2, columns, 2 * TILE), f32(columns, 2 * TILE)],
+        [f32(2, columns, height), f32(2, columns, square), f32(columns, square)],
         bits, parts, level, sibling, pair_weights,
     )
-    sent, got = [], []
-    for j in range(rounds):
-        sent.append(state)
-        got.append(swap(state, j, count))
-        if j < rounds - 2:
-            later = (state,) if BEHIND[j] else ()
-            maps, message = advance_maps(j + 1, maps, message, *later)
-        elif j == rounds - 2:
-            answers.append(swap(message, j + 1, count))
-        if j < rounds - 1:
-            (state,) = local_call(
-                functools.partial(state_kernel, j + 1),
-                [f32(columns, 2 * TILE)],
-                bits, state, got[j], weights[j],
-                weight=STATE_WEIGHT[j],
-            )
+    whole = TILE + HALF + 8 + 2 * columns
+    for j in range(APART):
+        other = swap(state, j, count)
+        shapes = [f32(columns, square), f32(columns, TILE)]
+        operands = [bits, state, other, answer, weights]
+        if j + 1 < APART:
+            answer, maps, weights = advance_maps(j + 1, maps, state)
+        else:
+            operands.append(maps)
+            shapes.append(f32(whole, TILE))
+        state, push, *packed = local_call(
+            functools.partial(state_kernel, j), shapes, *operands, weight=STATE_WEIGHT[j]
+        )
+        pushes.append(push)
+    packed = packed[0]
+    for j in range(APART, rounds - 1):
+        last = j == rounds - 2
+        shapes = [
+            f32(square, TILE), f32(columns, TILE), f32(whole - last * TILE, TILE),
+            f32(columns, square),
+        ]
+        step, push, packed, state, *rest = local_call(
+            functools.partial(round_kernel, j, last),
+            shapes if last else shapes + [f32(square, TILE)],
+            bits, maps, state, swap(packed, j, count),
+        )
+        maps = None if last else rest[0]
+        steps.append(step)
+        pushes.append(push)
+    got = swap(packed, rounds - 1, count)
     (descent,) = local_call(
         functools.partial(descend_kernel, rounds - 1),
         [f32(TILE + columns, 2 * height)],
-        bits, level, sibling, pair_weights, owns, states,
-        *sent[:-1], *got[:-1], *answers[:-1], *steps,
+        bits, level, sibling, pair_weights, owns, states, *pushes, *steps,
     )
     (shares,) = local_call(
         functools.partial(finish_kernel, rounds),
         [f32(members, columns, height)],
-        bits, sent[-1], got[-1], answers[-1], descent,
+        bits, state, got, descent,
     )
     spread = lax.all_to_all(shares, group, 0, 0)
     solution, final = local_call(

time: 99.2 us -> 96.5 us (0.973)
  waiting for transfers between devices: 13 us -> 26.7 us
  starting transfers between devices: 52.8 us -> 41.6 us
  blocking collectives: 15.3 us -> 10.3 us
    ppermute x12 -> x8, waiting for transfers between devices: 9.03 us -> 22.7 us  [swap(): return lax.ppermute(value, 'pair', [(n, n ^ SWAP[j]) for n in range(count)])]
    ppermute x12 -> x8, starting transfers between devices: 40.5 us -> 29.3 us  [swap(): return lax.ppermute(value, 'pair', [(n, n ^ SWAP[j]) for n in range(count)])]
    all_to_all x1, blocking collectives: 15.3 us -> 10.3 us  [shards(): spread = lax.all_to_all(shares, group, 0, 0)]
    pallas_call x16 -> x13, Pallas kernels: 15.7 us -> 15.8 us  [local_call(): pl.pallas_call(kernel, out_shape=out_shape, in_specs=[vmem] * len(operand...]
  transfers between devices with their start and end apart: 14 -> 10, of which waited for: 6 -> 7; matrix products, arithmetic and copies ran while one was open for 0% -> 0% of each run, Pallas kernels for 9% -> 6%
where the time goes in v8:
time: 96.5 us; the launch traced here: 96 us
  starting transfers between devices  41.6 us (43%)
  waiting for transfers between devices  26.7 us (28%)
  Pallas kernels  15.8 us (16%)
  blocking collectives  10.3 us (11%)
  between operations  1.5 us (2%)
    ppermute x8, starting transfers between devices, swap(): return lax.ppermute(value, 'pair', [(n, n ^ SWAP[j]) for n in range(count)])  29.3 us
    ppermute x8, waiting for transfers between devices, swap(): return lax.ppermute(value, 'pair', [(n, n ^ SWAP[j]) for n in range(count)])  22.7 us
    pallas_call x13, Pallas kernels, local_call(): pl.pallas_call(kernel, out_shape=out_shape, in_specs=[vmem] * len(operand...  15.8 us
    all_to_all x1, blocking collectives, shards(): spread = lax.all_to_all(shares, group, 0, 0)  10.3 us
    ppermute x1, starting transfers between devices, shards(): sibling = lax.ppermute(level, 'core', [(0, 1), (1, 0)])  8.92 us
    all_to_all x1, waiting for transfers between devices, shards(): parts = lax.all_to_all(part.reshape(members, columns, height), group, 0, 0)  3.93 us
    all_to_all x1, starting transfers between devices, shards(): parts = lax.all_to_all(part.reshape(members, columns, height), group, 0, 0)  3.38 us
  transfers between devices with their start and end apart: 10, of which 7 were waited for; matrix products, arithmetic and copies ran while one was open for 0% of the time, Pallas kernels for 6%

profile of v8, /device:TPU:1, one launch (start us, length us, event | category | flops | bytes accessed | tf_op | source)
XLA Modules:
  0.0 96.0 jit_solution(5441841845562235882)
XLA Ops:
  1.3 4.5 %shard_map.95 = (f32[896,128]{1,0:T(8,128)}, bf16[272,384]{1,0:T(8,128)(2,1)}, f32[256,256]{1,0:T(8,128)}) custom-call(f32[256,256]{1,0:T(8,128)} %bitcast.17, f32[256,128]{1,0:T(8,128)} %bitcast.20, bf16[384,256]{1,0:T(8,128)(2,1)} %bitcast.19, s32[1,1]{1,0:T(1,128)S(6)} %copy.10.tiles_hbm, bf16[384,384]{1,0:T(8,128)(2,1)} %bitcast.13, ...), custom_call_target="tpu_custom_call" | custom-call | tf_op jit(solution)/shard_map/pallas_call | solution.py:333
  5.8 8.9 %collective-permute-start = (f32[896,128]{1,0:T(8,128)}, f32[896,128]{1,0:T(8,128)S(1)}, u32[]{:S(2)}, u32[]{:S(2)}) collective-permute-start(f32[896,128]{1,0:T(8,128)} %get-tuple-element.37.level_ref), channel_id=1, source_target_pairs={{0,4},{4,0},{1,5},{5,1},{2,6},{6,2},{3,7},{7,3},{8,12},{12,8},{9,1... | collective-permute-start | bytes 1376264 | tf_op jit(solution)/shard_map/ppermute | solution.py:374
  14.7 3.4 %all-to-all-start = ((f32[8,32,256]{2,1,0:T(8,128)}), f32[8,32,256]{2,1,0:T(8,128)S(1)}, u32[]{:S(2)}, u32[]{:S(2)}) async-start(f32[8,32,256]{2,1,0:T(8,128)} %bitcast.16), calls=%async_computation | async-start | bytes 524288 | tf_op jit(solution)/shard_map/all_to_all | solution.py:379
  18.1 0.1 iota.7.bits_ref
  18.2 0.6 shard_map.96
  18.8 1.9 %collective-permute-start.1 = (f32[256,128]{1,0:T(8,128)S(1)}, f32[256,128]{1,0:T(8,128)S(1)}, u32[]{:S(2)}, u32[]{:S(2)}) collective-permute-start(f32[256,128]{1,0:T(8,128)S(1)} %get-tuple-element.38.own_ref), channel_id=1, source_target_pairs={{0,8},{8,0},{16,24},{24,16},{32,40},{40,32},{48,56},{56,48},{64,72... | collective-permute-start | bytes 393224 | tf_op jit(solution)/shard_map/ppermute | solution.py:29
  20.7 3.9 %all-to-all-done.refs_0_.parts_ref = f32[8,32,256]{2,1,0:T(8,128)S(1)} async-done(((f32[8,32,256]{2,1,0:T(8,128)}), f32[8,32,256]{2,1,0:T(8,128)S(1)}, u32[]{:S(2)}, u32[]{:S(2)}) %all-to-all-start) | async-done | bytes 262176 | tf_op jit(solution)/shard_map/all_to_all | solution.py:379
  24.6 0.5 shard_map.98
  25.1 1.9 %collective-permute-start.3 = (f32[32,256]{1,0:T(8,128)S(1)}, f32[32,256]{1,0:T(8,128)S(1)}, u32[]{:S(2)}, u32[]{:S(2)}) collective-permute-start(f32[32,256]{1,0:T(8,128)S(1)} %get-tuple-element.42.refs_0_.own_ref), channel_id=1, source_target_pairs={{0,8},{8,0},{16,24},{24,16},{32,40},{40,32},{48,56},{56,48},{64,72... | collective-permute-start | bytes 98312 | tf_op jit(solution)/shard_map/ppermute | solution.py:29
  27.1 0.6 shard_map.97
  27.6 1.9 %collective-permute-start.2 = (f32[256,128]{1,0:T(8,128)S(1)}, f32[256,128]{1,0:T(8,128)S(1)}, u32[]{:S(2)}, u32[]{:S(2)}) collective-permute-start(f32[256,128]{1,0:T(8,128)S(1)} %get-tuple-element.40.own_ref), channel_id=1, source_target_pairs={{0,24},{8,16},{16,8},{24,0},{32,56},{40,48},{48,40},{56,32},{64,88... | collective-permute-start | bytes 393224 | tf_op jit(solution)/shard_map/ppermute | solution.py:29
  29.6 0.2 collective-permute-done.3.other_ref
  29.8 0.3 shard_map.100
  30.1 4.4 %collective-permute-start.4 = (f32[32,256]{1,0:T(8,128)S(1)}, f32[32,256]{1,0:T(8,128)S(1)}, u32[]{:S(2)}, u32[]{:S(2)}) collective-permute-start(f32[32,256]{1,0:T(8,128)S(1)} %get-tuple-element.45.own_ref), channel_id=1, source_target_pairs={{0,24},{8,16},{16,8},{24,0},{32,56},{40,48},{48,40},{56,32},{64,88... | collective-permute-start | bytes 98312 | tf_op jit(solution)/shard_map/ppermute | solution.py:29
  34.5 1.0 %collective-permute-done.2.other_ref.answer_ref = f32[256,128]{1,0:T(8,128)S(1)} collective-permute-done((f32[256,128]{1,0:T(8,128)S(1)}, f32[256,128]{1,0:T(8,128)S(1)}, u32[]{:S(2)}, u32[]{:S(2)}) %collective-permute-start.2) | collective-permute-done | bytes 131104 | tf_op jit(solution)/shard_map/ppermute | solution.py:29
  35.5 0.6 shard_map.99
  36.0 0.5 collective-permute-done.4.other_ref
  36.6 0.3 shard_map.101
  36.9 1.9 %collective-permute-start.5 = (f32[264,128]{1,0:T(8,128)S(1)}, f32[264,128]{1,0:T(8,128)S(1)}, u32[]{:S(2)}, u32[]{:S(2)}) collective-permute-start(f32[264,128]{1,0:T(8,128)S(1)} %get-tuple-element.48), channel_id=1, source_target_pairs={{0,32},{8,40},{16,48},{24,56},{32,0},{40,8},{48,16},{56,24},{64,96... | collective-permute-start | bytes 405512 | tf_op jit(solution)/shard_map/ppermute | solution.py:29
  38.8 3.8 %collective-permute-done.5.other_ref = f32[264,128]{1,0:T(8,128)S(1)} collective-permute-done((f32[264,128]{1,0:T(8,128)S(1)}, f32[264,128]{1,0:T(8,128)S(1)}, u32[]{:S(2)}, u32[]{:S(2)}) %collective-permute-start.5) | collective-permute-done | bytes 135200 | tf_op jit(solution)/shard_map/ppermute | solution.py:29
  42.6 1.0 %shard_map.102 = (f32[256,128]{1,0:T(8,128)S(1)}, f32[32,128]{1,0:T(8,128)S(1)}, f32[264,128]{1,0:T(8,128)S(1)}, f32[32,256]{1,0:T(8,128)S(1)}, f32[256,128]{1,0:T(8,128)S(1)}) custom-call(s32[8,128]{1,0:T(8,128)S(1)} %iota.7.bits_ref, f32[256,128]{1,0:T(8,128)S(1)} %get-tuple-element.43.refs_0_.maps_ref, f32[32,256]{1,0:T(8,128)S(1)} %get-tuple-element.47.state_ref, ...), custom_call_target="tpu_custom_call" | custom-call | tf_op jit(solution)/shard_map/pallas_call | solution.py:333
  43.6 3.1 %collective-permute-start.6 = (f32[264,128]{1,0:T(8,128)S(1)}, f32[264,128]{1,0:T(8,128)S(1)}, u32[]{:S(2)}, u32[]{:S(2)}) collective-permute-start(f32[264,128]{1,0:T(8,128)S(1)} %get-tuple-element.51), channel_id=1, source_target_pairs={{0,64},{8,72},{16,80},{24,88},{32,96},{40,104},{48,112},{56,120},{... | collective-permute-start | bytes 405512 | tf_op jit(solution)/shard_map/ppermute | solution.py:29
  46.7 5.0 %collective-permute-done.6.other_ref = f32[264,128]{1,0:T(8,128)S(1)} collective-permute-done((f32[264,128]{1,0:T(8,128)S(1)}, f32[264,128]{1,0:T(8,128)S(1)}, u32[]{:S(2)}, u32[]{:S(2)}) %collective-permute-start.6) | collective-permute-done | bytes 135200 | tf_op jit(solution)/shard_map/ppermute | solution.py:29
  51.7 1.0 %shard_map.103 = (f32[256,128]{1,0:T(8,128)S(1)}, f32[32,128]{1,0:T(8,128)S(1)}, f32[264,128]{1,0:T(8,128)S(1)}, f32[32,256]{1,0:T(8,128)S(1)}, f32[256,128]{1,0:T(8,128)S(1)}) custom-call(s32[8,128]{1,0:T(8,128)S(1)} %iota.7.bits_ref, f32[256,128]{1,0:T(8,128)S(1)} %get-tuple-element.49.maps_ref, f32[32,256]{1,0:T(8,128)S(1)} %get-tuple-element.50.state_ref, ...), custom_call_target="tpu_custom_call" | custom-call | tf_op jit(solution)/shard_map/pallas_call | solution.py:333
  52.7 7.7 %collective-permute-start.7 = (f32[264,128]{1,0:T(8,128)S(1)}, f32[264,128]{1,0:T(8,128)S(1)}, u32[]{:S(2)}, u32[]{:S(2)}) collective-permute-start(f32[264,128]{1,0:T(8,128)S(1)} %get-tuple-element.54), channel_id=1, source_target_pairs={{0,128},{8,136},{16,144},{24,152},{32,160},{40,168},{48,176},{56,1... | collective-permute-start | bytes 405512 | tf_op jit(solution)/shard_map/ppermute | solution.py:29
  60.4 12.2 %collective-permute-done.7.other_ref = f32[264,128]{1,0:T(8,128)S(1)} collective-permute-done((f32[264,128]{1,0:T(8,128)S(1)}, f32[264,128]{1,0:T(8,128)S(1)}, u32[]{:S(2)}, u32[]{:S(2)}) %collective-permute-start.7) | collective-permute-done | bytes 135200 | tf_op jit(solution)/shard_map/ppermute | solution.py:29
  72.6 1.0 %shard_map.104 = (f32[256,128]{1,0:T(8,128)S(1)}, f32[32,128]{1,0:T(8,128)S(1)}, f32[136,128]{1,0:T(8,128)S(1)}, f32[32,256]{1,0:T(8,128)S(1)}) custom-call(s32[8,128]{1,0:T(8,128)S(1)} %iota.7.bits_ref, f32[256,128]{1,0:T(8,128)S(1)} %get-tuple-element.52.maps_ref, f32[32,256]{1,0:T(8,128)S(1)} %get-tuple-element.53.state_ref, ...), custom_call_target="tpu_custom_call" | custom-call | tf_op jit(solution)/shard_map/pallas_call | solution.py:333
  73.5 6.4 %collective-permute-start.8 = (f32[136,128]{1,0:T(8,128)S(1)}, f32[136,128]{1,0:T(8,128)S(1)}, u32[]{:S(2)}, u32[]{:S(2)}) collective-permute-start(f32[136,128]{1,0:T(8,128)S(1)} %get-tuple-element.56), channel_id=1, source_target_pairs={{0,384},{8,392},{16,400},{24,408},{32,416},{40,424},{48,432},{56,4... | collective-permute-start | bytes 208904 | tf_op jit(solution)/shard_map/ppermute | solution.py:29
  80.0 3.5 %shard_map.105.descent_ref = f32[160,512]{1,0:T(8,128)S(1)} custom-call(s32[8,128]{1,0:T(8,128)S(1)} %iota.7.bits_ref, f32[896,128]{1,0:T(8,128)S(1)} %copy-done, f32[896,128]{1,0:T(8,128)S(1)} %collective-permute-done.sibling_ref, f32[256,256]{1,0:T(8,128)S(1)} %get-tuple-element.41.weights_ref, f32[2,32,256]{2,1,0:T(8,128)S(1)} %get-tuple-element.57.owns_ref, ...), custom_call_target="tpu_custom_call" | custom-call | tf_op jit(solution)/shard_map/pallas_call | solution.py:333
  83.5 0.6 shard_map.106
  84.1 10.3 %all_to_all.10 = f32[8,32,256]{2,1,0:T(8,128)S(1)} all-to-all(f32[8,32,256]{2,1,0:T(8,128)S(1)} %shard_map.106), channel_id=1, replica_groups=mesh['pair'=64,'core'=2,'rep'=4] {'core','rep'}, dimensions={0} | all-to-all | bytes 524288 | tf_op jit(solution)/shard_map/all_to_all | solution.py:439
  94.4 1.5 %shard_map.107 = (f32[256,256]{1,0:T(8,128)}, f32[384,256]{1,0:T(8,128)}) custom-call(f32[256,256]{1,0:T(8,128)S(1)} %bitcast.15, bf16[272,384]{1,0:T(8,128)(2,1)S(1)} %copy-done.3, bf16[384,384]{1,0:T(8,128)(2,1)S(1)} %bitcast.14, bf16[768,384]{1,0:T(8,128)(2,1)S(1)} %bitcast.12), custom_call_target="tpu_custom_call" | custom-call | tf_op jit(solution)/shard_map/pallas_call | solution.py:333
  (12 shorter events, 0.0 us)
Async XLA Ops:
  5.8 12.4 %copy-start = (f32[896,128]{1,0:T(8,128)S(1)}, f32[896,128]{1,0:T(8,128)}, u32[]{:S(2)}) copy-start(f32[896,128]{1,0:T(8,128)} %get-tuple-element.37.level_ref) | copy-start | bytes 1376260
  5.8 12.3 %collective-permute-start = (f32[896,128]{1,0:T(8,128)}, f32[896,128]{1,0:T(8,128)S(1)}, u32[]{:S(2)}, u32[]{:S(2)}) collective-permute-start(f32[896,128]{1,0:T(8,128)} %get-tuple-element.37.level_ref), channel_id=1, source_target_pairs={{0,4},{4,0},{1,5},{5,1},{2,6},{6,2},{3,7},{7,3},{8,12},{12,8},{9,1... | collective-permute-start | bytes 1376264 | tf_op jit(solution)/shard_map/ppermute | solution.py:374
  14.7 9.9 %all-to-all-start = ((f32[8,32,256]{2,1,0:T(8,128)}), f32[8,32,256]{2,1,0:T(8,128)S(1)}, u32[]{:S(2)}, u32[]{:S(2)}) async-start(f32[8,32,256]{2,1,0:T(8,128)} %bitcast.16), calls=%async_computation | async-start | bytes 524288 | tf_op jit(solution)/shard_map/all_to_all | solution.py:379
  18.8 8.3 %collective-permute-start.1 = (f32[256,128]{1,0:T(8,128)S(1)}, f32[256,128]{1,0:T(8,128)S(1)}, u32[]{:S(2)}, u32[]{:S(2)}) collective-permute-start(f32[256,128]{1,0:T(8,128)S(1)} %get-tuple-element.38.own_ref), channel_id=1, source_target_pairs={{0,8},{8,0},{16,24},{24,16},{32,40},{40,32},{48,56},{56,48},{64,72... | collective-permute-start | bytes 393224 | tf_op jit(solution)/shard_map/ppermute | solution.py:29
  25.1 4.7 %collective-permute-start.3 = (f32[32,256]{1,0:T(8,128)S(1)}, f32[32,256]{1,0:T(8,128)S(1)}, u32[]{:S(2)}, u32[]{:S(2)}) collective-permute-start(f32[32,256]{1,0:T(8,128)S(1)} %get-tuple-element.42.refs_0_.own_ref), channel_id=1, source_target_pairs={{0,8},{8,0},{16,24},{24,16},{32,40},{40,32},{48,56},{56,48},{64,72... | collective-permute-start | bytes 98312 | tf_op jit(solution)/shard_map/ppermute | solution.py:29
  27.6 7.8 %collective-permute-start.2 = (f32[256,128]{1,0:T(8,128)S(1)}, f32[256,128]{1,0:T(8,128)S(1)}, u32[]{:S(2)}, u32[]{:S(2)}) collective-permute-start(f32[256,128]{1,0:T(8,128)S(1)} %get-tuple-element.40.own_ref), channel_id=1, source_target_pairs={{0,24},{8,16},{16,8},{24,0},{32,56},{40,48},{48,40},{56,32},{64,88... | collective-permute-start | bytes 393224 | tf_op jit(solution)/shard_map/ppermute | solution.py:29
  30.1 6.5 %collective-permute-start.4 = (f32[32,256]{1,0:T(8,128)S(1)}, f32[32,256]{1,0:T(8,128)S(1)}, u32[]{:S(2)}, u32[]{:S(2)}) collective-permute-start(f32[32,256]{1,0:T(8,128)S(1)} %get-tuple-element.45.own_ref), channel_id=1, source_target_pairs={{0,24},{8,16},{16,8},{24,0},{32,56},{40,48},{48,40},{56,32},{64,88... | collective-permute-start | bytes 98312 | tf_op jit(solution)/shard_map/ppermute | solution.py:29
  36.9 5.8 %collective-permute-start.5 = (f32[264,128]{1,0:T(8,128)S(1)}, f32[264,128]{1,0:T(8,128)S(1)}, u32[]{:S(2)}, u32[]{:S(2)}) collective-permute-start(f32[264,128]{1,0:T(8,128)S(1)} %get-tuple-element.48), channel_id=1, source_target_pairs={{0,32},{8,40},{16,48},{24,56},{32,0},{40,8},{48,16},{56,24},{64,96... | collective-permute-start | bytes 405512 | tf_op jit(solution)/shard_map/ppermute | solution.py:29
  43.6 8.1 %collective-permute-start.6 = (f32[264,128]{1,0:T(8,128)S(1)}, f32[264,128]{1,0:T(8,128)S(1)}, u32[]{:S(2)}, u32[]{:S(2)}) collective-permute-start(f32[264,128]{1,0:T(8,128)S(1)} %get-tuple-element.51), channel_id=1, source_target_pairs={{0,64},{8,72},{16,80},{24,88},{32,96},{40,104},{48,112},{56,120},{... | collective-permute-start | bytes 405512 | tf_op jit(solution)/shard_map/ppermute | solution.py:29
  52.7 19.9 %collective-permute-start.7 = (f32[264,128]{1,0:T(8,128)S(1)}, f32[264,128]{1,0:T(8,128)S(1)}, u32[]{:S(2)}, u32[]{:S(2)}) collective-permute-start(f32[264,128]{1,0:T(8,128)S(1)} %get-tuple-element.54), channel_id=1, source_target_pairs={{0,128},{8,136},{16,144},{24,152},{32,160},{40,168},{48,176},{56,1... | collective-permute-start | bytes 405512 | tf_op jit(solution)/shard_map/ppermute | solution.py:29
  73.5 9.9 %collective-permute-start.8 = (f32[136,128]{1,0:T(8,128)S(1)}, f32[136,128]{1,0:T(8,128)S(1)}, u32[]{:S(2)}, u32[]{:S(2)}) collective-permute-start(f32[136,128]{1,0:T(8,128)S(1)} %get-tuple-element.56), channel_id=1, source_target_pairs={{0,384},{8,392},{16,400},{24,408},{32,416},{40,424},{48,432},{56,4... | collective-permute-start | bytes 208904 | tf_op jit(solution)/shard_map/ppermute | solution.py:29
  83.5 10.9 %copy-start.1 = (bf16[1,1,768,384]{3,2,1,0:T(8,128)(2,1)S(1)}, bf16[1,1,768,384]{3,2,1,0:T(8,128)(2,1)}, u32[]{:S(2)}) copy-start(bf16[1,1,768,384]{3,2,1,0:T(8,128)(2,1)} %param.11) | copy-start | bytes 1769476
  84.1 10.4 %copy-start.2 = (bf16[1,1,384,384]{3,2,1,0:T(8,128)(2,1)S(1)}, bf16[1,1,384,384]{3,2,1,0:T(8,128)(2,1)}, u32[]{:S(2)}) copy-start(bf16[1,1,384,384]{3,2,1,0:T(8,128)(2,1)} %param.8) | copy-start | bytes 884740
  84.1 10.3 %copy-start.3 = (bf16[272,384]{1,0:T(8,128)(2,1)S(1)}, bf16[272,384]{1,0:T(8,128)(2,1)}, u32[]{:S(2)}) copy-start(bf16[272,384]{1,0:T(8,128)(2,1)} %get-tuple-element.69.forward_ref) | copy-start | bytes 626692

commit v9 on v8

--- a/solution.py
+++ b/solution.py
@@ -10,16 +10,17 @@
 TILE = 128
 HALF = TILE // 2
 MARKS = 16
-HIGHEST = lax.Precision.HIGHEST
+SPLIT = lax.Precision.HIGH
 SWAP = (1, 3, 4, 8, 16, 48)
 
 
 APART = 2
 MAPS_WEIGHT = (3, 10)
 STATE_WEIGHT = (30, 10)
-
-
-def dot(a, b, dims=((1,), (0,)), precision=HIGHEST):
+SIDE_WEIGHT = 1
+
+
+def dot(a, b, dims=((1,), (0,)), precision=SPLIT):
     return lax.dot_general(
         a, b, (dims, ((), ())), precision=precision, preferred_element_type=jnp.float32
     )
@@ -83,11 +84,6 @@
     weights_ref[TILE:, TILE:] = first[:TILE]
 
 
-def fill_step(right, first, second, turn, step_ref):
-    step_ref[:TILE] = jnp.where(right, first[:TILE], turn).T
-    step_ref[TILE:] = jnp.where(right, 0.0, second[:TILE])
-
-
 def pair_kernel(bits_ref, level_ref, sibling_ref, maps_ref, weights_ref):
     odd = pick(bits_ref, 0)
     own, other = level_ref[TILE : 3 * TILE], sibling_ref[TILE : 3 * TILE]
@@ -97,38 +93,57 @@
 
 
 def maps_kernel(j, later, bits_ref, own_ref, other_ref, *refs):
-    maps_ref, weights_ref, step_ref = refs[later:]
+    maps_ref, weights_ref = refs[later:]
     right = pick(bits_ref, j + 1)
     own, other = own_ref[...], other_ref[...]
     first, second = jnp.where(right, other, own), jnp.where(right, own, other)
     maps_ref[...], turn = join_maps(first, second)
     fill_weights(first, second, turn, weights_ref)
-    fill_step(right, first, second, turn, step_ref)
-
-
-def message(maps, state, last):
-    parts = [pack(maps[TILE:]), state[:, :TILE], state[:, TILE:]]
-    return jnp.concatenate(parts if last else [maps[:TILE]] + parts, axis=0)
-
-
-def push_of(right, own, other, answer):
-    return jnp.where(
-        right, other[:, :TILE], other[:, TILE:] + dot(own[:, :TILE], answer)
-    )
+
+
+def message(maps, state):
+    parts = [maps[:TILE], pack(maps[TILE:]), state[:, :TILE], state[:, TILE:]]
+    return jnp.concatenate(parts, axis=0)
+
+
+def last_message(right, maps, state):
+    half = jnp.where(right, state[:, TILE:], state[:, :TILE])
+    return jnp.concatenate([pack(maps[TILE:]), half], axis=0)
+
+
+def side_kernel(j, bits_ref, own_ref, state_ref, turn_ref, *refs):
+    *others, step_ref, push_ref = refs
+    right = pick(bits_ref, j + 1)
+    columns, square = state_ref.shape
+    if len(others) == 2:
+        other, other_state = others[0][...], others[1][...]
+        turn = turn_ref[:TILE, TILE:]
+    else:
+        other, other_state = open_message(others[0], columns)
+        turn = turn_ref[...]
+    own = own_ref[...]
+    step_ref[:TILE] = jnp.where(right, other[:TILE], turn).T
+    step_ref[TILE:] = jnp.where(right, 0.0, other[:TILE])
+    push_ref[...] = jnp.where(
+        right,
+        other_state[:, :TILE],
+        other_state[:, TILE:] + dot(state_ref[:, :TILE], other[TILE:]),
+    )
+
+
+def open_message(ref, columns):
+    offset = TILE + HALF + 8
+    maps = jnp.concatenate([ref[:TILE], unpack(ref[TILE:offset])], axis=0)
+    state = jnp.concatenate([ref[offset : offset + columns], ref[offset + columns :]], axis=1)
+    return maps, state
 
 
 def round_kernel(j, last, bits_ref, maps_ref, state_ref, other_ref, *refs):
-    step_ref, push_ref, message_ref, next_state_ref, *next_maps_ref = refs
+    turn_ref, message_ref, next_state_ref, *next_maps_ref = refs
     right = pick(bits_ref, j + 1)
     columns = state_ref.shape[0]
-    offset = TILE + HALF + 8
-    own = maps_ref[...]
-    answer = unpack(other_ref[TILE:offset])
-    other = jnp.concatenate([other_ref[:TILE], answer], axis=0)
-    own_state = state_ref[...]
-    other_state = jnp.concatenate(
-        [other_ref[offset : offset + columns], other_ref[offset + columns :]], axis=1
-    )
+    own, own_state = maps_ref[...], state_ref[...]
+    other, other_state = open_message(other_ref, columns)
     first, second = jnp.where(right, other, own), jnp.where(right, own, other)
     maps, turn = join_maps(first, second)
     early = jnp.where(right, other_state, own_state)
@@ -141,12 +156,13 @@
         ],
         axis=1,
     )
-    message_ref[...] = message(maps, state, last)
+    if last:
+        message_ref[...] = last_message(pick(bits_ref, j + 2), maps, state)
+    else:
+        message_ref[...] = message(maps, state)
+        next_maps_ref[0][...] = maps
     next_state_ref[...] = state
-    if not last:
-        next_maps_ref[0][...] = maps
-    fill_step(right, first, second, turn, step_ref)
-    push_ref[...] = push_of(right, own_state, other_state, answer)
+    turn_ref[...] = turn
 
 
 def join_state(first, second, weights):
@@ -174,19 +190,18 @@
     state_ref[...] = join_state(states[0], states[1], weights_ref[...])
 
 
-def state_kernel(j, bits_ref, own_ref, other_ref, answer_ref, weights_ref, *refs):
+def state_kernel(j, bits_ref, own_ref, other_ref, weights_ref, *refs):
     right = pick(bits_ref, j + 1)
     own, other = own_ref[...], other_ref[...]
     state = join_state(
         jnp.where(right, other, own), jnp.where(right, own, other), weights_ref[...]
     )
-    if len(refs) == 2:
-        state_ref, push_ref = refs
+    if len(refs) == 1:
+        state_ref = refs[0]
     else:
-        maps_ref, state_ref, push_ref, message_ref = refs
-        message_ref[...] = message(maps_ref[...], state, False)
+        maps_ref, state_ref, message_ref = refs
+        message_ref[...] = message(maps_ref[...], state)
     state_ref[...] = state
-    push_ref[...] = push_of(right, own, other, answer_ref[TILE:])
 
 
 def descend_kernel(rounds, bits_ref, level_ref, sibling_ref, weights_ref, owns_ref, states_ref, *refs):
@@ -233,11 +248,10 @@
 
 
 def finish_kernel(rounds, bits_ref, state_ref, other_ref, descent_ref, shares_ref):
-    columns, offset = state_ref.shape[0], HALF + 8
-    other = jnp.concatenate(
-        [other_ref[offset : offset + columns], other_ref[offset + columns :]], axis=1
-    )
-    push = push_of(pick(bits_ref, rounds), state_ref[...], other, unpack(other_ref[:offset]))
+    offset = HALF + 8
+    half = other_ref[offset:]
+    answered = dot(state_ref[:, :TILE], unpack(other_ref[:offset]))
+    push = half + jnp.where(pick(bits_ref, rounds), 0.0, answered)
     both = descent_ref[TILE:] + dot(push, descent_ref[:TILE])
     reps, height = shares_ref.shape[0] // 2, shares_ref.shape[2]
     for c in range(2):
@@ -252,9 +266,9 @@
 def first_kernel(
     inverse_hbm, couple_hbm, rhs_hbm, tiles_hbm, subtree_inverse_hbm, update_hbm, rows_hbm,
     level_rhs_hbm,
-    level_ref, forward_ref, part_ref,
+    level_hbm, forward_hbm, part_ref,
     inverse_ref, couple_ref, rhs_ref, tiles_ref, subtree_inverse_ref, update_ref, rows_ref,
-    level_rhs_ref, sems,
+    level_rhs_ref, sems, level_ref, forward_ref, store_sems,
 ):
     copies = fetch(
         sems,
@@ -275,6 +289,8 @@
     level_ref[height : height + TILE] = -dot(gain.T, gain)
     level_ref[height + TILE : 2 * height + TILE] = inverse_ref[:, :TILE]
     level_ref[2 * height + TILE :] = inverse_ref[:, TILE:]
+    store_level = pltpu.make_async_copy(level_ref, level_hbm, store_sems.at[0])
+    store_level.start()
     columns, sub_rows = rhs_ref.shape[1], rhs_ref.shape[0]
     copies[2].wait()
     copies[3].wait()
@@ -300,9 +316,13 @@
     for t in range(rows_ref.shape[1]):
         marks = jnp.where((row == 1) & (lane == t), rows_ref[:, t : t + 1], marks)
     forward_ref[columns:] = marks.astype(jnp.float32).astype(jnp.bfloat16)
+    store_forward = pltpu.make_async_copy(forward_ref, forward_hbm, store_sems.at[1])
+    store_forward.start()
     copies[7].wait()
     rest = 0.25 * level_rhs_ref[...].T - jnp.concatenate(totals, axis=1)
     part_ref[...] = dot(rest, inverse_ref[...], ((1,), (1,)))
+    store_level.wait()
+    store_forward.wait()
 
 
 def subtree_backward_kernel(
@@ -325,18 +345,24 @@
     final_ref[...] = jnp.where(live, final, 0.0).T
 
 
-def local_call(kernel, out_shape, *operands, fetched=(), later=(), weight=0, limit=8 * 2**20):
+def local_call(
+    kernel, out_shape, *operands, fetched=(), later=(), weight=0, limit=8 * 2**20, stored=0
+):
     vmem = pl.BlockSpec(memory_space=pltpu.VMEM)
     scratch = [pltpu.VMEM(part.shape, part.dtype) for part in fetched]
     if fetched:
         scratch.append(pltpu.SemaphoreType.DMA((len(fetched),)))
+    if stored:
+        scratch += [pltpu.VMEM(part.shape, part.dtype) for part in out_shape[:stored]]
+        scratch.append(pltpu.SemaphoreType.DMA((stored,)))
     return pl.pallas_call(
         kernel,
         out_shape=out_shape,
         in_specs=[vmem] * len(operands)
         + [pl.BlockSpec(memory_space=pltpu.HBM)] * len(fetched)
         + [pl.BlockSpec(memory_space=pl.ANY)] * len(later),
-        out_specs=[vmem] * len(out_shape),
+        out_specs=[pl.BlockSpec(memory_space=pltpu.HBM)] * stored
+        + [vmem] * (len(out_shape) - stored),
         scratch_shapes=scratch,
         cost_estimate=pl.CostEstimate(
             flops=weight * 10**9, bytes_accessed=weight * 2**20, transcendentals=0
@@ -369,7 +395,7 @@
             f32(width, height),
         ],
         fetched=(inverse, couple, rhs_sub, sub_tiles, subtree_inverse, block, rows, rhs_level),
-        limit=66 * 10**6,
+        limit=66 * 10**6, stored=2,
     )
     sibling = lax.ppermute(level, "core", [(0, 1), (1, 0)])
     maps, pair_weights = local_call(
@@ -380,17 +406,25 @@
     pushes, steps = [], []
     square = 2 * TILE
 
+    def set_aside(j, maps, state, turn, *others):
+        step, push = local_call(
+            functools.partial(side_kernel, j),
+            [f32(square, TILE), f32(columns, TILE)],
+            bits, maps, state, turn, *others, weight=SIDE_WEIGHT,
+        )
+        steps.append(step)
+        pushes.append(push)
+
     def advance_maps(j, maps, *later):
         other = swap(maps, j, count)
-        maps, weights, step = local_call(
+        joined, weights = local_call(
             functools.partial(maps_kernel, j, len(later)),
-            [f32(square, TILE), f32(square, square), f32(square, TILE)],
+            [f32(square, TILE), f32(square, square)],
             bits, maps, other, later=later, weight=MAPS_WEIGHT[j],
         )
-        steps.append(step)
-        return other, maps, weights
-
-    answer, maps, weights = advance_maps(0, maps, parts)
+        return maps, other, joined, weights
+
+    own_maps, other_maps, maps, weights = advance_maps(0, maps, parts)
     owns, states, state = local_call(
         start_kernel,
         [f32(2, columns, height), f32(2, columns, square), f32(columns, square)],
@@ -399,32 +433,35 @@
     whole = TILE + HALF + 8 + 2 * columns
     for j in range(APART):
         other = swap(state, j, count)
-        shapes = [f32(columns, square), f32(columns, TILE)]
-        operands = [bits, state, other, answer, weights]
+        shapes = [f32(columns, square)]
+        operands = [bits, state, other, weights]
+        aside = (j, own_maps, state, weights, other_maps, other)
         if j + 1 < APART:
-            answer, maps, weights = advance_maps(j + 1, maps, state)
+            own_maps, other_maps, maps, weights = advance_maps(j + 1, maps, state)
         else:
             operands.append(maps)
             shapes.append(f32(whole, TILE))
-        state, push, *packed = local_call(
+        state, *packed = local_call(
             functools.partial(state_kernel, j), shapes, *operands, weight=STATE_WEIGHT[j]
         )
-        pushes.append(push)
+        set_aside(*aside)
     packed = packed[0]
     for j in range(APART, rounds - 1):
         last = j == rounds - 2
         shapes = [
-            f32(square, TILE), f32(columns, TILE), f32(whole - last * TILE, TILE),
+            f32(TILE, TILE),
+            f32(HALF + 8 + columns if last else whole, TILE),
             f32(columns, square),
         ]
-        step, push, packed, state, *rest = local_call(
+        other = swap(packed, j, count)
+        aside = (j, maps, state)
+        turn, packed, state, *rest = local_call(
             functools.partial(round_kernel, j, last),
             shapes if last else shapes + [f32(square, TILE)],
-            bits, maps, state, swap(packed, j, count),
-        )
+            bits, maps, state, other,
+        )
+        set_aside(*aside, turn, other)
         maps = None if last else rest[0]
-        steps.append(step)
-        pushes.append(push)
     got = swap(packed, rounds - 1, count)
     (descent,) = local_call(
         functools.partial(descend_kernel, rounds - 1),

time: 96.5 us -> 94.3 us (0.977)
  Pallas kernels: 15.8 us -> 13.4 us
    pallas_call x13 -> x18, Pallas kernels: 15.8 us -> 13.4 us  [local_call(): pl.pallas_call(kernel, out_shape=out_shape, in_specs=[vmem] * len(operand...]
where the time goes in v9:
time: 94.3 us; the launch traced here: 93.8 us
  starting transfers between devices  41.3 us (44%)
  waiting for transfers between devices  26.3 us (28%)
  Pallas kernels  13.4 us (14%)
  blocking collectives  11.1 us (12%)
  between operations  1.51 us (2%)
    ppermute x8, starting transfers between devices, swap(): return lax.ppermute(value, 'pair', [(n, n ^ SWAP[j]) for n in range(count)])  29 us
    ppermute x8, waiting for transfers between devices, swap(): return lax.ppermute(value, 'pair', [(n, n ^ SWAP[j]) for n in range(count)])  22.2 us
    pallas_call x18, Pallas kernels, local_call(): pl.pallas_call(kernel, out_shape=out_shape, in_specs=[vmem] * len(operand...  13.4 us
    all_to_all x1, blocking collectives, shards(): spread = lax.all_to_all(shares, group, 0, 0)  11.1 us
    ppermute x1, starting transfers between devices, shards(): sibling = lax.ppermute(level, 'core', [(0, 1), (1, 0)])  8.92 us
    all_to_all x1, waiting for transfers between devices, shards(): parts = lax.all_to_all(part.reshape(members, columns, height), group, 0, 0)  4.08 us
    all_to_all x1, starting transfers between devices, shards(): parts = lax.all_to_all(part.reshape(members, columns, height), group, 0, 0)  3.38 us
  transfers between devices with their start and end apart: 10, of which 7 were waited for; matrix products, arithmetic and copies ran while one was open for 0% of the time, Pallas kernels for 6%

profile of v9, /device:TPU:1, one launch (start us, length us, event | category | flops | bytes accessed | tf_op | source)
XLA Modules:
  0.0 93.8 jit_solution(4105880304434505308)
XLA Ops:
  1.3 4.2 %shard_map.95 = (f32[896,128]{1,0:T(8,128)}, bf16[272,384]{1,0:T(8,128)(2,1)}, f32[256,256]{1,0:T(8,128)}) custom-call(f32[256,256]{1,0:T(8,128)} %bitcast.17, f32[256,128]{1,0:T(8,128)} %bitcast.20, bf16[384,256]{1,0:T(8,128)(2,1)} %bitcast.19, s32[1,1]{1,0:T(1,128)S(6)} %copy.10.tiles_hbm, bf16[384,384]{1,0:T(8,128)(2,1)} %bitcast.13, ...), custom_call_target="tpu_custom_call" | custom-call | tf_op jit(solution)/shard_map/pallas_call | solution.py:358
  5.5 8.9 %collective-permute-start = (f32[896,128]{1,0:T(8,128)}, f32[896,128]{1,0:T(8,128)S(1)}, u32[]{:S(2)}, u32[]{:S(2)}) collective-permute-start(f32[896,128]{1,0:T(8,128)} %get-tuple-element.39.level_ref), channel_id=1, source_target_pairs={{0,4},{4,0},{1,5},{5,1},{2,6},{6,2},{3,7},{7,3},{8,12},{12,8},{9,1... | collective-permute-start | bytes 1376264 | tf_op jit(solution)/shard_map/ppermute | solution.py:400
  14.4 3.4 %all-to-all-start = ((f32[8,32,256]{2,1,0:T(8,128)}), f32[8,32,256]{2,1,0:T(8,128)S(1)}, u32[]{:S(2)}, u32[]{:S(2)}) async-start(f32[8,32,256]{2,1,0:T(8,128)} %bitcast.16), calls=%async_computation | async-start | bytes 524288 | tf_op jit(solution)/shard_map/all_to_all | solution.py:405
  17.9 0.4 shard_map.96
  18.3 1.9 %collective-permute-start.1 = (f32[256,128]{1,0:T(8,128)S(1)}, f32[256,128]{1,0:T(8,128)S(1)}, u32[]{:S(2)}, u32[]{:S(2)}) collective-permute-start(f32[256,128]{1,0:T(8,128)S(1)} %get-tuple-element.40.own_ref), channel_id=1, source_target_pairs={{0,8},{8,0},{16,24},{24,16},{32,40},{40,32},{48,56},{56,48},{64,72... | collective-permute-start | bytes 393224 | tf_op jit(solution)/shard_map/ppermute | solution.py:30
  20.2 4.1 %all-to-all-done.refs_0_.parts_ref = f32[8,32,256]{2,1,0:T(8,128)S(1)} async-done(((f32[8,32,256]{2,1,0:T(8,128)}), f32[8,32,256]{2,1,0:T(8,128)S(1)}, u32[]{:S(2)}, u32[]{:S(2)}) %all-to-all-start) | async-done | bytes 262176 | tf_op jit(solution)/shard_map/all_to_all | solution.py:405
  24.3 0.4 shard_map.98
  24.7 1.9 %collective-permute-start.3 = (f32[32,256]{1,0:T(8,128)S(1)}, f32[32,256]{1,0:T(8,128)S(1)}, u32[]{:S(2)}, u32[]{:S(2)}) collective-permute-start(f32[32,256]{1,0:T(8,128)S(1)} %get-tuple-element.44.refs_0_.own_ref.state_ref), channel_id=1, source_target_pairs={{0,8},{8,0},{16,24},{24,16},{32,40},{40,32},{48,56},{56,48},{64,72... | collective-permute-start | bytes 98312 | tf_op jit(solution)/shard_map/ppermute | solution.py:30
  26.7 0.4 shard_map.97
  27.1 1.9 %collective-permute-start.2 = (f32[256,128]{1,0:T(8,128)S(1)}, f32[256,128]{1,0:T(8,128)S(1)}, u32[]{:S(2)}, u32[]{:S(2)}) collective-permute-start(f32[256,128]{1,0:T(8,128)S(1)} %get-tuple-element.42.own_ref), channel_id=1, source_target_pairs={{0,24},{8,16},{16,8},{24,0},{32,56},{40,48},{48,40},{56,32},{64,88... | collective-permute-start | bytes 393224 | tf_op jit(solution)/shard_map/ppermute | solution.py:30
  29.0 0.4 collective-permute-done.3.other_ref.refs_1_
  29.6 4.2 %collective-permute-start.4 = (f32[32,256]{1,0:T(8,128)S(1)}, f32[32,256]{1,0:T(8,128)S(1)}, u32[]{:S(2)}, u32[]{:S(2)}) collective-permute-start(f32[32,256]{1,0:T(8,128)S(1)} %shard_map.100.own_ref.state_ref), channel_id=1, source_target_pairs={{0,24},{8,16},{16,8},{24,0},{32,56},{40,48},{48,40},{56,32},{64,88... | collective-permute-start | bytes 98312 | tf_op jit(solution)/shard_map/ppermute | solution.py:30
  33.8 1.1 %collective-permute-done.2.other_ref.refs_0_ = f32[256,128]{1,0:T(8,128)S(1)} collective-permute-done((f32[256,128]{1,0:T(8,128)S(1)}, f32[256,128]{1,0:T(8,128)S(1)}, u32[]{:S(2)}, u32[]{:S(2)}) %collective-permute-start.2) | collective-permute-done | bytes 131104 | tf_op jit(solution)/shard_map/ppermute | solution.py:30
  34.9 0.4 shard_map.99
  35.3 0.6 collective-permute-done.4.other_ref.refs_1_
  36.1 1.9 %collective-permute-start.5 = (f32[264,128]{1,0:T(8,128)S(1)}, f32[264,128]{1,0:T(8,128)S(1)}, u32[]{:S(2)}, u32[]{:S(2)}) collective-permute-start(f32[264,128]{1,0:T(8,128)S(1)} %get-tuple-element.49), channel_id=1, source_target_pairs={{0,32},{8,40},{16,48},{24,56},{32,0},{40,8},{48,16},{56,24},{64,96... | collective-permute-start | bytes 405512 | tf_op jit(solution)/shard_map/ppermute | solution.py:30
  38.1 3.8 %collective-permute-done.5.other_ref.refs_0_ = f32[264,128]{1,0:T(8,128)S(1)} collective-permute-done((f32[264,128]{1,0:T(8,128)S(1)}, f32[264,128]{1,0:T(8,128)S(1)}, u32[]{:S(2)}, u32[]{:S(2)}) %collective-permute-start.5) | collective-permute-done | bytes 135200 | tf_op jit(solution)/shard_map/ppermute | solution.py:30
  41.9 0.6 shard_map.102
  42.5 3.1 %collective-permute-start.6 = (f32[264,128]{1,0:T(8,128)S(1)}, f32[264,128]{1,0:T(8,128)S(1)}, u32[]{:S(2)}, u32[]{:S(2)}) collective-permute-start(f32[264,128]{1,0:T(8,128)S(1)} %get-tuple-element.52), channel_id=1, source_target_pairs={{0,64},{8,72},{16,80},{24,88},{32,96},{40,104},{48,112},{56,120},{... | collective-permute-start | bytes 405512 | tf_op jit(solution)/shard_map/ppermute | solution.py:30
  45.9 4.7 %collective-permute-done.6.other_ref.refs_0_ = f32[264,128]{1,0:T(8,128)S(1)} collective-permute-done((f32[264,128]{1,0:T(8,128)S(1)}, f32[264,128]{1,0:T(8,128)S(1)}, u32[]{:S(2)}, u32[]{:S(2)}) %collective-permute-start.6) | collective-permute-done | bytes 135200 | tf_op jit(solution)/shard_map/ppermute | solution.py:30
  50.6 0.6 shard_map.103
  51.2 7.6 %collective-permute-start.7 = (f32[264,128]{1,0:T(8,128)S(1)}, f32[264,128]{1,0:T(8,128)S(1)}, u32[]{:S(2)}, u32[]{:S(2)}) collective-permute-start(f32[264,128]{1,0:T(8,128)S(1)} %get-tuple-element.55), channel_id=1, source_target_pairs={{0,128},{8,136},{16,144},{24,152},{32,160},{40,168},{48,176},{56,1... | collective-permute-start | bytes 405512 | tf_op jit(solution)/shard_map/ppermute | solution.py:30
  58.9 0.3 shard_map.107
  59.1 0.3 shard_map.108
  59.5 11.6 %collective-permute-done.7.other_ref.refs_0_ = f32[264,128]{1,0:T(8,128)S(1)} collective-permute-done((f32[264,128]{1,0:T(8,128)S(1)}, f32[264,128]{1,0:T(8,128)S(1)}, u32[]{:S(2)}, u32[]{:S(2)}) %collective-permute-start.7) | collective-permute-done | bytes 135200 | tf_op jit(solution)/shard_map/ppermute | solution.py:30
  71.1 0.6 shard_map.104
  71.7 6.4 %collective-permute-start.8 = (f32[104,128]{1,0:T(8,128)S(1)}, f32[104,128]{1,0:T(8,128)S(1)}, u32[]{:S(2)}, u32[]{:S(2)}) collective-permute-start(f32[104,128]{1,0:T(8,128)S(1)} %get-tuple-element.57), channel_id=1, source_target_pairs={{0,384},{8,392},{16,400},{24,408},{32,416},{40,424},{48,432},{56,4... | collective-permute-start | bytes 159752 | tf_op jit(solution)/shard_map/ppermute | solution.py:30
  78.1 0.3 shard_map.109
  78.4 2.2 %shard_map.110.descent_ref = f32[160,512]{1,0:T(8,128)S(1)} custom-call(s32[8,128]{1,0:T(8,128)S(1)} %iota.7.bits_ref, f32[896,128]{1,0:T(8,128)S(1)} %copy-done, f32[896,128]{1,0:T(8,128)S(1)} %collective-permute-done.sibling_ref, f32[256,256]{1,0:T(8,128)S(1)} %get-tuple-element.43.weights_ref, f32[2,32,256]{2,1,0:T(8,128)S(1)} %get-tuple-element.58.owns_ref, ...), custom_call_target="tpu_custom_call" | custom-call | tf_op jit(solution)/shard_map/pallas_call | solution.py:358
  80.6 0.5 shard_map.111
  81.1 11.1 %all_to_all.10 = f32[8,32,256]{2,1,0:T(8,128)S(1)} all-to-all(f32[8,32,256]{2,1,0:T(8,128)S(1)} %shard_map.111), channel_id=1, replica_groups=mesh['pair'=64,'core'=2,'rep'=4] {'core','rep'}, dimensions={0} | all-to-all | bytes 524288 | tf_op jit(solution)/shard_map/all_to_all | solution.py:476
  92.2 1.5 %shard_map.112 = (f32[256,256]{1,0:T(8,128)}, f32[384,256]{1,0:T(8,128)}) custom-call(f32[256,256]{1,0:T(8,128)S(1)} %bitcast.15, bf16[272,384]{1,0:T(8,128)(2,1)S(1)} %copy-done.3, bf16[384,384]{1,0:T(8,128)(2,1)S(1)} %bitcast.14, bf16[768,384]{1,0:T(8,128)(2,1)S(1)} %bitcast.12), custom_call_target="tpu_custom_call" | custom-call | tf_op jit(solution)/shard_map/pallas_call | solution.py:358
  (17 shorter events, 0.8 us)
Async XLA Ops:
  5.5 12.4 %copy-start = (f32[896,128]{1,0:T(8,128)S(1)}, f32[896,128]{1,0:T(8,128)}, u32[]{:S(2)}) copy-start(f32[896,128]{1,0:T(8,128)} %get-tuple-element.39.level_ref) | copy-start | bytes 1376260
  5.5 12.3 %collective-permute-start = (f32[896,128]{1,0:T(8,128)}, f32[896,128]{1,0:T(8,128)S(1)}, u32[]{:S(2)}, u32[]{:S(2)}) collective-permute-start(f32[896,128]{1,0:T(8,128)} %get-tuple-element.39.level_ref), channel_id=1, source_target_pairs={{0,4},{4,0},{1,5},{5,1},{2,6},{6,2},{3,7},{7,3},{8,12},{12,8},{9,1... | collective-permute-start | bytes 1376264 | tf_op jit(solution)/shard_map/ppermute | solution.py:400
  14.4 9.9 %all-to-all-start = ((f32[8,32,256]{2,1,0:T(8,128)}), f32[8,32,256]{2,1,0:T(8,128)S(1)}, u32[]{:S(2)}, u32[]{:S(2)}) async-start(f32[8,32,256]{2,1,0:T(8,128)} %bitcast.16), calls=%async_computation | async-start | bytes 524288 | tf_op jit(solution)/shard_map/all_to_all | solution.py:405
  18.3 8.3 %collective-permute-start.1 = (f32[256,128]{1,0:T(8,128)S(1)}, f32[256,128]{1,0:T(8,128)S(1)}, u32[]{:S(2)}, u32[]{:S(2)}) collective-permute-start(f32[256,128]{1,0:T(8,128)S(1)} %get-tuple-element.40.own_ref), channel_id=1, source_target_pairs={{0,8},{8,0},{16,24},{24,16},{32,40},{40,32},{48,56},{56,48},{64,72... | collective-permute-start | bytes 393224 | tf_op jit(solution)/shard_map/ppermute | solution.py:30
  24.7 4.7 %collective-permute-start.3 = (f32[32,256]{1,0:T(8,128)S(1)}, f32[32,256]{1,0:T(8,128)S(1)}, u32[]{:S(2)}, u32[]{:S(2)}) collective-permute-start(f32[32,256]{1,0:T(8,128)S(1)} %get-tuple-element.44.refs_0_.own_ref.state_ref), channel_id=1, source_target_pairs={{0,8},{8,0},{16,24},{24,16},{32,40},{40,32},{48,56},{56,48},{64,72... | collective-permute-start | bytes 98312 | tf_op jit(solution)/shard_map/ppermute | solution.py:30
  27.1 7.8 %collective-permute-start.2 = (f32[256,128]{1,0:T(8,128)S(1)}, f32[256,128]{1,0:T(8,128)S(1)}, u32[]{:S(2)}, u32[]{:S(2)}) collective-permute-start(f32[256,128]{1,0:T(8,128)S(1)} %get-tuple-element.42.own_ref), channel_id=1, source_target_pairs={{0,24},{8,16},{16,8},{24,0},{32,56},{40,48},{48,40},{56,32},{64,88... | collective-permute-start | bytes 393224 | tf_op jit(solution)/shard_map/ppermute | solution.py:30
  29.6 6.4 %collective-permute-start.4 = (f32[32,256]{1,0:T(8,128)S(1)}, f32[32,256]{1,0:T(8,128)S(1)}, u32[]{:S(2)}, u32[]{:S(2)}) collective-permute-start(f32[32,256]{1,0:T(8,128)S(1)} %shard_map.100.own_ref.state_ref), channel_id=1, source_target_pairs={{0,24},{8,16},{16,8},{24,0},{32,56},{40,48},{48,40},{56,32},{64,88... | collective-permute-start | bytes 98312 | tf_op jit(solution)/shard_map/ppermute | solution.py:30
  36.1 5.8 %collective-permute-start.5 = (f32[264,128]{1,0:T(8,128)S(1)}, f32[264,128]{1,0:T(8,128)S(1)}, u32[]{:S(2)}, u32[]{:S(2)}) collective-permute-start(f32[264,128]{1,0:T(8,128)S(1)} %get-tuple-element.49), channel_id=1, source_target_pairs={{0,32},{8,40},{16,48},{24,56},{32,0},{40,8},{48,16},{56,24},{64,96... | collective-permute-start | bytes 405512 | tf_op jit(solution)/shard_map/ppermute | solution.py:30
  42.5 8.1 %collective-permute-start.6 = (f32[264,128]{1,0:T(8,128)S(1)}, f32[264,128]{1,0:T(8,128)S(1)}, u32[]{:S(2)}, u32[]{:S(2)}) collective-permute-start(f32[264,128]{1,0:T(8,128)S(1)} %get-tuple-element.52), channel_id=1, source_target_pairs={{0,64},{8,72},{16,80},{24,88},{32,96},{40,104},{48,112},{56,120},{... | collective-permute-start | bytes 405512 | tf_op jit(solution)/shard_map/ppermute | solution.py:30
  51.2 19.9 %collective-permute-start.7 = (f32[264,128]{1,0:T(8,128)S(1)}, f32[264,128]{1,0:T(8,128)S(1)}, u32[]{:S(2)}, u32[]{:S(2)}) collective-permute-start(f32[264,128]{1,0:T(8,128)S(1)} %get-tuple-element.55), channel_id=1, source_target_pairs={{0,128},{8,136},{16,144},{24,152},{32,160},{40,168},{48,176},{56,1... | collective-permute-start | bytes 405512 | tf_op jit(solution)/shard_map/ppermute | solution.py:30
  71.7 8.9 %collective-permute-start.8 = (f32[104,128]{1,0:T(8,128)S(1)}, f32[104,128]{1,0:T(8,128)S(1)}, u32[]{:S(2)}, u32[]{:S(2)}) collective-permute-start(f32[104,128]{1,0:T(8,128)S(1)} %get-tuple-element.57), channel_id=1, source_target_pairs={{0,384},{8,392},{16,400},{24,408},{32,416},{40,424},{48,432},{56,4... | collective-permute-start | bytes 159752 | tf_op jit(solution)/shard_map/ppermute | solution.py:30
  80.6 11.7 %copy-start.1 = (bf16[1,1,768,384]{3,2,1,0:T(8,128)(2,1)S(1)}, bf16[1,1,768,384]{3,2,1,0:T(8,128)(2,1)}, u32[]{:S(2)}) copy-start(bf16[1,1,768,384]{3,2,1,0:T(8,128)(2,1)} %param.11) | copy-start | bytes 1769476
  81.1 11.2 %copy-start.2 = (bf16[1,1,384,384]{3,2,1,0:T(8,128)(2,1)S(1)}, bf16[1,1,384,384]{3,2,1,0:T(8,128)(2,1)}, u32[]{:S(2)}) copy-start(bf16[1,1,384,384]{3,2,1,0:T(8,128)(2,1)} %param.8) | copy-start | bytes 884740
  81.1 11.2 %copy-start.3 = (bf16[272,384]{1,0:T(8,128)(2,1)S(1)}, bf16[272,384]{1,0:T(8,128)(2,1)}, u32[]{:S(2)}) copy-start(bf16[272,384]{1,0:T(8,128)(2,1)} %get-tuple-element.73.forward_ref) | copy-start | bytes 626692

commit v10 on v9

--- a/solution.py
+++ b/solution.py
@@ -10,7 +10,6 @@
 TILE = 128
 HALF = TILE // 2
 MARKS = 16
-SPLIT = lax.Precision.HIGH
 SWAP = (1, 3, 4, 8, 16, 48)
 
 
@@ -20,10 +19,19 @@
 SIDE_WEIGHT = 1
 
 
-def dot(a, b, dims=((1,), (0,)), precision=SPLIT):
-    return lax.dot_general(
-        a, b, (dims, ((), ())), precision=precision, preferred_element_type=jnp.float32
-    )
+def dot(a, b, dims=((1,), (0,))):
+    return lax.dot_general(a, b, (dims, ((), ())), preferred_element_type=jnp.float32)
+
+
+def halves(value):
+    high = value.astype(jnp.bfloat16)
+    return high, (value - high.astype(jnp.float32)).astype(jnp.bfloat16)
+
+
+def fine_dot(a, b, dims=((1,), (0,))):
+    (a_high, a_low), (b_high, b_low) = halves(a), halves(b)
+    small = dot(a_high, b_low, dims) + dot(a_low, b_high, dims)
+    return small + dot(a_high, b_high, dims)
 
 
 def swap(value, j, count):
@@ -71,9 +79,9 @@
 
 def join_maps(first, second):
     early = first[:TILE]
-    product = dot(second, early)
+    product = fine_dot(second, early)
     turn = product[TILE:]
-    answer = first[TILE:] + dot(early.T, turn)
+    answer = first[TILE:] + fine_dot(early.T, turn)
     return jnp.concatenate([product[:TILE], answer], axis=0), turn
 
 
@@ -127,7 +135,7 @@
     push_ref[...] = jnp.where(
         right,
         other_state[:, :TILE],
-        other_state[:, TILE:] + dot(state_ref[:, :TILE], other[TILE:]),
+        other_state[:, TILE:] + fine_dot(state_ref[:, :TILE], other[TILE:]),
     )
 
 
@@ -151,8 +159,8 @@
     entry = early[:, :TILE]
     state = jnp.concatenate(
         [
-            late[:, :TILE] + dot(entry, second[:TILE], ((1,), (1,))),
-            early[:, TILE:] + dot(late[:, TILE:], first[:TILE]) + dot(entry, turn),
+            late[:, :TILE] + fine_dot(entry, second[:TILE], ((1,), (1,))),
+            early[:, TILE:] + fine_dot(late[:, TILE:], first[:TILE]) + fine_dot(entry, turn),
         ],
         axis=1,
     )
@@ -168,7 +176,7 @@
 def join_state(first, second, weights):
     mixed = jnp.concatenate([first[:, :TILE], second[:, TILE:]], axis=1)
     kept = jnp.concatenate([second[:, :TILE], first[:, TILE:]], axis=1)
-    return kept + dot(mixed, weights)
+    return kept + fine_dot(mixed, weights)
 
 
 def start_kernel(
@@ -185,7 +193,7 @@
         for r in range(1, reps):
             own = own + parts_ref[c * reps + r]
         owns_ref[c] = own
-        states.append(jnp.concatenate([own[:, TILE:], -dot(own, gains[c])], axis=1))
+        states.append(jnp.concatenate([own[:, TILE:], -fine_dot(own, gains[c])], axis=1))
         states_ref[c] = states[c]
     state_ref[...] = join_state(states[0], states[1], weights_ref[...])
 
@@ -220,29 +228,29 @@
     before, after = jnp.where(right, basis, 0.0), jnp.where(right, 0.0, basis)
     for j in reversed(range(rounds)):
         right = pick(bits_ref, j + 1)
-        push = under(pushes[j][...]) + dot(jnp.concatenate([before, after], axis=1), steps[j][...])
+        push = under(pushes[j][...]) + fine_dot(jnp.concatenate([before, after], axis=1), steps[j][...])
         before, after = jnp.where(right, push, before), jnp.where(right, after, push)
     own, other = level_ref[...], sibling_ref[...]
     levels = (jnp.where(odd, other, own), jnp.where(odd, own, other))
     maps = [level[TILE : 3 * TILE] for level in levels]
     entry = states_ref[0, :, :TILE]
-    middle_before = under(entry) + dot(before, maps[0][:TILE], ((1,), (1,)))
+    middle_before = under(entry) + fine_dot(before, maps[0][:TILE], ((1,), (1,)))
     middle_after = (
-        under(states_ref[1, :, TILE:] + dot(entry, maps[1][TILE:]))
-        + dot(before, weights_ref[:TILE, TILE:], ((1,), (1,)))
-        + dot(after, maps[1][:TILE])
+        under(states_ref[1, :, TILE:] + fine_dot(entry, maps[1][TILE:]))
+        + fine_dot(before, weights_ref[:TILE, TILE:], ((1,), (1,)))
+        + fine_dot(after, maps[1][:TILE])
     )
     ends = ((before, middle_after), (middle_before, after))
     for c in range(2):
         level = levels[c]
-        forward = under(owns_ref[c]) + dot(ends[c][0], level[:height], ((1,), (1,)))
+        forward = under(owns_ref[c]) + fine_dot(ends[c][0], level[:height], ((1,), (1,)))
         forward = jnp.concatenate(
             [forward[:, :TILE], forward[:, TILE:] - ends[c][1]], axis=1
         )
-        descent_ref[:, 2 * c * TILE : (2 * c + 1) * TILE] = dot(
+        descent_ref[:, 2 * c * TILE : (2 * c + 1) * TILE] = fine_dot(
             forward, level[height + TILE : 2 * height + TILE]
         )
-        descent_ref[:, (2 * c + 1) * TILE : (2 * c + 2) * TILE] = dot(
+        descent_ref[:, (2 * c + 1) * TILE : (2 * c + 2) * TILE] = fine_dot(
             forward, level[2 * height + TILE :]
         )
 
@@ -250,9 +258,9 @@
 def finish_kernel(rounds, bits_ref, state_ref, other_ref, descent_ref, shares_ref):
     offset = HALF + 8
     half = other_ref[offset:]
-    answered = dot(state_ref[:, :TILE], unpack(other_ref[:offset]))
+    answered = fine_dot(state_ref[:, :TILE], unpack(other_ref[:offset]))
     push = half + jnp.where(pick(bits_ref, rounds), 0.0, answered)
-    both = descent_ref[TILE:] + dot(push, descent_ref[:TILE])
+    both = descent_ref[TILE:] + fine_dot(push, descent_ref[:TILE])
     reps, height = shares_ref.shape[0] // 2, shares_ref.shape[2]
     for c in range(2):
         for r in range(reps):
@@ -284,9 +292,9 @@
     height = inverse_ref.shape[0]
     copies[0].wait()
     copies[1].wait()
-    gain = -dot(inverse_ref[...], couple_ref[...])
+    gain = -fine_dot(inverse_ref[...], couple_ref[...])
     level_ref[:height] = gain
-    level_ref[height : height + TILE] = -dot(gain.T, gain)
+    level_ref[height : height + TILE] = -fine_dot(gain.T, gain)
     level_ref[height + TILE : 2 * height + TILE] = inverse_ref[:, :TILE]
     level_ref[2 * height + TILE :] = inverse_ref[:, TILE:]
     store_level = pltpu.make_async_copy(level_ref, level_hbm, store_sems.at[0])
@@ -297,11 +305,11 @@
     live = live_columns(tiles_ref[...], columns, sub_rows)
     masked = jnp.where(live, rhs_ref[...].astype(jnp.float32).T, 0.0).astype(jnp.bfloat16)
     copies[4].wait()
-    solved = dot(masked, subtree_inverse_ref[...], ((1,), (1,)), None)
+    solved = dot(masked, subtree_inverse_ref[...], ((1,), (1,)))
     forward = jnp.where(live, solved, 0.0).astype(jnp.bfloat16)
     forward_ref[:columns] = forward
     copies[5].wait()
-    contrib = dot(forward, update_ref[...], ((1,), (1,)), None)
+    contrib = dot(forward, update_ref[...], ((1,), (1,)))
     copies[6].wait()
     totals = []
     for s in range(level_rhs_ref.shape[0] // TILE):
@@ -320,7 +328,7 @@
     store_forward.start()
     copies[7].wait()
     rest = 0.25 * level_rhs_ref[...].T - jnp.concatenate(totals, axis=1)
-    part_ref[...] = dot(rest, inverse_ref[...], ((1,), (1,)))
+    part_ref[...] = fine_dot(rest, inverse_ref[...], ((1,), (1,)))
     store_level.wait()
     store_forward.wait()
 
@@ -339,9 +347,9 @@
             here = marks[1:2, t : t + 1] == s
             tile = jnp.where(here, solution_ref[:, s * TILE : (s + 1) * TILE], tile)
         picked.append(tile.astype(jnp.bfloat16))
-    pulled = dot(jnp.concatenate(picked, axis=1), update_ref[...], precision=None)
+    pulled = dot(jnp.concatenate(picked, axis=1), update_ref[...])
     residue = forward_ref[:columns].astype(jnp.float32) - jnp.where(live, pulled, 0.0)
-    final = dot(residue.astype(jnp.bfloat16), subtree_inverse_ref[...], precision=None)
+    final = dot(residue.astype(jnp.bfloat16), subtree_inverse_ref[...])
     final_ref[...] = jnp.where(live, final, 0.0).T
 
 

time: 94.3 us -> 94.3 us (level)
  transfers between devices with their start and end apart: 10 -> 10, of which waited for: 7 -> 7; matrix products, arithmetic and copies ran while one was open for 0% -> 0% of each run, Pallas kernels for 6% -> 5%
where the time goes in v10:
time: 94.3 us; the launch traced here: 93.8 us
  starting transfers between devices  41.3 us (44%)
  waiting for transfers between devices  26.3 us (28%)
  Pallas kernels  13.2 us (14%)
  blocking collectives  11.3 us (12%)
  between operations  1.51 us (2%)
    ppermute x8, starting transfers between devices, swap(): return lax.ppermute(value, 'pair', [(n, n ^ SWAP[j]) for n in range(count)])  29 us
    ppermute x8, waiting for transfers between devices, swap(): return lax.ppermute(value, 'pair', [(n, n ^ SWAP[j]) for n in range(count)])  22.2 us
    pallas_call x18, Pallas kernels, local_call(): pl.pallas_call(kernel, out_shape=out_shape, in_specs=[vmem] * len(operand...  13.2 us
    all_to_all x1, blocking collectives, shards(): spread = lax.all_to_all(shares, group, 0, 0)  11.3 us
    ppermute x1, starting transfers between devices, shards(): sibling = lax.ppermute(level, 'core', [(0, 1), (1, 0)])  8.92 us
    all_to_all x1, waiting for transfers between devices, shards(): parts = lax.all_to_all(part.reshape(members, columns, height), group, 0, 0)  4.08 us
    all_to_all x1, starting transfers between devices, shards(): parts = lax.all_to_all(part.reshape(members, columns, height), group, 0, 0)  3.38 us
  transfers between devices with their start and end apart: 10, of which 7 were waited for; matrix products, arithmetic and copies ran while one was open for 0% of the time, Pallas kernels for 5%

profile of v10, /device:TPU:1, one launch (start us, length us, event | category | flops | bytes accessed | tf_op | source)
XLA Modules:
  0.0 93.8 jit_solution(13529114653254859727)
XLA Ops:
  1.3 4.2 %shard_map.95 = (f32[896,128]{1,0:T(8,128)}, bf16[272,384]{1,0:T(8,128)(2,1)}, f32[256,256]{1,0:T(8,128)}) custom-call(f32[256,256]{1,0:T(8,128)} %bitcast.17, f32[256,128]{1,0:T(8,128)} %bitcast.20, bf16[384,256]{1,0:T(8,128)(2,1)} %bitcast.19, s32[1,1]{1,0:T(1,128)S(6)} %copy.10.tiles_hbm, bf16[384,384]{1,0:T(8,128)(2,1)} %bitcast.13, ...), custom_call_target="tpu_custom_call" | custom-call | tf_op jit(solution)/shard_map/pallas_call | solution.py:366
  5.4 8.9 %collective-permute-start = (f32[896,128]{1,0:T(8,128)}, f32[896,128]{1,0:T(8,128)S(1)}, u32[]{:S(2)}, u32[]{:S(2)}) collective-permute-start(f32[896,128]{1,0:T(8,128)} %get-tuple-element.39.level_ref), channel_id=1, source_target_pairs={{0,4},{4,0},{1,5},{5,1},{2,6},{6,2},{3,7},{7,3},{8,12},{12,8},{9,1... | collective-permute-start | bytes 1376264 | tf_op jit(solution)/shard_map/ppermute | solution.py:408
  14.4 3.4 %all-to-all-start = ((f32[8,32,256]{2,1,0:T(8,128)}), f32[8,32,256]{2,1,0:T(8,128)S(1)}, u32[]{:S(2)}, u32[]{:S(2)}) async-start(f32[8,32,256]{2,1,0:T(8,128)} %bitcast.16), calls=%async_computation | async-start | bytes 524288 | tf_op jit(solution)/shard_map/all_to_all | solution.py:413
  17.9 0.4 shard_map.96
  18.3 1.9 %collective-permute-start.1 = (f32[256,128]{1,0:T(8,128)S(1)}, f32[256,128]{1,0:T(8,128)S(1)}, u32[]{:S(2)}, u32[]{:S(2)}) collective-permute-start(f32[256,128]{1,0:T(8,128)S(1)} %get-tuple-element.40.own_ref), channel_id=1, source_target_pairs={{0,8},{8,0},{16,24},{24,16},{32,40},{40,32},{48,56},{56,48},{64,72... | collective-permute-start | bytes 393224 | tf_op jit(solution)/shard_map/ppermute | solution.py:38
  20.2 4.1 %all-to-all-done.refs_0_.parts_ref = f32[8,32,256]{2,1,0:T(8,128)S(1)} async-done(((f32[8,32,256]{2,1,0:T(8,128)}), f32[8,32,256]{2,1,0:T(8,128)S(1)}, u32[]{:S(2)}, u32[]{:S(2)}) %all-to-all-start) | async-done | bytes 262176 | tf_op jit(solution)/shard_map/all_to_all | solution.py:413
  24.3 0.4 shard_map.98
  24.7 1.9 %collective-permute-start.3 = (f32[32,256]{1,0:T(8,128)S(1)}, f32[32,256]{1,0:T(8,128)S(1)}, u32[]{:S(2)}, u32[]{:S(2)}) collective-permute-start(f32[32,256]{1,0:T(8,128)S(1)} %get-tuple-element.44.refs_0_.own_ref.state_ref), channel_id=1, source_target_pairs={{0,8},{8,0},{16,24},{24,16},{32,40},{40,32},{48,56},{56,48},{64,72... | collective-permute-start | bytes 98312 | tf_op jit(solution)/shard_map/ppermute | solution.py:38
  26.6 0.4 shard_map.97
  27.1 1.9 %collective-permute-start.2 = (f32[256,128]{1,0:T(8,128)S(1)}, f32[256,128]{1,0:T(8,128)S(1)}, u32[]{:S(2)}, u32[]{:S(2)}) collective-permute-start(f32[256,128]{1,0:T(8,128)S(1)} %get-tuple-element.42.own_ref), channel_id=1, source_target_pairs={{0,24},{8,16},{16,8},{24,0},{32,56},{40,48},{48,40},{56,32},{64,88... | collective-permute-start | bytes 393224 | tf_op jit(solution)/shard_map/ppermute | solution.py:38
  29.0 0.4 collective-permute-done.3.other_ref.refs_1_
  29.5 4.2 %collective-permute-start.4 = (f32[32,256]{1,0:T(8,128)S(1)}, f32[32,256]{1,0:T(8,128)S(1)}, u32[]{:S(2)}, u32[]{:S(2)}) collective-permute-start(f32[32,256]{1,0:T(8,128)S(1)} %shard_map.100.own_ref.state_ref), channel_id=1, source_target_pairs={{0,24},{8,16},{16,8},{24,0},{32,56},{40,48},{48,40},{56,32},{64,88... | collective-permute-start | bytes 98312 | tf_op jit(solution)/shard_map/ppermute | solution.py:38
  33.8 1.1 %collective-permute-done.2.other_ref.refs_0_ = f32[256,128]{1,0:T(8,128)S(1)} collective-permute-done((f32[256,128]{1,0:T(8,128)S(1)}, f32[256,128]{1,0:T(8,128)S(1)}, u32[]{:S(2)}, u32[]{:S(2)}) %collective-permute-start.2) | collective-permute-done | bytes 131104 | tf_op jit(solution)/shard_map/ppermute | solution.py:38
  34.9 0.4 shard_map.99
  35.3 0.6 collective-permute-done.4.other_ref.refs_1_
  36.1 1.9 %collective-permute-start.5 = (f32[264,128]{1,0:T(8,128)S(1)}, f32[264,128]{1,0:T(8,128)S(1)}, u32[]{:S(2)}, u32[]{:S(2)}) collective-permute-start(f32[264,128]{1,0:T(8,128)S(1)} %get-tuple-element.49), channel_id=1, source_target_pairs={{0,32},{8,40},{16,48},{24,56},{32,0},{40,8},{48,16},{56,24},{64,96... | collective-permute-start | bytes 405512 | tf_op jit(solution)/shard_map/ppermute | solution.py:38
  38.1 3.8 %collective-permute-done.5.other_ref.refs_0_ = f32[264,128]{1,0:T(8,128)S(1)} collective-permute-done((f32[264,128]{1,0:T(8,128)S(1)}, f32[264,128]{1,0:T(8,128)S(1)}, u32[]{:S(2)}, u32[]{:S(2)}) %collective-permute-start.5) | collective-permute-done | bytes 135200 | tf_op jit(solution)/shard_map/ppermute | solution.py:38
  41.9 0.6 shard_map.102
  42.5 3.1 %collective-permute-start.6 = (f32[264,128]{1,0:T(8,128)S(1)}, f32[264,128]{1,0:T(8,128)S(1)}, u32[]{:S(2)}, u32[]{:S(2)}) collective-permute-start(f32[264,128]{1,0:T(8,128)S(1)} %get-tuple-element.52), channel_id=1, source_target_pairs={{0,64},{8,72},{16,80},{24,88},{32,96},{40,104},{48,112},{56,120},{... | collective-permute-start | bytes 405512 | tf_op jit(solution)/shard_map/ppermute | solution.py:38
  45.9 4.7 %collective-permute-done.6.other_ref.refs_0_ = f32[264,128]{1,0:T(8,128)S(1)} collective-permute-done((f32[264,128]{1,0:T(8,128)S(1)}, f32[264,128]{1,0:T(8,128)S(1)}, u32[]{:S(2)}, u32[]{:S(2)}) %collective-permute-start.6) | collective-permute-done | bytes 135200 | tf_op jit(solution)/shard_map/ppermute | solution.py:38
  50.6 0.6 shard_map.103
  51.2 7.6 %collective-permute-start.7 = (f32[264,128]{1,0:T(8,128)S(1)}, f32[264,128]{1,0:T(8,128)S(1)}, u32[]{:S(2)}, u32[]{:S(2)}) collective-permute-start(f32[264,128]{1,0:T(8,128)S(1)} %get-tuple-element.55), channel_id=1, source_target_pairs={{0,128},{8,136},{16,144},{24,152},{32,160},{40,168},{48,176},{56,1... | collective-permute-start | bytes 405512 | tf_op jit(solution)/shard_map/ppermute | solution.py:38
  58.8 0.3 shard_map.107
  59.1 0.3 shard_map.108
  59.5 11.6 %collective-permute-done.7.other_ref.refs_0_ = f32[264,128]{1,0:T(8,128)S(1)} collective-permute-done((f32[264,128]{1,0:T(8,128)S(1)}, f32[264,128]{1,0:T(8,128)S(1)}, u32[]{:S(2)}, u32[]{:S(2)}) %collective-permute-start.7) | collective-permute-done | bytes 135200 | tf_op jit(solution)/shard_map/ppermute | solution.py:38
  71.0 0.6 shard_map.104
  71.7 6.4 %collective-permute-start.8 = (f32[104,128]{1,0:T(8,128)S(1)}, f32[104,128]{1,0:T(8,128)S(1)}, u32[]{:S(2)}, u32[]{:S(2)}) collective-permute-start(f32[104,128]{1,0:T(8,128)S(1)} %get-tuple-element.57), channel_id=1, source_target_pairs={{0,384},{8,392},{16,400},{24,408},{32,416},{40,424},{48,432},{56,4... | collective-permute-start | bytes 159752 | tf_op jit(solution)/shard_map/ppermute | solution.py:38
  78.1 0.3 shard_map.109
  78.4 2.0 %shard_map.110.descent_ref = f32[160,512]{1,0:T(8,128)S(1)} custom-call(s32[8,128]{1,0:T(8,128)S(1)} %iota.7.bits_ref, f32[896,128]{1,0:T(8,128)S(1)} %copy-done, f32[896,128]{1,0:T(8,128)S(1)} %collective-permute-done.sibling_ref, f32[256,256]{1,0:T(8,128)S(1)} %get-tuple-element.43.weights_ref, f32[2,32,256]{2,1,0:T(8,128)S(1)} %get-tuple-element.58.owns_ref, ...), custom_call_target="tpu_custom_call" | custom-call | tf_op jit(solution)/shard_map/pallas_call | solution.py:366
  80.4 0.5 shard_map.111
  81.0 11.3 %all_to_all.10 = f32[8,32,256]{2,1,0:T(8,128)S(1)} all-to-all(f32[8,32,256]{2,1,0:T(8,128)S(1)} %shard_map.111), channel_id=1, replica_groups=mesh['pair'=64,'core'=2,'rep'=4] {'core','rep'}, dimensions={0} | all-to-all | bytes 524288 | tf_op jit(solution)/shard_map/all_to_all | solution.py:484
  92.3 1.5 %shard_map.112 = (f32[256,256]{1,0:T(8,128)}, f32[384,256]{1,0:T(8,128)}) custom-call(f32[256,256]{1,0:T(8,128)S(1)} %bitcast.15, bf16[272,384]{1,0:T(8,128)(2,1)S(1)} %copy-done.3, bf16[384,384]{1,0:T(8,128)(2,1)S(1)} %bitcast.14, bf16[768,384]{1,0:T(8,128)(2,1)S(1)} %bitcast.12), custom_call_target="tpu_custom_call" | custom-call | tf_op jit(solution)/shard_map/pallas_call | solution.py:366
  (17 shorter events, 0.8 us)
Async XLA Ops:
  5.4 12.4 %copy-start = (f32[896,128]{1,0:T(8,128)S(1)}, f32[896,128]{1,0:T(8,128)}, u32[]{:S(2)}) copy-start(f32[896,128]{1,0:T(8,128)} %get-tuple-element.39.level_ref) | copy-start | bytes 1376260
  5.4 12.3 %collective-permute-start = (f32[896,128]{1,0:T(8,128)}, f32[896,128]{1,0:T(8,128)S(1)}, u32[]{:S(2)}, u32[]{:S(2)}) collective-permute-start(f32[896,128]{1,0:T(8,128)} %get-tuple-element.39.level_ref), channel_id=1, source_target_pairs={{0,4},{4,0},{1,5},{5,1},{2,6},{6,2},{3,7},{7,3},{8,12},{12,8},{9,1... | collective-permute-start | bytes 1376264 | tf_op jit(solution)/shard_map/ppermute | solution.py:408
  14.4 9.9 %all-to-all-start = ((f32[8,32,256]{2,1,0:T(8,128)}), f32[8,32,256]{2,1,0:T(8,128)S(1)}, u32[]{:S(2)}, u32[]{:S(2)}) async-start(f32[8,32,256]{2,1,0:T(8,128)} %bitcast.16), calls=%async_computation | async-start | bytes 524288 | tf_op jit(solution)/shard_map/all_to_all | solution.py:413
  18.3 8.3 %collective-permute-start.1 = (f32[256,128]{1,0:T(8,128)S(1)}, f32[256,128]{1,0:T(8,128)S(1)}, u32[]{:S(2)}, u32[]{:S(2)}) collective-permute-start(f32[256,128]{1,0:T(8,128)S(1)} %get-tuple-element.40.own_ref), channel_id=1, source_target_pairs={{0,8},{8,0},{16,24},{24,16},{32,40},{40,32},{48,56},{56,48},{64,72... | collective-permute-start | bytes 393224 | tf_op jit(solution)/shard_map/ppermute | solution.py:38
  24.7 4.7 %collective-permute-start.3 = (f32[32,256]{1,0:T(8,128)S(1)}, f32[32,256]{1,0:T(8,128)S(1)}, u32[]{:S(2)}, u32[]{:S(2)}) collective-permute-start(f32[32,256]{1,0:T(8,128)S(1)} %get-tuple-element.44.refs_0_.own_ref.state_ref), channel_id=1, source_target_pairs={{0,8},{8,0},{16,24},{24,16},{32,40},{40,32},{48,56},{56,48},{64,72... | collective-permute-start | bytes 98312 | tf_op jit(solution)/shard_map/ppermute | solution.py:38
  27.1 7.8 %collective-permute-start.2 = (f32[256,128]{1,0:T(8,128)S(1)}, f32[256,128]{1,0:T(8,128)S(1)}, u32[]{:S(2)}, u32[]{:S(2)}) collective-permute-start(f32[256,128]{1,0:T(8,128)S(1)} %get-tuple-element.42.own_ref), channel_id=1, source_target_pairs={{0,24},{8,16},{16,8},{24,0},{32,56},{40,48},{48,40},{56,32},{64,88... | collective-permute-start | bytes 393224 | tf_op jit(solution)/shard_map/ppermute | solution.py:38
  29.5 6.4 %collective-permute-start.4 = (f32[32,256]{1,0:T(8,128)S(1)}, f32[32,256]{1,0:T(8,128)S(1)}, u32[]{:S(2)}, u32[]{:S(2)}) collective-permute-start(f32[32,256]{1,0:T(8,128)S(1)} %shard_map.100.own_ref.state_ref), channel_id=1, source_target_pairs={{0,24},{8,16},{16,8},{24,0},{32,56},{40,48},{48,40},{56,32},{64,88... | collective-permute-start | bytes 98312 | tf_op jit(solution)/shard_map/ppermute | solution.py:38
  36.1 5.8 %collective-permute-start.5 = (f32[264,128]{1,0:T(8,128)S(1)}, f32[264,128]{1,0:T(8,128)S(1)}, u32[]{:S(2)}, u32[]{:S(2)}) collective-permute-start(f32[264,128]{1,0:T(8,128)S(1)} %get-tuple-element.49), channel_id=1, source_target_pairs={{0,32},{8,40},{16,48},{24,56},{32,0},{40,8},{48,16},{56,24},{64,96... | collective-permute-start | bytes 405512 | tf_op jit(solution)/shard_map/ppermute | solution.py:38
  42.5 8.1 %collective-permute-start.6 = (f32[264,128]{1,0:T(8,128)S(1)}, f32[264,128]{1,0:T(8,128)S(1)}, u32[]{:S(2)}, u32[]{:S(2)}) collective-permute-start(f32[264,128]{1,0:T(8,128)S(1)} %get-tuple-element.52), channel_id=1, source_target_pairs={{0,64},{8,72},{16,80},{24,88},{32,96},{40,104},{48,112},{56,120},{... | collective-permute-start | bytes 405512 | tf_op jit(solution)/shard_map/ppermute | solution.py:38
  51.2 19.9 %collective-permute-start.7 = (f32[264,128]{1,0:T(8,128)S(1)}, f32[264,128]{1,0:T(8,128)S(1)}, u32[]{:S(2)}, u32[]{:S(2)}) collective-permute-start(f32[264,128]{1,0:T(8,128)S(1)} %get-tuple-element.55), channel_id=1, source_target_pairs={{0,128},{8,136},{16,144},{24,152},{32,160},{40,168},{48,176},{56,1... | collective-permute-start | bytes 405512 | tf_op jit(solution)/shard_map/ppermute | solution.py:38
  71.7 8.8 %collective-permute-start.8 = (f32[104,128]{1,0:T(8,128)S(1)}, f32[104,128]{1,0:T(8,128)S(1)}, u32[]{:S(2)}, u32[]{:S(2)}) collective-permute-start(f32[104,128]{1,0:T(8,128)S(1)} %get-tuple-element.57), channel_id=1, source_target_pairs={{0,384},{8,392},{16,400},{24,408},{32,416},{40,424},{48,432},{56,4... | collective-permute-start | bytes 159752 | tf_op jit(solution)/shard_map/ppermute | solution.py:38
  80.4 11.8 %copy-start.1 = (bf16[1,1,768,384]{3,2,1,0:T(8,128)(2,1)S(1)}, bf16[1,1,768,384]{3,2,1,0:T(8,128)(2,1)}, u32[]{:S(2)}) copy-start(bf16[1,1,768,384]{3,2,1,0:T(8,128)(2,1)} %param.11) | copy-start | bytes 1769476
  81.0 11.3 %copy-start.2 = (bf16[1,1,384,384]{3,2,1,0:T(8,128)(2,1)S(1)}, bf16[1,1,384,384]{3,2,1,0:T(8,128)(2,1)}, u32[]{:S(2)}) copy-start(bf16[1,1,384,384]{3,2,1,0:T(8,128)(2,1)} %param.8) | copy-start | bytes 884740
  81.0 11.3 %copy-start.3 = (bf16[272,384]{1,0:T(8,128)(2,1)S(1)}, bf16[272,384]{1,0:T(8,128)(2,1)}, u32[]{:S(2)}) copy-start(bf16[272,384]{1,0:T(8,128)(2,1)} %get-tuple-element.73.forward_ref) | copy-start | bytes 626692

commit v11 on v10

--- a/solution.py
+++ b/solution.py
@@ -13,7 +13,7 @@
 SWAP = (1, 3, 4, 8, 16, 48)
 
 
-APART = 2
+APART = 1
 MAPS_WEIGHT = (3, 10)
 STATE_WEIGHT = (30, 10)
 SIDE_WEIGHT = 1

time: 94.3 us -> 93.5 us (level)
  starting transfers between devices: 41.3 us -> 32.9 us
  waiting for transfers between devices: 26.3 us -> 33.9 us
    ppermute x8 -> x7, starting transfers between devices: 29 us -> 20.6 us  [swap(): return lax.ppermute(value, 'pair', [(n, n ^ SWAP[j]) for n in range(count)])]
    ppermute x8 -> x7, waiting for transfers between devices: 22.2 us -> 29.9 us  [swap(): return lax.ppermute(value, 'pair', [(n, n ^ SWAP[j]) for n in range(count)])]
    pallas_call x18 -> x17, Pallas kernels: 13.2 us -> 13.4 us  [local_call(): pl.pallas_call(kernel, out_shape=out_shape, in_specs=[vmem] * len(operand...]
  transfers between devices with their start and end apart: 10 -> 9, of which waited for: 7 -> 7; matrix products, arithmetic and copies ran while one was open for 0% -> 0% of each run, Pallas kernels for 5% -> 5%
where the time goes in v11:
time: 93.5 us; the launch traced here: 93 us
  waiting for transfers between devices  33.9 us (36%)
  starting transfers between devices  32.9 us (35%)
  Pallas kernels  13.4 us (14%)
  blocking collectives  11.2 us (12%)
  between operations  1.48 us (2%)
    ppermute x7, waiting for transfers between devices, swap(): return lax.ppermute(value, 'pair', [(n, n ^ SWAP[j]) for n in range(count)])  29.9 us
    ppermute x7, starting transfers between devices, swap(): return lax.ppermute(value, 'pair', [(n, n ^ SWAP[j]) for n in range(count)])  20.6 us
    pallas_call x17, Pallas kernels, local_call(): pl.pallas_call(kernel, out_shape=out_shape, in_specs=[vmem] * len(operand...  13.4 us
    all_to_all x1, blocking collectives, shards(): spread = lax.all_to_all(shares, group, 0, 0)  11.2 us
    ppermute x1, starting transfers between devices, shards(): sibling = lax.ppermute(level, 'core', [(0, 1), (1, 0)])  8.92 us
    all_to_all x1, waiting for transfers between devices, shards(): parts = lax.all_to_all(part.reshape(members, columns, height), group, 0, 0)  4.08 us
    all_to_all x1, starting transfers between devices, shards(): parts = lax.all_to_all(part.reshape(members, columns, height), group, 0, 0)  3.38 us
  transfers between devices with their start and end apart: 9, of which 7 were waited for; matrix products, arithmetic and copies ran while one was open for 0% of the time, Pallas kernels for 5%

profile of v11, /device:TPU:1, one launch (start us, length us, event | category | flops | bytes accessed | tf_op | source)
XLA Modules:
  0.0 93.0 jit_solution(12528382898088154234)
XLA Ops:
  1.3 4.2 %shard_map.95 = (f32[896,128]{1,0:T(8,128)}, bf16[272,384]{1,0:T(8,128)(2,1)}, f32[256,256]{1,0:T(8,128)}) custom-call(f32[256,256]{1,0:T(8,128)} %bitcast.17, f32[256,128]{1,0:T(8,128)} %bitcast.20, bf16[384,256]{1,0:T(8,128)(2,1)} %bitcast.19, s32[1,1]{1,0:T(1,128)S(6)} %copy.10.tiles_hbm, bf16[384,384]{1,0:T(8,128)(2,1)} %bitcast.13, ...), custom_call_target="tpu_custom_call" | custom-call | tf_op jit(solution)/shard_map/pallas_call | solution.py:366
  5.4 8.9 %collective-permute-start = (f32[896,128]{1,0:T(8,128)}, f32[896,128]{1,0:T(8,128)S(1)}, u32[]{:S(2)}, u32[]{:S(2)}) collective-permute-start(f32[896,128]{1,0:T(8,128)} %get-tuple-element.41.level_ref), channel_id=1, source_target_pairs={{0,4},{4,0},{1,5},{5,1},{2,6},{6,2},{3,7},{7,3},{8,12},{12,8},{9,1... | collective-permute-start | bytes 1376264 | tf_op jit(solution)/shard_map/ppermute | solution.py:408
  14.4 3.4 %all-to-all-start = ((f32[8,32,256]{2,1,0:T(8,128)}), f32[8,32,256]{2,1,0:T(8,128)S(1)}, u32[]{:S(2)}, u32[]{:S(2)}) async-start(f32[8,32,256]{2,1,0:T(8,128)} %bitcast.16), calls=%async_computation | async-start | bytes 524288 | tf_op jit(solution)/shard_map/all_to_all | solution.py:413
  17.9 0.4 shard_map.96
  18.3 1.9 %collective-permute-start.1 = (f32[256,128]{1,0:T(8,128)S(1)}, f32[256,128]{1,0:T(8,128)S(1)}, u32[]{:S(2)}, u32[]{:S(2)}) collective-permute-start(f32[256,128]{1,0:T(8,128)S(1)} %get-tuple-element.42.own_ref), channel_id=1, source_target_pairs={{0,8},{8,0},{16,24},{24,16},{32,40},{40,32},{48,56},{56,48},{64,72... | collective-permute-start | bytes 393224 | tf_op jit(solution)/shard_map/ppermute | solution.py:38
  20.2 4.1 %all-to-all-done.refs_0_.parts_ref = f32[8,32,256]{2,1,0:T(8,128)S(1)} async-done(((f32[8,32,256]{2,1,0:T(8,128)}), f32[8,32,256]{2,1,0:T(8,128)S(1)}, u32[]{:S(2)}, u32[]{:S(2)}) %all-to-all-start) | async-done | bytes 262176 | tf_op jit(solution)/shard_map/all_to_all | solution.py:413
  24.3 0.4 shard_map.98
  24.7 1.9 %collective-permute-start.2 = (f32[32,256]{1,0:T(8,128)S(1)}, f32[32,256]{1,0:T(8,128)S(1)}, u32[]{:S(2)}, u32[]{:S(2)}) collective-permute-start(f32[32,256]{1,0:T(8,128)S(1)} %get-tuple-element.46.own_ref.state_ref), channel_id=1, source_target_pairs={{0,8},{8,0},{16,24},{24,16},{32,40},{40,32},{48,56},{56,48},{64,72... | collective-permute-start | bytes 98312 | tf_op jit(solution)/shard_map/ppermute | solution.py:38
  26.6 0.4 shard_map.97
  27.1 2.3 %collective-permute-done.2.other_ref.refs_1_ = f32[32,256]{1,0:T(8,128)S(1)} collective-permute-done((f32[32,256]{1,0:T(8,128)S(1)}, f32[32,256]{1,0:T(8,128)S(1)}, u32[]{:S(2)}, u32[]{:S(2)}) %collective-permute-start.2) | collective-permute-done | bytes 32800 | tf_op jit(solution)/shard_map/ppermute | solution.py:38
  29.6 1.9 %collective-permute-start.3 = (f32[264,128]{1,0:T(8,128)S(1)}, f32[264,128]{1,0:T(8,128)S(1)}, u32[]{:S(2)}, u32[]{:S(2)}) collective-permute-start(f32[264,128]{1,0:T(8,128)S(1)} %get-tuple-element.49), channel_id=1, source_target_pairs={{0,24},{8,16},{16,8},{24,0},{32,56},{40,48},{48,40},{56,32},{64,88... | collective-permute-start | bytes 405512 | tf_op jit(solution)/shard_map/ppermute | solution.py:38
  31.5 5.0 %collective-permute-done.3.other_ref.refs_0_ = f32[264,128]{1,0:T(8,128)S(1)} collective-permute-done((f32[264,128]{1,0:T(8,128)S(1)}, f32[264,128]{1,0:T(8,128)S(1)}, u32[]{:S(2)}, u32[]{:S(2)}) %collective-permute-start.3) | collective-permute-done | bytes 135200 | tf_op jit(solution)/shard_map/ppermute | solution.py:38
  36.5 0.6 shard_map.100
  37.1 1.9 %collective-permute-start.4 = (f32[264,128]{1,0:T(8,128)S(1)}, f32[264,128]{1,0:T(8,128)S(1)}, u32[]{:S(2)}, u32[]{:S(2)}) collective-permute-start(f32[264,128]{1,0:T(8,128)S(1)} %get-tuple-element.52), channel_id=1, source_target_pairs={{0,32},{8,40},{16,48},{24,56},{32,0},{40,8},{48,16},{56,24},{64,96... | collective-permute-start | bytes 405512 | tf_op jit(solution)/shard_map/ppermute | solution.py:38
  39.0 3.8 %collective-permute-done.4.other_ref.refs_0_ = f32[264,128]{1,0:T(8,128)S(1)} collective-permute-done((f32[264,128]{1,0:T(8,128)S(1)}, f32[264,128]{1,0:T(8,128)S(1)}, u32[]{:S(2)}, u32[]{:S(2)}) %collective-permute-start.4) | collective-permute-done | bytes 135200 | tf_op jit(solution)/shard_map/ppermute | solution.py:38
  42.9 0.6 shard_map.101
  43.5 1.9 %collective-permute-start.5 = (f32[264,128]{1,0:T(8,128)S(1)}, f32[264,128]{1,0:T(8,128)S(1)}, u32[]{:S(2)}, u32[]{:S(2)}) collective-permute-start(f32[264,128]{1,0:T(8,128)S(1)} %get-tuple-element.55), channel_id=1, source_target_pairs={{0,64},{8,72},{16,80},{24,88},{32,96},{40,104},{48,112},{56,120},{... | collective-permute-start | bytes 405512 | tf_op jit(solution)/shard_map/ppermute | solution.py:38
  45.6 0.3 shard_map.105
  45.9 5.4 %collective-permute-done.5.other_ref.refs_0_ = f32[264,128]{1,0:T(8,128)S(1)} collective-permute-done((f32[264,128]{1,0:T(8,128)S(1)}, f32[264,128]{1,0:T(8,128)S(1)}, u32[]{:S(2)}, u32[]{:S(2)}) %collective-permute-start.5) | collective-permute-done | bytes 135200 | tf_op jit(solution)/shard_map/ppermute | solution.py:38
  51.3 0.6 shard_map.102
  51.9 5.7 %collective-permute-start.6 = (f32[264,128]{1,0:T(8,128)S(1)}, f32[264,128]{1,0:T(8,128)S(1)}, u32[]{:S(2)}, u32[]{:S(2)}) collective-permute-start(f32[264,128]{1,0:T(8,128)S(1)} %get-tuple-element.58), channel_id=1, source_target_pairs={{0,128},{8,136},{16,144},{24,152},{32,160},{40,168},{48,176},{56,1... | collective-permute-start | bytes 405512 | tf_op jit(solution)/shard_map/ppermute | solution.py:38
  57.6 0.3 shard_map.106
  57.9 0.3 shard_map.107
  58.2 12.0 %collective-permute-done.6.other_ref.refs_0_ = f32[264,128]{1,0:T(8,128)S(1)} collective-permute-done((f32[264,128]{1,0:T(8,128)S(1)}, f32[264,128]{1,0:T(8,128)S(1)}, u32[]{:S(2)}, u32[]{:S(2)}) %collective-permute-start.6) | collective-permute-done | bytes 135200 | tf_op jit(solution)/shard_map/ppermute | solution.py:38
  70.2 0.6 shard_map.103
  70.8 5.3 %collective-permute-start.7 = (f32[104,128]{1,0:T(8,128)S(1)}, f32[104,128]{1,0:T(8,128)S(1)}, u32[]{:S(2)}, u32[]{:S(2)}) collective-permute-start(f32[104,128]{1,0:T(8,128)S(1)} %get-tuple-element.60), channel_id=1, source_target_pairs={{0,384},{8,392},{16,400},{24,408},{32,416},{40,424},{48,432},{56,4... | collective-permute-start | bytes 159752 | tf_op jit(solution)/shard_map/ppermute | solution.py:38
  76.2 0.3 shard_map.108
  76.5 2.0 %shard_map.109.descent_ref = f32[160,512]{1,0:T(8,128)S(1)} custom-call(s32[8,128]{1,0:T(8,128)S(1)} %iota.7.bits_ref, f32[896,128]{1,0:T(8,128)S(1)} %copy-done, f32[896,128]{1,0:T(8,128)S(1)} %collective-permute-done.sibling_ref, f32[256,256]{1,0:T(8,128)S(1)} %get-tuple-element.45.weights_ref, f32[2,32,256]{2,1,0:T(8,128)S(1)} %get-tuple-element.61.owns_ref, ...), custom_call_target="tpu_custom_call" | custom-call | tf_op jit(solution)/shard_map/pallas_call | solution.py:366
  78.5 1.3 %collective-permute-done.7.other_ref = f32[104,128]{1,0:T(8,128)S(1)} collective-permute-done((f32[104,128]{1,0:T(8,128)S(1)}, f32[104,128]{1,0:T(8,128)S(1)}, u32[]{:S(2)}, u32[]{:S(2)}) %collective-permute-start.7) | collective-permute-done | bytes 53280 | tf_op jit(solution)/shard_map/ppermute | solution.py:38
  79.7 0.5 shard_map.110
  80.3 11.2 %all_to_all.10 = f32[8,32,256]{2,1,0:T(8,128)S(1)} all-to-all(f32[8,32,256]{2,1,0:T(8,128)S(1)} %shard_map.110), channel_id=1, replica_groups=mesh['pair'=64,'core'=2,'rep'=4] {'core','rep'}, dimensions={0} | all-to-all | bytes 524288 | tf_op jit(solution)/shard_map/all_to_all | solution.py:484
  91.5 1.5 %shard_map.111 = (f32[256,256]{1,0:T(8,128)}, f32[384,256]{1,0:T(8,128)}) custom-call(f32[256,256]{1,0:T(8,128)S(1)} %bitcast.15, bf16[272,384]{1,0:T(8,128)(2,1)S(1)} %copy-done.3, bf16[384,384]{1,0:T(8,128)(2,1)S(1)} %bitcast.14, bf16[768,384]{1,0:T(8,128)(2,1)S(1)} %bitcast.12), custom_call_target="tpu_custom_call" | custom-call | tf_op jit(solution)/shard_map/pallas_call | solution.py:366
  (14 shorter events, 0.4 us)
Async XLA Ops:
  5.4 12.4 %copy-start = (f32[896,128]{1,0:T(8,128)S(1)}, f32[896,128]{1,0:T(8,128)}, u32[]{:S(2)}) copy-start(f32[896,128]{1,0:T(8,128)} %get-tuple-element.41.level_ref) | copy-start | bytes 1376260
  5.4 12.3 %collective-permute-start = (f32[896,128]{1,0:T(8,128)}, f32[896,128]{1,0:T(8,128)S(1)}, u32[]{:S(2)}, u32[]{:S(2)}) collective-permute-start(f32[896,128]{1,0:T(8,128)} %get-tuple-element.41.level_ref), channel_id=1, source_target_pairs={{0,4},{4,0},{1,5},{5,1},{2,6},{6,2},{3,7},{7,3},{8,12},{12,8},{9,1... | collective-permute-start | bytes 1376264 | tf_op jit(solution)/shard_map/ppermute | solution.py:408
  14.4 9.9 %all-to-all-start = ((f32[8,32,256]{2,1,0:T(8,128)}), f32[8,32,256]{2,1,0:T(8,128)S(1)}, u32[]{:S(2)}, u32[]{:S(2)}) async-start(f32[8,32,256]{2,1,0:T(8,128)} %bitcast.16), calls=%async_computation | async-start | bytes 524288 | tf_op jit(solution)/shard_map/all_to_all | solution.py:413
  18.3 8.3 %collective-permute-start.1 = (f32[256,128]{1,0:T(8,128)S(1)}, f32[256,128]{1,0:T(8,128)S(1)}, u32[]{:S(2)}, u32[]{:S(2)}) collective-permute-start(f32[256,128]{1,0:T(8,128)S(1)} %get-tuple-element.42.own_ref), channel_id=1, source_target_pairs={{0,8},{8,0},{16,24},{24,16},{32,40},{40,32},{48,56},{56,48},{64,72... | collective-permute-start | bytes 393224 | tf_op jit(solution)/shard_map/ppermute | solution.py:38
  24.7 4.7 %collective-permute-start.2 = (f32[32,256]{1,0:T(8,128)S(1)}, f32[32,256]{1,0:T(8,128)S(1)}, u32[]{:S(2)}, u32[]{:S(2)}) collective-permute-start(f32[32,256]{1,0:T(8,128)S(1)} %get-tuple-element.46.own_ref.state_ref), channel_id=1, source_target_pairs={{0,8},{8,0},{16,24},{24,16},{32,40},{40,32},{48,56},{56,48},{64,72... | collective-permute-start | bytes 98312 | tf_op jit(solution)/shard_map/ppermute | solution.py:38
  29.6 7.0 %collective-permute-start.3 = (f32[264,128]{1,0:T(8,128)S(1)}, f32[264,128]{1,0:T(8,128)S(1)}, u32[]{:S(2)}, u32[]{:S(2)}) collective-permute-start(f32[264,128]{1,0:T(8,128)S(1)} %get-tuple-element.49), channel_id=1, source_target_pairs={{0,24},{8,16},{16,8},{24,0},{32,56},{40,48},{48,40},{56,32},{64,88... | collective-permute-start | bytes 405512 | tf_op jit(solution)/shard_map/ppermute | solution.py:38
  37.1 5.7 %collective-permute-start.4 = (f32[264,128]{1,0:T(8,128)S(1)}, f32[264,128]{1,0:T(8,128)S(1)}, u32[]{:S(2)}, u32[]{:S(2)}) collective-permute-start(f32[264,128]{1,0:T(8,128)S(1)} %get-tuple-element.52), channel_id=1, source_target_pairs={{0,32},{8,40},{16,48},{24,56},{32,0},{40,8},{48,16},{56,24},{64,96... | collective-permute-start | bytes 405512 | tf_op jit(solution)/shard_map/ppermute | solution.py:38
  43.5 7.8 %collective-permute-start.5 = (f32[264,128]{1,0:T(8,128)S(1)}, f32[264,128]{1,0:T(8,128)S(1)}, u32[]{:S(2)}, u32[]{:S(2)}) collective-permute-start(f32[264,128]{1,0:T(8,128)S(1)} %get-tuple-element.55), channel_id=1, source_target_pairs={{0,64},{8,72},{16,80},{24,88},{32,96},{40,104},{48,112},{56,120},{... | collective-permute-start | bytes 405512 | tf_op jit(solution)/shard_map/ppermute | solution.py:38
  51.9 18.3 %collective-permute-start.6 = (f32[264,128]{1,0:T(8,128)S(1)}, f32[264,128]{1,0:T(8,128)S(1)}, u32[]{:S(2)}, u32[]{:S(2)}) collective-permute-start(f32[264,128]{1,0:T(8,128)S(1)} %get-tuple-element.58), channel_id=1, source_target_pairs={{0,128},{8,136},{16,144},{24,152},{32,160},{40,168},{48,176},{56,1... | collective-permute-start | bytes 405512 | tf_op jit(solution)/shard_map/ppermute | solution.py:38
  70.8 8.9 %collective-permute-start.7 = (f32[104,128]{1,0:T(8,128)S(1)}, f32[104,128]{1,0:T(8,128)S(1)}, u32[]{:S(2)}, u32[]{:S(2)}) collective-permute-start(f32[104,128]{1,0:T(8,128)S(1)} %get-tuple-element.60), channel_id=1, source_target_pairs={{0,384},{8,392},{16,400},{24,408},{32,416},{40,424},{48,432},{56,4... | collective-permute-start | bytes 159752 | tf_op jit(solution)/shard_map/ppermute | solution.py:38
  79.7 11.7 %copy-start.1 = (bf16[1,1,768,384]{3,2,1,0:T(8,128)(2,1)S(1)}, bf16[1,1,768,384]{3,2,1,0:T(8,128)(2,1)}, u32[]{:S(2)}) copy-start(bf16[1,1,768,384]{3,2,1,0:T(8,128)(2,1)} %param.11) | copy-start | bytes 1769476
  80.3 11.2 %copy-start.2 = (bf16[1,1,384,384]{3,2,1,0:T(8,128)(2,1)S(1)}, bf16[1,1,384,384]{3,2,1,0:T(8,128)(2,1)}, u32[]{:S(2)}) copy-start(bf16[1,1,384,384]{3,2,1,0:T(8,128)(2,1)} %param.8) | copy-start | bytes 884740
  80.3 11.2 %copy-start.3 = (bf16[272,384]{1,0:T(8,128)(2,1)S(1)}, bf16[272,384]{1,0:T(8,128)(2,1)}, u32[]{:S(2)}) copy-start(bf16[272,384]{1,0:T(8,128)(2,1)} %get-tuple-element.77.forward_ref) | copy-start | bytes 626692
